TPU v7x, 32 devices: a whole 2x2x4 slice. The times are simulated.
32 devices in a mesh: dp: 4 (over y, x), seq: 8 (over z, core).
Axes of the slice: x: 2, y: 2, z: 4, core: 2. Of those that a mesh axis runs over, the one named last changes fastest.
Arguments:
- latents: bfloat16 [8, 2048, 1536], P('dp', 'seq'), may hold values from -6 to 6
- context: bfloat16 [8, 512, 1536], P('dp', 'seq'), may hold values from -6 to 6
- modulation: float32 [8, 6, 1536], P('dp'), may hold values from -4 to 4
- cotangent: bfloat16 [8, 2048, 1536], P('dp', 'seq'), may hold values from -6 to 6
- modtable: bfloat16 [6, 1536], P(None, ('dp', 'seq')), may hold values from -3 to 3
- selfquery: bfloat16 [1536, 1536], P(('dp', 'seq')), may hold values from -0.15625 to 0.15625
- selfkey: bfloat16 [1536, 1536], P(('dp', 'seq')), may hold values from -0.15625 to 0.15625
- selfvalue: bfloat16 [1536, 1536], P(('dp', 'seq')), may hold values from -0.15625 to 0.15625
- selfout: bfloat16 [1536, 1536], P(('dp', 'seq')), may hold values from -1.75 to 1.75
- querygain: bfloat16 [1536], P(('dp', 'seq')), may hold values from 0.099609375 to 1.8984375
- keygain: bfloat16 [1536], P(('dp', 'seq')), may hold values from 0.099609375 to 1.8984375
- normgain: bfloat16 [1536], P(('dp', 'seq')), may hold values from 0.099609375 to 1.8984375
- normbias: bfloat16 [1536], P(('dp', 'seq')), may hold values from -3 to 3
- crossquery: bfloat16 [1536, 1536], P(('dp', 'seq')), may hold values from -0.15625 to 0.15625
- crosskey: bfloat16 [1536, 1536], P(('dp', 'seq')), may hold values from -0.15625 to 0.15625
- crossvalue: bfloat16 [1536, 1536], P(('dp', 'seq')), may hold values from -0.15625 to 0.15625
- crossout: bfloat16 [1536, 1536], P(('dp', 'seq')), may hold values from -0.875 to 0.875
- crossqgain: bfloat16 [1536], P(('dp', 'seq')), may hold values from 0.099609375 to 1.8984375
- crosskgain: bfloat16 [1536], P(('dp', 'seq')), may hold values from 0.099609375 to 1.8984375
- upmatrix: bfloat16 [1536, 8960], P(('dp', 'seq')), may hold values from -0.15625 to 0.15625
- downmatrix: bfloat16 [8960, 1536], P(('dp', 'seq')), may hold values from -0.0625 to 0.0625
Outputs:
- layer_output: bfloat16 [8, 2048, 1536], P('dp', 'seq')
- latents_gradient: float32 [8, 2048, 1536], P('dp', 'seq')
- context_gradient: float32 [8, 512, 1536], P('dp', 'seq')
- modulation_gradient: float32 [8, 6, 1536], P('dp')
- modtable_gradient: float32 [6, 1536], P(None, ('dp', 'seq'))
- selfquery_gradient: float32 [1536, 1536], P(('dp', 'seq'))
- selfkey_gradient: float32 [1536, 1536], P(('dp', 'seq'))
- selfvalue_gradient: float32 [1536, 1536], P(('dp', 'seq'))
- selfout_gradient: float32 [1536, 1536], P(('dp', 'seq'))
- querygain_gradient: float32 [1536], P(('dp', 'seq'))
- keygain_gradient: float32 [1536], P(('dp', 'seq'))
- normgain_gradient: float32 [1536], P(('dp', 'seq'))
- normbias_gradient: float32 [1536], P(('dp', 'seq'))
- crossquery_gradient: float32 [1536, 1536], P(('dp', 'seq'))
- crosskey_gradient: float32 [1536, 1536], P(('dp', 'seq'))
- crossvalue_gradient: float32 [1536, 1536], P(('dp', 'seq'))
- crossout_gradient: float32 [1536, 1536], P(('dp', 'seq'))
- crossqgain_gradient: float32 [1536], P(('dp', 'seq'))
- crosskgain_gradient: float32 [1536], P(('dp', 'seq'))
- upmatrix_gradient: float32 [1536, 8960], P(('dp', 'seq'))
- downmatrix_gradient: float32 [8960, 1536], P(('dp', 'seq'))
All inputs are finite; a program needn't handle non-finite values.
Results may differ from a plain program's by a relative error of at most 0.019.
Values may be sent and summed in bfloat16 or wider, within the bound.
No kernel may reach another device: no remote copies, remote signals or barrier semaphores. Data moves between devices by JAX's collectives and lax.ppermute only.
A program may use at most 304 MiB of HBM per device.

v0:
```python
import jax
import jax.numpy as jnp
from jax import lax
from jax.sharding import PartitionSpec as P

HEADS = 12
HEAD_DIM = 128
GRID_H = 32
GRID_W = 32


eps_value = 1e-06


def layer_norm(values):
    center = values - jnp.mean(values, axis=-1, keepdims=True)
    return center * lax.rsqrt(jnp.mean(center * center, axis=-1, keepdims=True) + eps_value)


def rms_norm(values, norm_gain):
    return (
        values
        * lax.rsqrt(jnp.mean(values * values, axis=-1, keepdims=True) + eps_value)
        * norm_gain
    )


def affine_norm(values, norm_gain, norm_shift):
    return layer_norm(values) * norm_gain + norm_shift


def gelu_tanh(values):
    return jax.nn.gelu(values, approximate=True)


def frequencies(number):
    return jnp.power(10000.0, -jnp.arange(number, dtype=jnp.float32) / number)


def rotary_tables(positions):
    pair_count = HEAD_DIM // 2
    side_pairs = pair_count // 3
    lead_pairs = pair_count - 2 * side_pairs
    frame_index = (positions // (GRID_H * GRID_W)).astype(jnp.float32)
    row_index = (positions // GRID_W % GRID_H).astype(jnp.float32)
    column_index = (positions % GRID_W).astype(jnp.float32)
    angles = jnp.concatenate(
        [
            frame_index[:, None] * frequencies(lead_pairs),
            row_index[:, None] * frequencies(side_pairs),
            column_index[:, None] * frequencies(side_pairs),
        ],
        axis=1,
    )
    return (jnp.cos(angles), jnp.sin(angles))


def rotate(values, cosine, sine_table):
    shaped = values.reshape(values.shape[:-1] + (HEADS, HEAD_DIM // 2, 2))
    even_part = shaped[..., 0]
    odd_part = shaped[..., 1]
    cos_rows = cosine[:, None, :]
    sin_rows = sine_table[:, None, :]
    turned = jnp.stack(
        [even_part * cos_rows - odd_part * sin_rows, even_part * sin_rows + odd_part * cos_rows],
        axis=-1,
    )
    return turned.reshape(values.shape)


def project(operand, weights):
    return jnp.einsum("crd,de->cre", operand, weights, preferred_element_type=jnp.float32)


def project_back(gradient, weights):
    return jnp.einsum("cre,de->crd", gradient, weights, preferred_element_type=jnp.float32)


def weight_term(operand, gradient):
    return jnp.einsum("crd,cre->de", operand, gradient, preferred_element_type=jnp.float32)


def heads_first(values):
    return values.reshape(values.shape[0], values.shape[1], HEADS, HEAD_DIM).transpose(2, 0, 1, 3)


def heads_last(values):
    return values.transpose(1, 2, 0, 3).reshape(values.shape[1], values.shape[2], HEADS * HEAD_DIM)


def table_row(mod_rows, position):
    return mod_rows[:, position][:, None, :]


def head_scores(head_query, head_key):
    return jnp.einsum(
        "crd,ckd->crk", head_query, head_key, preferred_element_type=jnp.float32
    ) * HEAD_DIM ** (-0.5)


def head_forward(operands):
    head_query, head_key, head_value = operands
    scores = head_scores(head_query, head_key)
    max_score = jnp.max(scores, axis=-1, keepdims=True)
    exp_score = jnp.exp(scores - max_score)
    total_score = jnp.sum(exp_score, axis=-1, keepdims=True)
    attention = (exp_score / total_score).astype(jnp.bfloat16)
    outputs = jnp.einsum("crk,ckd->crd", attention, head_value, preferred_element_type=jnp.float32)
    return (outputs, max_score, total_score)


def head_backward(operands):
    head_query, head_key, head_value, head_grad, max_score, total_score = operands
    attention = jnp.exp(head_scores(head_query, head_key) - max_score) / total_score
    value_grad = jnp.einsum(
        "crk,crd->ckd",
        attention.astype(jnp.bfloat16),
        head_grad,
        preferred_element_type=jnp.float32,
    )
    attn_grad = jnp.einsum(
        "crd,ckd->crk", head_grad, head_value, preferred_element_type=jnp.float32
    )
    score_grad = attention * (attn_grad - jnp.sum(attention * attn_grad, axis=-1, keepdims=True))
    score_low = (score_grad * HEAD_DIM ** (-0.5)).astype(jnp.bfloat16)
    query_grad = jnp.einsum("crk,ckd->crd", score_low, head_key, preferred_element_type=jnp.float32)
    key_grad = jnp.einsum("crk,crd->ckd", score_low, head_query, preferred_element_type=jnp.float32)
    return (query_grad, key_grad, value_grad)


def run_clip(latents, context, modulation, cotangent, shards):
    (
        modtable,
        selfquery,
        selfkey,
        selfvalue,
        selfout,
        querygain,
        keygain,
        normgain,
        normbias,
        crossquery,
        crosskey,
        crossvalue,
        crossout,
        crossqgain,
        crosskgain,
        upmatrix,
        downmatrix,
    ) = shards
    fetched = (
        lax.all_gather(modtable, ("dp", "seq"), axis=1, tiled=True),
        lax.all_gather(selfquery, ("dp", "seq"), axis=0, tiled=True),
        lax.all_gather(selfkey, ("dp", "seq"), axis=0, tiled=True),
        lax.all_gather(selfvalue, ("dp", "seq"), axis=0, tiled=True),
        lax.all_gather(selfout, ("dp", "seq"), axis=0, tiled=True),
        lax.all_gather(querygain, ("dp", "seq"), axis=0, tiled=True),
        lax.all_gather(keygain, ("dp", "seq"), axis=0, tiled=True),
        lax.all_gather(normgain, ("dp", "seq"), axis=0, tiled=True),
        lax.all_gather(normbias, ("dp", "seq"), axis=0, tiled=True),
        lax.all_gather(crossquery, ("dp", "seq"), axis=0, tiled=True),
        lax.all_gather(crosskey, ("dp", "seq"), axis=0, tiled=True),
        lax.all_gather(crossvalue, ("dp", "seq"), axis=0, tiled=True),
        lax.all_gather(crossout, ("dp", "seq"), axis=0, tiled=True),
        lax.all_gather(crossqgain, ("dp", "seq"), axis=0, tiled=True),
        lax.all_gather(crosskgain, ("dp", "seq"), axis=0, tiled=True),
        lax.all_gather(upmatrix, ("dp", "seq"), axis=0, tiled=True),
        lax.all_gather(downmatrix, ("dp", "seq"), axis=0, tiled=True),
    )
    (
        whole_modtable,
        whole_selfquery,
        whole_selfkey,
        whole_selfvalue,
        whole_selfout,
        whole_querygain,
        whole_keygain,
        whole_normgain,
        whole_normbias,
        whole_crossquery,
        whole_crosskey,
        whole_crossvalue,
        whole_crossout,
        whole_crossqgain,
        whole_crosskgain,
        whole_upmatrix,
        whole_downmatrix,
    ) = fetched
    gain_query = whole_querygain.astype(jnp.float32)
    gain_key = whole_keygain.astype(jnp.float32)
    gain_norm = whole_normgain.astype(jnp.float32)
    bias_norm = whole_normbias.astype(jnp.float32)
    gain_crossq = whole_crossqgain.astype(jnp.float32)
    gain_crossk = whole_crosskgain.astype(jnp.float32)
    row_count = latents.shape[1]
    positions = lax.axis_index("seq") * row_count + jnp.arange(row_count, dtype=jnp.int32)
    cosine, sine_table = rotary_tables(positions)

    def turned_norm(raw_values, norm_gain):
        return rotate(rms_norm(raw_values, norm_gain), cosine, sine_table)

    latent_rows = latents.astype(jnp.float32)
    mod_rows = modulation + whole_modtable.astype(jnp.float32)[None]
    normed_a = layer_norm(latent_rows)
    attn_in = (normed_a * (1.0 + table_row(mod_rows, 1)) + table_row(mod_rows, 0)).astype(
        jnp.bfloat16
    )
    query_raw = project(attn_in, whole_selfquery)
    key_raw = project(attn_in, whole_selfkey)
    value_raw = project(attn_in, whole_selfvalue)
    query_heads = heads_first(turned_norm(query_raw, gain_query).astype(jnp.bfloat16))
    key_heads = heads_first(turned_norm(key_raw, gain_key).astype(jnp.bfloat16))
    value_heads = heads_first(value_raw.astype(jnp.bfloat16))
    key_all, value_all = (
        lax.all_gather(key_heads, "seq", axis=2, tiled=True),
        lax.all_gather(value_heads, "seq", axis=2, tiled=True),
    )
    self_heads, self_peak, self_total = lax.map(head_forward, (query_heads, key_all, value_all))
    attended = heads_last(self_heads).astype(jnp.bfloat16)
    self_branch = project(attended, whole_selfout)
    hidden_one = latent_rows + self_branch * table_row(mod_rows, 2)
    cross_in = affine_norm(hidden_one, gain_norm, bias_norm).astype(jnp.bfloat16)
    crossq_raw = project(cross_in, whole_crossquery)
    crossk_raw = project(context, whole_crosskey)
    crossv_raw = project(context, whole_crossvalue)
    crossq_heads = heads_first(rms_norm(crossq_raw, gain_crossq).astype(jnp.bfloat16))
    crossk_local = heads_first(rms_norm(crossk_raw, gain_crossk).astype(jnp.bfloat16))
    crossv_local = heads_first(crossv_raw.astype(jnp.bfloat16))
    crossk_all, crossv_all = (
        lax.all_gather(crossk_local, "seq", axis=2, tiled=True),
        lax.all_gather(crossv_local, "seq", axis=2, tiled=True),
    )
    cross_heads, cross_peak, cross_total = lax.map(
        head_forward, (crossq_heads, crossk_all, crossv_all)
    )
    crossed = heads_last(cross_heads).astype(jnp.bfloat16)
    hidden_two = hidden_one + project(crossed, whole_crossout)
    normed_m = layer_norm(hidden_two)
    mlp_in = (normed_m * (1.0 + table_row(mod_rows, 4)) + table_row(mod_rows, 3)).astype(
        jnp.bfloat16
    )
    up_values = project(mlp_in, whole_upmatrix)
    activation = gelu_tanh(up_values).astype(jnp.bfloat16)
    down_values = project(activation, whole_downmatrix)
    layer_output = (hidden_two + down_values * table_row(mod_rows, 5)).astype(jnp.bfloat16)
    (
        back_selfquery,
        back_selfkey,
        back_selfvalue,
        back_selfout,
        back_crossquery,
        back_crosskey,
        back_crossvalue,
        back_crossout,
        back_upmatrix,
        back_downmatrix,
    ) = (
        lax.all_gather(selfquery, ("dp", "seq"), axis=0, tiled=True),
        lax.all_gather(selfkey, ("dp", "seq"), axis=0, tiled=True),
        lax.all_gather(selfvalue, ("dp", "seq"), axis=0, tiled=True),
        lax.all_gather(selfout, ("dp", "seq"), axis=0, tiled=True),
        lax.all_gather(crossquery, ("dp", "seq"), axis=0, tiled=True),
        lax.all_gather(crosskey, ("dp", "seq"), axis=0, tiled=True),
        lax.all_gather(crossvalue, ("dp", "seq"), axis=0, tiled=True),
        lax.all_gather(crossout, ("dp", "seq"), axis=0, tiled=True),
        lax.all_gather(upmatrix, ("dp", "seq"), axis=0, tiled=True),
        lax.all_gather(downmatrix, ("dp", "seq"), axis=0, tiled=True),
    )
    out_grad = cotangent.astype(jnp.float32)
    gate_m_grad = jnp.sum(out_grad * down_values, axis=1)
    down_grad = (out_grad * table_row(mod_rows, 5)).astype(jnp.bfloat16)
    act_grad = project_back(down_grad, back_downmatrix)
    gelu_back = jax.vjp(gelu_tanh, up_values)[1]
    up_grad = gelu_back(act_grad)[0].astype(jnp.bfloat16)
    mlp_grad = project_back(up_grad, back_upmatrix)
    shift_m_grad = jnp.sum(mlp_grad, axis=1)
    scale_m_grad = jnp.sum(mlp_grad * normed_m, axis=1)
    norm_m_back = jax.vjp(layer_norm, hidden_two)[1]
    two_grad = out_grad + norm_m_back(mlp_grad * (1.0 + table_row(mod_rows, 4)))[0]
    cross_grad = two_grad.astype(jnp.bfloat16)
    crossed_grad = project_back(cross_grad, back_crossout).astype(jnp.bfloat16)
    crossq_grad, crossk_full, crossv_full = lax.map(
        head_backward,
        (crossq_heads, crossk_all, crossv_all, heads_first(crossed_grad), cross_peak, cross_total),
    )
    crossk_own, crossv_own = (
        lax.psum_scatter(
            crossk_full.astype(jnp.bfloat16), "seq", scatter_dimension=2, tiled=True
        ).astype(jnp.float32),
        lax.psum_scatter(
            crossv_full.astype(jnp.bfloat16), "seq", scatter_dimension=2, tiled=True
        ).astype(jnp.float32),
    )
    crossv_low = heads_last(crossv_own).astype(jnp.bfloat16)
    crossk_back = jax.vjp(rms_norm, crossk_raw, gain_crossk)[1]
    crossk_rawgrad, crossk_gaingrad = crossk_back(heads_last(crossk_own))
    crossk_low = crossk_rawgrad.astype(jnp.bfloat16)
    context_gradient = project_back(crossk_low, back_crosskey) + project_back(
        crossv_low, back_crossvalue
    )
    crossq_back = jax.vjp(rms_norm, crossq_raw, gain_crossq)[1]
    crossq_rawgrad, crossq_gaingrad = crossq_back(heads_last(crossq_grad))
    crossq_low = crossq_rawgrad.astype(jnp.bfloat16)
    crossin_grad = project_back(crossq_low, back_crossquery)
    affine_back = jax.vjp(affine_norm, hidden_one, gain_norm, bias_norm)[1]
    hidden_normgrad, normgain_grad, normbias_grad = affine_back(crossin_grad)
    one_grad = two_grad + hidden_normgrad
    gate_a_grad = jnp.sum(one_grad * self_branch, axis=1)
    branch_grad = (one_grad * table_row(mod_rows, 2)).astype(jnp.bfloat16)
    attended_grad = project_back(branch_grad, back_selfout).astype(jnp.bfloat16)
    query_grad, key_full, value_full = lax.map(
        head_backward,
        (query_heads, key_all, value_all, heads_first(attended_grad), self_peak, self_total),
    )
    key_own, value_own = (
        lax.psum_scatter(
            key_full.astype(jnp.bfloat16), "seq", scatter_dimension=2, tiled=True
        ).astype(jnp.float32),
        lax.psum_scatter(
            value_full.astype(jnp.bfloat16), "seq", scatter_dimension=2, tiled=True
        ).astype(jnp.float32),
    )
    value_low = heads_last(value_own).astype(jnp.bfloat16)
    query_back = jax.vjp(turned_norm, query_raw, gain_query)[1]
    query_rawgrad, query_gaingrad = query_back(heads_last(query_grad))
    key_back = jax.vjp(turned_norm, key_raw, gain_key)[1]
    key_rawgrad, key_gaingrad = key_back(heads_last(key_own))
    query_low = query_rawgrad.astype(jnp.bfloat16)
    key_low = key_rawgrad.astype(jnp.bfloat16)
    attn_grad = (
        project_back(query_low, back_selfquery)
        + project_back(key_low, back_selfkey)
        + project_back(value_low, back_selfvalue)
    )
    shift_a_grad = jnp.sum(attn_grad, axis=1)
    scale_a_grad = jnp.sum(attn_grad * normed_a, axis=1)
    norm_a_back = jax.vjp(layer_norm, latent_rows)[1]
    latents_gradient = one_grad + norm_a_back(attn_grad * (1.0 + table_row(mod_rows, 1)))[0]
    local_mod = jnp.stack(
        [shift_a_grad, scale_a_grad, gate_a_grad, shift_m_grad, scale_m_grad, gate_m_grad], axis=1
    )
    modulation_gradient = lax.psum(local_mod.astype(jnp.bfloat16), "seq").astype(jnp.float32)
    table_term = jnp.sum(local_mod, axis=0)
    pairs = (
        (activation, down_grad),
        (mlp_in, up_grad),
        (crossed, cross_grad),
        (cross_in, crossq_low),
        (context, crossk_low),
        (context, crossv_low),
        (attn_in, query_low),
        (attn_in, key_low),
        (attn_in, value_low),
        (attended, branch_grad),
    )
    gains = (
        normgain_grad,
        normbias_grad,
        crossq_gaingrad,
        crossk_gaingrad,
        query_gaingrad,
        key_gaingrad,
        table_term,
    )
    return (layer_output, latents_gradient, context_gradient, modulation_gradient, pairs, gains)


def body(
    latents,
    context,
    modulation,
    cotangent,
    modtable,
    selfquery,
    selfkey,
    selfvalue,
    selfout,
    querygain,
    keygain,
    normgain,
    normbias,
    crossquery,
    crosskey,
    crossvalue,
    crossout,
    crossqgain,
    crosskgain,
    upmatrix,
    downmatrix,
):
    shards = (
        modtable,
        selfquery,
        selfkey,
        selfvalue,
        selfout,
        querygain,
        keygain,
        normgain,
        normbias,
        crossquery,
        crosskey,
        crossvalue,
        crossout,
        crossqgain,
        crosskgain,
        upmatrix,
        downmatrix,
    )
    outputs = []
    latent_grads = []
    context_grads = []
    modulation_grads = []
    pair_lists = []
    gain_total = None
    for index in range(latents.shape[0]):
        result = run_clip(
            latents[index : index + 1],
            context[index : index + 1],
            modulation[index : index + 1],
            cotangent[index : index + 1],
            shards,
        )
        outputs.append(result[0])
        latent_grads.append(result[1])
        context_grads.append(result[2])
        modulation_grads.append(result[3])
        pair_lists.append(result[4])
        if gain_total is None:
            gain_total = result[5]
        else:
            gain_total = jax.tree.map(lambda left, right: left + right, gain_total, result[5])
    terms = []
    for number in range(10):
        operand = jnp.concatenate([entry[number][0] for entry in pair_lists], axis=0)
        gradient = jnp.concatenate([entry[number][1] for entry in pair_lists], axis=0)
        terms.append(weight_term(operand, gradient))
    (
        down_term,
        up_term,
        crossout_term,
        crossquery_term,
        crosskey_term,
        crossvalue_term,
        selfquery_term,
        selfkey_term,
        selfvalue_term,
        selfout_term,
    ) = terms
    (
        normgain_grad,
        normbias_grad,
        crossq_gaingrad,
        crossk_gaingrad,
        query_gaingrad,
        key_gaingrad,
        table_term,
    ) = gain_total
    early = (
        lax.psum_scatter(down_term, ("dp", "seq"), scatter_dimension=0, tiled=True),
        lax.psum_scatter(up_term, ("dp", "seq"), scatter_dimension=0, tiled=True),
        lax.psum_scatter(crossout_term, ("dp", "seq"), scatter_dimension=0, tiled=True),
        lax.psum_scatter(crossquery_term, ("dp", "seq"), scatter_dimension=0, tiled=True),
        lax.psum_scatter(crosskey_term, ("dp", "seq"), scatter_dimension=0, tiled=True),
        lax.psum_scatter(crossvalue_term, ("dp", "seq"), scatter_dimension=0, tiled=True),
        lax.psum_scatter(normgain_grad, ("dp", "seq"), scatter_dimension=0, tiled=True),
        lax.psum_scatter(normbias_grad, ("dp", "seq"), scatter_dimension=0, tiled=True),
        lax.psum_scatter(crossq_gaingrad, ("dp", "seq"), scatter_dimension=0, tiled=True),
        lax.psum_scatter(crossk_gaingrad, ("dp", "seq"), scatter_dimension=0, tiled=True),
    )
    late = (
        lax.psum_scatter(selfquery_term, ("dp", "seq"), scatter_dimension=0, tiled=True),
        lax.psum_scatter(selfkey_term, ("dp", "seq"), scatter_dimension=0, tiled=True),
        lax.psum_scatter(selfvalue_term, ("dp", "seq"), scatter_dimension=0, tiled=True),
        lax.psum_scatter(selfout_term, ("dp", "seq"), scatter_dimension=0, tiled=True),
        lax.psum_scatter(table_term.T, ("dp", "seq"), scatter_dimension=0, tiled=True),
        lax.psum_scatter(query_gaingrad, ("dp", "seq"), scatter_dimension=0, tiled=True),
        lax.psum_scatter(key_gaingrad, ("dp", "seq"), scatter_dimension=0, tiled=True),
    )
    layer_output = jnp.concatenate(outputs, axis=0)
    latents_gradient = jnp.concatenate(latent_grads, axis=0)
    context_gradient = jnp.concatenate(context_grads, axis=0)
    modulation_gradient = jnp.concatenate(modulation_grads, axis=0)
    return (
        layer_output,
        latents_gradient,
        context_gradient,
        modulation_gradient,
        late[4].T,
        late[0],
        late[1],
        late[2],
        late[3],
        late[5],
        late[6],
        early[6],
        early[7],
        early[3],
        early[4],
        early[5],
        early[2],
        early[8],
        early[9],
        early[1],
        early[0],
    )


def solution(mesh):
    return jax.shard_map(
        body,
        mesh=mesh,
        in_specs=(
            P("dp", "seq", None),
            P("dp", "seq", None),
            P("dp", None, None),
            P("dp", "seq", None),
            P(None, ("dp", "seq")),
            P(("dp", "seq"), None),
            P(("dp", "seq"), None),
            P(("dp", "seq"), None),
            P(("dp", "seq"), None),
            P(("dp", "seq")),
            P(("dp", "seq")),
            P(("dp", "seq")),
            P(("dp", "seq")),
            P(("dp", "seq"), None),
            P(("dp", "seq"), None),
            P(("dp", "seq"), None),
            P(("dp", "seq"), None),
            P(("dp", "seq")),
            P(("dp", "seq")),
            P(("dp", "seq"), None),
            P(("dp", "seq"), None),
        ),
        out_specs=(
            P("dp", "seq", None),
            P("dp", "seq", None),
            P("dp", "seq", None),
            P("dp", None, None),
            P(None, ("dp", "seq")),
            P(("dp", "seq"), None),
            P(("dp", "seq"), None),
            P(("dp", "seq"), None),
            P(("dp", "seq"), None),
            P(("dp", "seq")),
            P(("dp", "seq")),
            P(("dp", "seq")),
            P(("dp", "seq")),
            P(("dp", "seq"), None),
            P(("dp", "seq"), None),
            P(("dp", "seq"), None),
            P(("dp", "seq"), None),
            P(("dp", "seq")),
            P(("dp", "seq")),
            P(("dp", "seq"), None),
            P(("dp", "seq"), None),
        ),
        check_vma=False,
    )
```

profile of v0, /device:TPU:0, one launch (start us, length us, event | category | flops | bytes accessed | tf_op | source)
XLA Modules:
  0.0 4509.3 jit_solution(10381239823068575462)
XLA Ops:
  10.6 44.0 all-gather
  167.6 41.8 all-gather.26.cloned.1.call-done
  217.9 56.9 %all-gather.34.cloned.1.call-done = bf16[1536,1536]{1,0:T(8,128)(2,1)} async-done(((bf16[48,1536]{1,0:T(8,128)(2,1)}), bf16[1536,1536]{1,0:T(8,128)(2,1)}) %all-gather.34.cloned.1.call-update) | async-done | bytes 4718608 | tf_op jit(solution)/shard_map/all_gather | solution.py:162
  282.0 58.2 %all-gather.38.cloned.1.call-done = bf16[1536,1536]{1,0:T(8,128)(2,1)} async-done(((bf16[48,1536]{1,0:T(8,128)(2,1)}), bf16[1536,1536]{1,0:T(8,128)(2,1)}) %all-gather.38.cloned.1.call-update) | async-done | bytes 4718608 | tf_op jit(solution)/shard_map/all_gather | solution.py:163
  355.6 50.5 %all-gather.24.cloned.1.call-done = bf16[12,1,2048,128]{2,3,0,1:T(8,128)(2,1)} async-done(((bf16[12,1,256,128]{2,3,0,1:T(8,128)(2,1)}), bf16[12,1,2048,128]{2,3,0,1:T(8,128)(2,1)}) %all-gather.24.cloned.1.call-update) | async-done | bytes 6291472 | tf_op jit(solution)/shard_map/all_gather | solution.py:215
  414.9 56.2 %all-gather.28.cloned.1.call-done = bf16[12,1,2048,128]{2,3,0,1:T(8,128)(2,1)} async-done(((bf16[12,1,256,128]{2,3,0,1:T(8,128)(2,1)}), bf16[12,1,2048,128]{2,3,0,1:T(8,128)(2,1)}) %all-gather.28.cloned.1.call-update) | async-done | bytes 6291472 | tf_op jit(solution)/shard_map/all_gather | solution.py:216
  479.9 45.5 %while.112 = (s32[]{:T(128)}, bf16[12,1,256,128]{2,3,0,1:T(8,128)(2,1)S(1)}, f32[12,1,256,1]{2,3,1,0:T(1,128)S(1)}, f32[12,1,256,1]{2,3,1,0:T(1,128)S(1)}, bf16[...) while((s32[]{:T(128)}, ...), condition=%wide.region_7.8_spmd, body=%wide.region_4.7_spmd.sunk | while | flops 272104960 | bytes 7548001 | solution.py:218
  542.6 58.8 %all-gather.32.cloned.1.call-done = bf16[1536,1536]{1,0:T(8,128)(2,1)} async-done(((bf16[48,1536]{1,0:T(8,128)(2,1)}), bf16[1536,1536]{1,0:T(8,128)(2,1)}) %all-gather.32.cloned.1.call-update) | async-done | bytes 4718608 | tf_op jit(solution)/shard_map/all_gather | solution.py:161
  654.2 40.3 while.113
  726.7 161.4 %all-gather.44.cloned.1.call-done = bf16[1536,8960]{1,0:T(8,128)(2,1)} async-done(((bf16[48,8960]{1,0:T(8,128)(2,1)}), bf16[1536,8960]{1,0:T(8,128)(2,1)}) %all-gather.44.cloned.1.call-update) | async-done | bytes 27525136 | tf_op jit(solution)/shard_map/all_gather | solution.py:167
  903.3 151.9 %all-gather.46.cloned.1.call-done = bf16[8960,1536]{1,0:T(8,128)(2,1)} async-done(((bf16[280,1536]{1,0:T(8,128)(2,1)}), bf16[8960,1536]{1,0:T(8,128)(2,1)}) %all-gather.46.cloned.1.call-update) | async-done | bytes 27525136 | tf_op jit(solution)/shard_map/all_gather | solution.py:168
  1103.0 96.1 %while.116 = (s32[]{:T(128)}, f32[12,1,256,128]{2,3,0,1:T(8,128)}, bf16[12,1,512,128]{3,2,1,0:T(8,128)(2,1)}, bf16[12,1,512,128]{3,2,1,0:T(8,128)(2,1)}, bf16[12...) while((s32[]{:T(128)}, f32[12,1,256,128]{2,3,0,1:T(8,128)}, ...), condition=%wide.region_40.41_spmd, body=%wide.region_38.40_spmd.sunk | while | flops 169082624 | bytes 5256313 | solution.py:282
  1223.4 101.8 %while.117 = (s32[]{:T(128)}, f32[12,1,256,128]{3,2,1,0:T(8,128)S(1)}, bf16[12,1,2048,128]{3,2,1,0:T(8,128)(2,1)}, bf16[12,1,2048,128]{2,3,0,1:T(8,128)(2,1)}, b...) while((s32[]{:T(128)}, ...), condition=%wide.region_46.47_spmd, body=%wide.region_44.46_spmd.sunk | while | flops 676331264 | bytes 19805304 | solution.py:311
  1327.1 66.3 %reduce-scatter.28.cloned.1.call-done = bf16[12,1,256,128]{3,2,1,0:T(8,128)(2,1)} async-done(((bf16[12,1,2048,128]{3,2,1,0:T(8,128)(2,1)}), bf16[12,1,256,128]{3,2,1,0:T(8,128)(2,1)}) %reduce-scatter.28.cloned.1.call-update) | async-done | bytes 786448 | tf_op jit(solution)/shard_map/reduce_scatter | solution.py:316
  1528.3 41.4 all-gather.48.cloned.1.call-done
  1578.5 56.2 %all-gather.50.cloned.1.call-done = bf16[12,1,2048,128]{2,3,0,1:T(8,128)(2,1)} async-done(((bf16[12,1,256,128]{2,3,0,1:T(8,128)(2,1)}), bf16[12,1,2048,128]{2,3,0,1:T(8,128)(2,1)}) %all-gather.50.cloned.1.call-update) | async-done | bytes 6291472 | tf_op jit(solution)/shard_map/all_gather | solution.py:216
  1643.4 44.8 while.114
  1705.6 40.3 while.115
  1857.9 96.4 %while.118 = (s32[]{:T(128)}, f32[12,1,256,128]{2,3,0,1:T(8,128)}, bf16[12,1,512,128]{3,2,1,0:T(8,128)(2,1)}, bf16[12,1,512,128]{3,2,1,0:T(8,128)(2,1)}, bf16[12...) while((s32[]{:T(128)}, f32[12,1,256,128]{2,3,0,1:T(8,128)}, ...), condition=%wide.region_57.58_spmd, body=%wide.region_55.57_spmd.sunk | while | flops 169082624 | bytes 5256313 | solution.py:282
  1979.3 109.7 %while.119 = (s32[]{:T(128)}, f32[12,1,256,128]{3,2,1,0:T(8,128)S(1)}, bf16[12,1,2048,128]{3,2,1,0:T(8,128)(2,1)}, bf16[12,1,2048,128]{2,3,0,1:T(8,128)(2,1)}, b...) while((s32[]{:T(128)}, ...), condition=%wide.region_63.64_spmd, body=%wide.region_61.63_spmd.sunk | while | flops 676331264 | bytes 19805304 | solution.py:311
  2094.5 62.7 %reduce-scatter.32.cloned.1.call-done = bf16[12,1,256,128]{3,2,1,0:T(8,128)(2,1)} async-done(((bf16[12,1,2048,128]{3,2,1,0:T(8,128)(2,1)}), bf16[12,1,256,128]{3,2,1,0:T(8,128)(2,1)}) %reduce-scatter.32.cloned.1.call-update) | async-done | bytes 786448 | tf_op jit(solution)/shard_map/reduce_scatter | solution.py:316
  2187.0 40.7 reduce-scatter.34.cloned.1.call-done
  2495.3 40.0 all-reduce.21
  2573.0 142.3 %reduce-scatter.52.cloned.1.call-done = f32[48,1536]{1,0:T(8,128)} async-done(((f32[1536,1536]{1,0:T(8,128)}), f32[48,1536]{1,0:T(8,128)}) %reduce-scatter.52.cloned.1.call-update) | async-done | bytes 294928 | tf_op jit(solution)/shard_map/reduce_scatter | solution.py:463
  2715.3 141.0 %reduce-scatter.54.cloned.1.call-done = f32[48,1536]{1,0:T(8,128)} async-done(((f32[1536,1536]{1,0:T(8,128)}), f32[48,1536]{1,0:T(8,128)}) %reduce-scatter.54.cloned.1.call-update) | async-done | bytes 294928 | tf_op jit(solution)/shard_map/reduce_scatter | solution.py:462
  2856.3 142.2 %reduce-scatter.60.cloned.1.call-done = f32[48,1536]{1,0:T(8,128)} async-done(((f32[1536,1536]{1,0:T(8,128)}), f32[48,1536]{1,0:T(8,128)}) %reduce-scatter.60.cloned.1.call-update) | async-done | bytes 294928
  2998.5 141.0 %reduce-scatter.62.cloned.1.call-done = f32[48,1536]{1,0:T(8,128)} async-done(((f32[1536,1536]{1,0:T(8,128)}), f32[48,1536]{1,0:T(8,128)}) %reduce-scatter.62.cloned.1.call-update) | async-done | bytes 294928
  3139.5 141.9 %reduce-scatter.44.cloned.1.call-done = f32[48,1536]{1,0:T(8,128)} async-done(((f32[1536,1536]{1,0:T(8,128)}), f32[48,1536]{1,0:T(8,128)}) %reduce-scatter.44.cloned.1.call-update) | async-done | bytes 294928 | tf_op jit(solution)/shard_map/reduce_scatter | solution.py:472
  3281.4 141.1 %reduce-scatter.46.cloned.1.call-done = f32[48,1536]{1,0:T(8,128)} async-done(((f32[1536,1536]{1,0:T(8,128)}), f32[48,1536]{1,0:T(8,128)}) %reduce-scatter.46.cloned.1.call-update) | async-done | bytes 294928 | tf_op jit(solution)/shard_map/reduce_scatter | solution.py:473
  3422.5 142.1 %reduce-scatter.48.cloned.1.call-done = f32[48,1536]{1,0:T(8,128)} async-done(((f32[1536,1536]{1,0:T(8,128)}), f32[48,1536]{1,0:T(8,128)}) %reduce-scatter.48.cloned.1.call-update) | async-done | bytes 294928 | tf_op jit(solution)/shard_map/reduce_scatter | solution.py:474
  3564.6 468.2 %reduce-scatter.56.cloned.1.call-done = f32[48,8960]{1,0:T(8,128)} async-done(((f32[1536,8960]{1,0:T(8,128)}), f32[48,8960]{1,0:T(8,128)}) %reduce-scatter.56.cloned.1.call-update) | async-done | bytes 1720336 | tf_op jit(solution)/shard_map/reduce_scatter | solution.py:461
  4032.8 469.5 %reduce-scatter.64.cloned.1.call-done = f32[280,1536]{1,0:T(8,128)} async-done(((f32[8960,1536]{1,0:T(8,128)}), f32[280,1536]{1,0:T(8,128)}) %reduce-scatter.64.cloned.1.call-update) | async-done | bytes 1720336
  (1302 shorter events, 1573.0 us)
Async XLA Ops:
  8.7 200.7 %all-gather.26.cloned.1.call-start = ((), (), s32[]{:S(2)}) async-start(), calls=%async_computation.22 | async-start | bytes 4866048 | tf_op jit(solution)/shard_map/all_gather | solution.py:155
  9.4 265.3 %all-gather.34.cloned.1.call-start = ((), (), s32[]{:S(2)}) async-start(), calls=%async_computation.26 | async-start | bytes 4866048 | tf_op jit(solution)/shard_map/all_gather | solution.py:162
  10.0 330.1 %all-gather.38.cloned.1.call-start = ((), (), s32[]{:S(2)}) async-start(), calls=%async_computation.28 | async-start | bytes 4866048 | tf_op jit(solution)/shard_map/all_gather | solution.py:163
  10.6 395.6 %all-gather.24.cloned.1.call-start = ((), (), s32[]{:S(2)}) async-start(), calls=%async_computation.21 | async-start | bytes 7077888 | tf_op jit(solution)/shard_map/all_gather | solution.py:215
  167.2 303.9 %all-gather.28.cloned.1.call-start = ((), (), s32[]{:S(2)}) async-start(), calls=%async_computation.23 | async-start | bytes 7077888 | tf_op jit(solution)/shard_map/all_gather | solution.py:216
  216.3 319.6 %all-gather.30.cloned.1.call-start = ((), (), s32[]{:S(2)}) async-start(), calls=%async_computation.24 | async-start | bytes 4866048 | tf_op jit(solution)/shard_map/all_gather | solution.py:156
  217.1 384.3 %all-gather.32.cloned.1.call-start = ((), (), s32[]{:S(2)}) async-start(), calls=%async_computation.25 | async-start | bytes 4866048 | tf_op jit(solution)/shard_map/all_gather | solution.py:161
  217.8 409.5 %all-gather.36.cloned.1.call-start = ((), (), s32[]{:S(2)}) async-start(), calls=%async_computation.27 | async-start | bytes 1769472 | tf_op jit(solution)/shard_map/all_gather | solution.py:230
  281.9 372.3 %all-gather.40.cloned.1.call-start = ((), (), s32[]{:S(2)}) async-start(), calls=%async_computation.29 | async-start | bytes 1769472 | tf_op jit(solution)/shard_map/all_gather | solution.py:231
  344.3 375.9 %all-gather.42.cloned.1.call-start = ((), (), s32[]{:S(2)}) async-start(), calls=%async_computation.30 | async-start | bytes 4866048 | tf_op jit(solution)/shard_map/all_gather | solution.py:164
  344.9 543.2 %all-gather.44.cloned.1.call-start = ((), (), s32[]{:S(2)}) async-start(), calls=%async_computation.31 | async-start | bytes 28385280 | tf_op jit(solution)/shard_map/all_gather | solution.py:167
  345.7 709.5 %all-gather.46.cloned.1.call-start = ((), (), s32[]{:S(2)}) async-start(), calls=%async_computation.32 | async-start | bytes 28385280 | tf_op jit(solution)/shard_map/all_gather | solution.py:168
  346.2 1047.2 %reduce-scatter.28.cloned.1.call-start = ((), (), s32[]{:S(2)}) async-start(), calls=%async_computation.37 | async-start | bytes 7077888 | tf_op jit(solution)/shard_map/reduce_scatter | solution.py:316
  1325.8 192.0 %reduce-scatter.36.cloned.1.call-start = ((), (), s32[]{:S(2)}) async-start(), calls=%async_computation.41 | async-start | bytes 1769472 | tf_op jit(solution)/shard_map/reduce_scatter | solution.py:287
  1327.0 242.7 %all-gather.48.cloned.1.call-start = ((), (), s32[]{:S(2)}) async-start(), calls=%async_computation.33 | async-start | bytes 7077888 | tf_op jit(solution)/shard_map/all_gather | solution.py:215
  1513.0 192.5 %all-gather.54.cloned.1.call-start = ((), (), s32[]{:S(2)}) async-start(), calls=%async_computation.36 | async-start | bytes 1769472 | tf_op jit(solution)/shard_map/all_gather | solution.py:231
  1517.8 187.8 %all-gather.52.cloned.1.call-start = ((), (), s32[]{:S(2)}) async-start(), calls=%async_computation.35 | async-start | bytes 1769472 | tf_op jit(solution)/shard_map/all_gather | solution.py:230
  1521.8 635.4 %reduce-scatter.32.cloned.1.call-start = ((), (), s32[]{:S(2)}) async-start(), calls=%async_computation.39 | async-start | bytes 7077888 | tf_op jit(solution)/shard_map/reduce_scatter | solution.py:316
  2089.8 173.4 %reduce-scatter.40.cloned.1.call-start = ((), (), s32[]{:S(2)}) async-start(), calls=%async_computation.43 | async-start | bytes 1769472 | tf_op jit(solution)/shard_map/reduce_scatter | solution.py:287
  2090.3 207.3 %reduce-scatter.38.cloned.1.call-start = ((), (), s32[]{:S(2)}) async-start(), calls=%async_computation.42 | async-start | bytes 1769472 | tf_op jit(solution)/shard_map/reduce_scatter | solution.py:290
  2091.1 241.4 %reduce-scatter.42.cloned.1.call-start = ((), (), s32[]{:S(2)}) async-start(), calls=%async_computation.44 | async-start | bytes 1769472 | tf_op jit(solution)/shard_map/reduce_scatter | solution.py:290
  2094.4 450.0 %reduce-scatter.58.cloned.1.call-start = ((), (), s32[]{:S(2)}) async-start(), calls=%async_computation.52 | async-start | bytes 811008
  2236.2 336.8 %reduce-scatter.50.cloned.1.call-start = ((), (), s32[]{:S(2)}) async-start(), calls=%async_computation.48 | async-start | bytes 9732096 | tf_op jit(solution)/shard_map/reduce_scatter | solution.py:475
  2242.5 472.8 %reduce-scatter.52.cloned.1.call-start = ((), (), s32[]{:S(2)}) async-start(), calls=%async_computation.49 | async-start | bytes 9732096 | tf_op jit(solution)/shard_map/reduce_scatter | solution.py:463
  2250.4 605.9 %reduce-scatter.54.cloned.1.call-start = ((), (), s32[]{:S(2)}) async-start(), calls=%async_computation.50 | async-start | bytes 9732096 | tf_op jit(solution)/shard_map/reduce_scatter | solution.py:462
  2258.1 740.3 %reduce-scatter.60.cloned.1.call-start = ((), (), s32[]{:S(2)}) async-start(), calls=%async_computation.53 | async-start | bytes 9732096
  2279.9 859.6 %reduce-scatter.62.cloned.1.call-start = ((), (), s32[]{:S(2)}) async-start(), calls=%async_computation.54 | async-start | bytes 9732096
  2348.2 933.2 %reduce-scatter.44.cloned.1.call-start = ((), (), s32[]{:S(2)}) async-start(), calls=%async_computation.45 | async-start | bytes 9732096 | tf_op jit(solution)/shard_map/reduce_scatter | solution.py:472
  2356.1 1066.4 %reduce-scatter.46.cloned.1.call-start = ((), (), s32[]{:S(2)}) async-start(), calls=%async_computation.46 | async-start | bytes 9732096 | tf_op jit(solution)/shard_map/reduce_scatter | solution.py:473
  2363.7 1200.9 %reduce-scatter.48.cloned.1.call-start = ((), (), s32[]{:S(2)}) async-start(), calls=%async_computation.47 | async-start | bytes 9732096 | tf_op jit(solution)/shard_map/reduce_scatter | solution.py:474
  2374.6 1658.2 %reduce-scatter.56.cloned.1.call-start = ((), (), s32[]{:S(2)}) async-start(), calls=%async_computation.51 | async-start | bytes 56770560 | tf_op jit(solution)/shard_map/reduce_scatter | solution.py:461
  2402.3 2099.9 %reduce-scatter.64.cloned.1.call-start = ((), (), s32[]{:S(2)}) async-start(), calls=%async_computation.55 | async-start | bytes 56770560
  (191 other events, 2731.9 us)
Sparse Core Ops, SparseCore 0:
  11.1 66.9 all-gather.21
  81.0 62.7 all-gather.19
  146.9 62.4 all-gather.25
  212.2 62.4 all-gather.33
  277.6 62.4 all-gather.37
  342.1 63.9 all-gather.23
  407.7 63.3 all-gather.27
  474.2 61.6 all-gather.29
  538.9 62.4 all-gather.31
  657.0 63.1 all-gather.41
  723.3 164.7 all-gather.43
  891.0 164.1 all-gather.45
  1325.4 67.9 reduce-scatter.27
  1395.6 68.1 reduce-scatter.29
  1466.5 32.5 reduce-scatter.35
  1506.0 63.6 all-gather.47
  1571.3 63.3 all-gather.49
  2089.1 67.9 reduce-scatter.31
  2159.5 68.1 reduce-scatter.33
  2230.4 32.6 reduce-scatter.39
  2265.4 32.1 reduce-scatter.37
  2337.5 93.2 reduce-scatter.57
  2437.3 135.6 reduce-scatter.49
  2580.5 134.7 reduce-scatter.51
  2721.6 134.6 reduce-scatter.53
  2863.8 134.6 reduce-scatter.59
  3005.0 134.4 reduce-scatter.61
  3146.8 134.5 reduce-scatter.43
  3287.9 134.5 reduce-scatter.45
  3430.0 134.5 reduce-scatter.47
  3571.5 461.2 reduce-scatter.55
  4040.8 461.4 reduce-scatter.63
  (5 shorter events, 128.2 us)
where the time goes:
time: 4530 us; the launch traced here: 4510 us
  waiting for transfers between devices  3070 us (68%)
  matrix products  901 us (20%)
  local copies, waits for them, and re-layouts  221 us (5%)
  blocking collectives  148 us (3%)
  other arithmetic  141 us (3%)
    unnamed x41, waiting for transfers between devices  762 us
    reduce_scatter x1, waiting for transfers between devices, body(): lax.psum_scatter(up_term, ('dp', 'seq'), scatter_dimension=0, tiled=True)  468 us
    all_gather x1, waiting for transfers between devices, run_clip(): lax.all_gather(upmatrix, ('dp', 'seq'), axis=0, tiled=True)  161 us
    all_gather x1, waiting for transfers between devices, run_clip(): lax.all_gather(downmatrix, ('dp', 'seq'), axis=0, tiled=True)  152 us
    dot_general x96, matrix products, head_scores(): jnp.einsum('crd,ckd->crk', head_query, head_key, preferred_element_type=j...  145 us
    reduce_scatter x1, waiting for transfers between devices, body(): lax.psum_scatter(crossquery_term, ('dp', 'seq'), scatter_dimension=0, til...  142 us
    reduce_scatter x1, waiting for transfers between devices, body(): lax.psum_scatter(selfvalue_term, ('dp', 'seq'), scatter_dimension=0, tile...  142 us
    reduce_scatter x1, waiting for transfers between devices, body(): lax.psum_scatter(selfquery_term, ('dp', 'seq'), scatter_dimension=0, tile...  142 us
  transfers between devices with their start and end apart: 37, of which 32 were waited for; matrix products, arithmetic and copies ran while one was open for 13% of the time, Pallas kernels for 0%

commit v1 on v0

v1 whole, which is shorter than its diff:
```python
import functools
import math

import jax
import jax.numpy as jnp
import numpy as np
from jax import lax
from jax.experimental import pallas as pl
from jax.experimental.pallas import tpu as pltpu
from jax.sharding import PartitionSpec as P

HEADS = 12
HEAD_DIM = 128
GRID_H = 32
GRID_W = 32
EPS = 1e-06
BF = jnp.bfloat16
F32 = jnp.float32
SCALE = HEAD_DIM ** (-0.5)
SCALE_LOG2 = SCALE * math.log2(math.e)


def layer_norm(values):
    center = values - jnp.mean(values, axis=-1, keepdims=True)
    return center * lax.rsqrt(jnp.mean(center * center, axis=-1, keepdims=True) + EPS)


def layer_norm_back(values, gradient):
    center = values - jnp.mean(values, axis=-1, keepdims=True)
    inverse = lax.rsqrt(jnp.mean(center * center, axis=-1, keepdims=True) + EPS)
    normed = center * inverse
    return inverse * (
        gradient
        - jnp.mean(gradient, axis=-1, keepdims=True)
        - normed * jnp.mean(gradient * normed, axis=-1, keepdims=True)
    )


def gelu_tanh(values):
    return jax.nn.gelu(values, approximate=True)


def dot_nn(left, right, out=F32):
    return lax.dot_general(left, right, (((1,), (0,)), ((), ())), preferred_element_type=F32).astype(out)


def dot_nt(left, right, out=F32):
    return lax.dot_general(left, right, (((1,), (1,)), ((), ())), preferred_element_type=F32).astype(out)


def dot_tn(left, right, out=F32):
    return lax.dot_general(left, right, (((0,), (0,)), ((), ())), preferred_element_type=F32).astype(out)


def rotary_tables(positions):
    pairs = HEAD_DIM // 2
    side = pairs // 3
    lead = pairs - 2 * side

    def rates(number):
        return np.power(np.float32(10000.0), -np.arange(number, dtype=np.float32) / np.float32(number))

    def lanes(start, values):
        row = np.zeros((pairs,), np.float32)
        row[start : start + len(values)] = values
        return np.repeat(row, 2)[None]

    frame = (positions // (GRID_H * GRID_W)).astype(F32)[:, None]
    line = (positions // GRID_W % GRID_H).astype(F32)[:, None]
    column = (positions % GRID_W).astype(F32)[:, None]
    angles = (
        frame * lanes(0, rates(lead))
        + line * lanes(lead, rates(side))
        + column * lanes(lead + side, rates(side))
    )
    even = (np.arange(HEAD_DIM) % 2 == 0)[None]
    sine = jnp.sin(angles)
    return jnp.cos(angles), jnp.where(even, -sine, 0.0), jnp.where(even, 0.0, sine)


def turn(values, cosine, following, previous):
    return (
        values * cosine
        + pltpu.roll(values, HEAD_DIM - 1, 1) * following
        + pltpu.roll(values, 1, 1) * previous
    )


def head_lanes(head):
    return slice(head * HEAD_DIM, (head + 1) * HEAD_DIM)


def row_block(rows):
    return 128 if rows % 128 == 0 else rows


def row_spec(block, width):
    return pl.BlockSpec((block, width), lambda step: (step, 0))


def fixed_spec(width):
    return pl.BlockSpec((1, width), lambda step: (0, 0))


def params(mebibytes):
    return pltpu.CompilerParams(vmem_limit_bytes=mebibytes * 2**20)


def normed_turned(raw_ref, gain_ref, tables, write):
    raw = raw_ref[...]
    inverse = lax.rsqrt(jnp.mean(raw * raw, axis=-1, keepdims=True) + EPS)
    normed = raw * inverse * gain_ref[...]
    for head in range(HEADS):
        piece = normed[:, head_lanes(head)]
        if tables is not None:
            piece = turn(piece, *tables)
        write(head, piece.astype(BF))


def self_post(raw, gain_query, gain_key, tables, groups):
    rows, width = raw.shape[0], raw.shape[1] // 3
    block = row_block(rows)
    per_group = HEADS // groups

    def kernel(query_ref, key_ref, value_ref, gq_ref, gk_ref, cos_ref, next_ref, last_ref, query_out, *outs):
        turns = (cos_ref[...], next_ref[...], last_ref[...])

        def write_query(head, piece):
            query_out[:, head_lanes(head)] = piece

        def write_key(head, piece):
            start = (head % per_group) * 2 * HEAD_DIM
            outs[head // per_group][:, start : start + HEAD_DIM] = piece

        normed_turned(query_ref, gq_ref, turns, write_query)
        normed_turned(key_ref, gk_ref, turns, write_key)
        for head in range(HEADS):
            start = (head % per_group) * 2 * HEAD_DIM + HEAD_DIM
            outs[head // per_group][:, start : start + HEAD_DIM] = value_ref[:, head_lanes(head)].astype(BF)

    out_width = per_group * 2 * HEAD_DIM
    return pl.pallas_call(
        kernel,
        grid=(rows // block,),
        in_specs=[pl.BlockSpec((block, width), lambda step, part=part: (step, part)) for part in range(3)]
        + [fixed_spec(width)] * 2
        + [row_spec(block, HEAD_DIM)] * 3,
        out_specs=[row_spec(block, width)] + [row_spec(block, out_width)] * groups,
        out_shape=[jax.ShapeDtypeStruct((rows, width), BF)]
        + [jax.ShapeDtypeStruct((rows, out_width), BF)] * groups,
        compiler_params=params(32),
        cost_estimate=pl.CostEstimate(flops=rows * width * 20, bytes_accessed=rows * width * 18, transcendentals=0),
        name="self_post",
    )(raw, raw, raw, gain_query, gain_key, *tables)


def query_post(raw, gain):
    rows, width = raw.shape
    block = row_block(rows)

    def kernel(raw_ref, gain_ref, out_ref):
        def write(head, piece):
            out_ref[:, head_lanes(head)] = piece

        normed_turned(raw_ref, gain_ref, None, write)

    return pl.pallas_call(
        kernel,
        grid=(rows // block,),
        in_specs=[row_spec(block, width), fixed_spec(width)],
        out_specs=row_spec(block, width),
        out_shape=jax.ShapeDtypeStruct((rows, width), BF),
        compiler_params=params(24),
        cost_estimate=pl.CostEstimate(flops=rows * width * 10, bytes_accessed=rows * width * 6, transcendentals=0),
        name="query_post",
    )(raw, gain)


def text_post(raw, gain):
    rows, width = raw.shape[0], raw.shape[1] // 2
    block = row_block(rows)

    def kernel(key_ref, value_ref, gain_ref, out_ref):
        def write(head, piece):
            out_ref[:, 2 * head * HEAD_DIM : (2 * head + 1) * HEAD_DIM] = piece

        normed_turned(key_ref, gain_ref, None, write)
        for head in range(HEADS):
            start = (2 * head + 1) * HEAD_DIM
            out_ref[:, start : start + HEAD_DIM] = value_ref[:, head_lanes(head)].astype(BF)

    return pl.pallas_call(
        kernel,
        grid=(rows // block,),
        in_specs=[pl.BlockSpec((block, width), lambda step, part=part: (step, part)) for part in range(2)]
        + [fixed_spec(width)],
        out_specs=row_spec(block, 2 * width),
        out_shape=jax.ShapeDtypeStruct((rows, 2 * width), BF),
        compiler_params=params(24),
        cost_estimate=pl.CostEstimate(flops=rows * width * 10, bytes_accessed=rows * width * 12, transcendentals=0),
        name="text_post",
    )(raw, raw, gain)


def norm_back(raw, gain, gradient):
    inverse = lax.rsqrt(jnp.mean(raw * raw, axis=-1, keepdims=True) + EPS)
    normed = raw * inverse
    gained = gradient * gain
    back = (gained - normed * jnp.mean(gained * normed, axis=-1, keepdims=True)) * inverse
    return back, jnp.sum(gradient * normed, axis=0, keepdims=True)


def turned_back(piece, turns):
    return piece if turns is None else turn(piece, turns[0], -turns[1], -turns[2])


def accumulate(ref, term):
    @pl.when(pl.program_id(0) == 0)
    def _():
        ref[...] = jnp.zeros_like(ref)

    ref[...] += term


def self_query_back(gradients, raw, gain, tables):
    rows, width = raw.shape[0], raw.shape[1] // 3
    block = row_block(rows)
    groups = len(gradients)
    per_group = HEADS // groups

    def kernel(*refs):
        grads = refs[:groups]
        raw_ref, gain_ref, cos_ref, next_ref, last_ref, low_ref, gain_out = refs[groups:]
        turns = (cos_ref[...], next_ref[...], last_ref[...])
        pieces = [
            turned_back(grads[head // per_group][:, head_lanes(head % per_group)], turns)
            for head in range(HEADS)
        ]
        back, term = norm_back(raw_ref[...], gain_ref[...], jnp.concatenate(pieces, axis=1))
        low_ref[...] = back.astype(BF)
        accumulate(gain_out, term)

    return pl.pallas_call(
        kernel,
        grid=(rows // block,),
        in_specs=[row_spec(block, per_group * HEAD_DIM)] * groups
        + [row_spec(block, width), fixed_spec(width)]
        + [row_spec(block, HEAD_DIM)] * 3,
        out_specs=[row_spec(block, width), fixed_spec(width)],
        out_shape=[jax.ShapeDtypeStruct((rows, width), BF), jax.ShapeDtypeStruct((1, width), F32)],
        compiler_params=params(32),
        cost_estimate=pl.CostEstimate(flops=rows * width * 15, bytes_accessed=rows * width * 10, transcendentals=0),
        name="self_query_back",
    )(*gradients, raw, gain, *tables)


def self_keyvalue_back(gradients, raw, gain, tables):
    rows, width = raw.shape[0], raw.shape[1] // 3
    block = row_block(rows)
    groups = len(gradients)
    per_group = HEADS // groups

    def kernel(*refs):
        grads = refs[:groups]
        raw_ref, gain_ref, cos_ref, next_ref, last_ref, low_ref, gain_out = refs[groups:]
        turns = (cos_ref[...], next_ref[...], last_ref[...])
        pieces = []
        for head in range(HEADS):
            start = (head % per_group) * 2 * HEAD_DIM
            ref = grads[head // per_group]
            pieces.append(turned_back(ref[:, start : start + HEAD_DIM], turns))
            value = ref[:, start + HEAD_DIM : start + 2 * HEAD_DIM].astype(BF)
            low_ref[:, width + head * HEAD_DIM : width + (head + 1) * HEAD_DIM] = value
        back, term = norm_back(raw_ref[...], gain_ref[...], jnp.concatenate(pieces, axis=1))
        low_ref[:, :width] = back.astype(BF)
        accumulate(gain_out, term)

    return pl.pallas_call(
        kernel,
        grid=(rows // block,),
        in_specs=[row_spec(block, per_group * 2 * HEAD_DIM)] * groups
        + [pl.BlockSpec((block, width), lambda step: (step, 1)), fixed_spec(width)]
        + [row_spec(block, HEAD_DIM)] * 3,
        out_specs=[row_spec(block, 2 * width), fixed_spec(width)],
        out_shape=[jax.ShapeDtypeStruct((rows, 2 * width), BF), jax.ShapeDtypeStruct((1, width), F32)],
        compiler_params=params(32),
        cost_estimate=pl.CostEstimate(flops=rows * width * 15, bytes_accessed=rows * width * 18, transcendentals=0),
        name="self_keyvalue_back",
    )(*gradients, raw, gain, *tables)


def query_back(gradient, raw, gain):
    rows, width = raw.shape
    block = row_block(rows)

    def kernel(grad_ref, raw_ref, gain_ref, low_ref, gain_out):
        back, term = norm_back(raw_ref[...], gain_ref[...], grad_ref[...])
        low_ref[...] = back.astype(BF)
        accumulate(gain_out, term)

    return pl.pallas_call(
        kernel,
        grid=(rows // block,),
        in_specs=[row_spec(block, width), row_spec(block, width), fixed_spec(width)],
        out_specs=[row_spec(block, width), fixed_spec(width)],
        out_shape=[jax.ShapeDtypeStruct((rows, width), BF), jax.ShapeDtypeStruct((1, width), F32)],
        compiler_params=params(24),
        cost_estimate=pl.CostEstimate(flops=rows * width * 15, bytes_accessed=rows * width * 10, transcendentals=0),
        name="query_back",
    )(gradient, raw, gain)


def text_back(gradient, raw, gain):
    rows, width = raw.shape[0], raw.shape[1] // 2
    block = row_block(rows)

    def kernel(grad_ref, raw_ref, gain_ref, low_ref, gain_out):
        pieces = []
        for head in range(HEADS):
            start = 2 * head * HEAD_DIM
            pieces.append(grad_ref[:, start : start + HEAD_DIM])
            value = grad_ref[:, start + HEAD_DIM : start + 2 * HEAD_DIM].astype(BF)
            low_ref[:, width + head * HEAD_DIM : width + (head + 1) * HEAD_DIM] = value
        back, term = norm_back(raw_ref[...], gain_ref[...], jnp.concatenate(pieces, axis=1))
        low_ref[:, :width] = back.astype(BF)
        accumulate(gain_out, term)

    return pl.pallas_call(
        kernel,
        grid=(rows // block,),
        in_specs=[row_spec(block, 2 * width), row_spec(block, width), fixed_spec(width)],
        out_specs=[row_spec(block, 2 * width), fixed_spec(width)],
        out_shape=[jax.ShapeDtypeStruct((rows, 2 * width), BF), jax.ShapeDtypeStruct((1, width), F32)],
        compiler_params=params(24),
        cost_estimate=pl.CostEstimate(flops=rows * width * 15, bytes_accessed=rows * width * 16, transcendentals=0),
        name="text_back",
    )(gradient, raw, gain)


def attend(query, chunks, base, heads):
    rows = query.shape[0]
    count = len(chunks)
    keys = chunks[0].shape[0]

    def kernel(query_ref, *refs):
        out_ref, log_ref = refs[count:]
        query_head = query_ref[...]
        scores = [dot_nt(ref[:, :HEAD_DIM], query_head) for ref in refs[:count]]
        peak = functools.reduce(
            jnp.maximum, [jnp.max(score, axis=0, keepdims=True) for score in scores]
        )
        shift = peak * SCALE_LOG2
        total = jnp.zeros((1, rows), F32)
        summed = jnp.zeros((HEAD_DIM, rows), F32)
        for ref, score in zip(refs[:count], scores):
            weight = jnp.exp2(score * SCALE_LOG2 - shift)
            total += jnp.sum(weight, axis=0, keepdims=True)
            summed += dot_tn(ref[:, HEAD_DIM:], weight.astype(BF))
        out_ref[...] = (summed / total).T.astype(BF)
        log_ref[0] = shift + jnp.log2(total)

    return pl.pallas_call(
        kernel,
        grid=(heads,),
        in_specs=[pl.BlockSpec((rows, HEAD_DIM), lambda head: (0, base + head))]
        + [pl.BlockSpec((keys, 2 * HEAD_DIM), lambda head: (0, head))] * count,
        out_specs=[
            pl.BlockSpec((rows, HEAD_DIM), lambda head: (0, head)),
            pl.BlockSpec((1, 1, rows), lambda head: (head, 0, 0)),
        ],
        out_shape=[
            jax.ShapeDtypeStruct((rows, heads * HEAD_DIM), BF),
            jax.ShapeDtypeStruct((heads, 1, rows), F32),
        ],
        compiler_params=params(40),
        cost_estimate=pl.CostEstimate(
            flops=heads * rows * keys * count * HEAD_DIM * 4 * 2,
            bytes_accessed=heads * HEAD_DIM * 2 * (2 * rows + 2 * keys * count),
            transcendentals=heads * rows * keys * count,
        ),
        name="attend",
    )(query, *chunks)


def attend_back(query, chunks, gradient, logs, base, heads):
    rows = query.shape[0]
    count = len(chunks)
    keys = chunks[0].shape[0]

    def kernel(query_ref, grad_ref, log_ref, *refs):
        query_grad = refs[count]
        query_head, grad_head = query_ref[...], grad_ref[...]
        shift = log_ref[0]
        weights, value_grads = [], []
        delta = jnp.zeros((1, rows), F32)
        for ref in refs[:count]:
            weight = jnp.exp2(dot_nt(ref[:, :HEAD_DIM], query_head) * SCALE_LOG2 - shift)
            value_grad = dot_nt(ref[:, HEAD_DIM:], grad_head)
            delta += jnp.sum(weight * value_grad, axis=0, keepdims=True)
            weights.append(weight)
            value_grads.append(value_grad)
        summed = jnp.zeros((HEAD_DIM, rows), F32)
        for ref, out, weight, value_grad in zip(refs[:count], refs[count + 1 :], weights, value_grads):
            score_grad = (weight * (value_grad - delta)).astype(BF)
            out[:, :HEAD_DIM] = (dot_nn(score_grad, query_head) * SCALE).astype(BF)
            out[:, HEAD_DIM:] = dot_nn(weight.astype(BF), grad_head).astype(BF)
            summed += dot_tn(ref[:, :HEAD_DIM], score_grad)
        query_grad[...] = (summed * SCALE).T

    return pl.pallas_call(
        kernel,
        grid=(heads,),
        in_specs=[
            pl.BlockSpec((rows, HEAD_DIM), lambda head: (0, base + head)),
            pl.BlockSpec((rows, HEAD_DIM), lambda head: (0, base + head)),
            pl.BlockSpec((1, 1, rows), lambda head: (head, 0, 0)),
        ]
        + [pl.BlockSpec((keys, 2 * HEAD_DIM), lambda head: (0, head))] * count,
        out_specs=[pl.BlockSpec((rows, HEAD_DIM), lambda head: (0, head))]
        + [pl.BlockSpec((keys, 2 * HEAD_DIM), lambda head: (0, head))] * count,
        out_shape=[jax.ShapeDtypeStruct((rows, heads * HEAD_DIM), F32)]
        + [jax.ShapeDtypeStruct((keys, heads * 2 * HEAD_DIM), BF)] * count,
        compiler_params=params(40),
        cost_estimate=pl.CostEstimate(
            flops=heads * rows * keys * count * HEAD_DIM * 10 * 2,
            bytes_accessed=heads * HEAD_DIM * 2 * (5 * rows + 4 * keys * count),
            transcendentals=heads * rows * keys * count,
        ),
        name="attend_back",
    )(query, gradient, logs, *chunks)


def place_rows(numbers, left, right, rows, total):
    slots, _, right_width = right[0][0].shape
    left_width = left[0][0].shape[2]
    count = len(left)

    def kernel(numbers_ref, *refs):
        whole_ref, small_ref = refs[4 * count :]
        step = pl.program_id(0)
        for at in range(count):
            for core in range(2):

                @pl.when((step // slots == at) & (numbers_ref[0] == core))
                def _():
                    for other in range(2):
                        place = pl.ds((other ^ core) * rows, rows)
                        left_ref, right_ref = refs[4 * at + other], refs[4 * at + 2 + other]
                        whole_ref[place, :right_width] = left_ref[0, :, :right_width]
                        whole_ref[place, right_width:] = right_ref[0]
                        small_ref[place] = left_ref[0, :, right_width:]

    def source(at, width):
        return pl.BlockSpec(
            (1, rows, width),
            lambda step, numbers_ref: (jnp.clip(step - at * slots, 0, slots - 1), 0, 0),
        )

    def index(step, numbers_ref):
        return (numbers_ref[step + 1], 0)

    in_specs, arrays = [], []
    for at in range(count):
        in_specs += [source(at, left_width)] * 2 + [source(at, right_width)] * 2
        arrays += [*left[at], *right[at]]
    return pl.pallas_call(
        kernel,
        grid_spec=pltpu.PrefetchScalarGridSpec(
            num_scalar_prefetch=1,
            grid=(count * slots,),
            in_specs=in_specs,
            out_specs=[
                pl.BlockSpec((2 * rows, 2 * right_width), index),
                pl.BlockSpec((2 * rows, left_width - right_width), index),
            ],
        ),
        out_shape=[
            jax.ShapeDtypeStruct((total, 2 * right_width), BF),
            jax.ShapeDtypeStruct((total, left_width - right_width), BF),
        ],
        compiler_params=params(32),
        cost_estimate=pl.CostEstimate(flops=0, bytes_accessed=8 * total * right_width, transcendentals=0),
        name="place_rows",
    )(numbers, *arrays)


def after(value, *others):
    return lax.optimization_barrier((value,) + others)[0]


def together(*values):
    return lax.optimization_barrier(values)


class Plan:
    def __init__(self, mesh):
        self.dp_n = mesh.shape["dp"]
        self.seq_n = mesh.shape["seq"]
        self.total = self.dp_n * self.seq_n
        self.half = self.seq_n // 2
        self.columns = self.seq_n // 2
        self.groups = 3 if self.half <= 4 else 1
        self.dp_bits = [1 << i for i in range(self.dp_n.bit_length() - 1)]
        self.group_bits = [1 << i for i in range(self.half.bit_length() - 1)]

    def start(self):
        self.dp = lax.axis_index("dp")
        self.seq = lax.axis_index("seq")
        self.me = self.dp * self.seq_n + self.seq
        self.core = self.seq % 2
        self.column = self.seq // 2
        self.top = self.seq // self.half

    def over_seq(self, value, offset):
        return lax.ppermute(value, "seq", [(i, i ^ offset) for i in range(self.seq_n)])

    def over_dp(self, value, offset):
        return lax.ppermute(value, "dp", [(i, i ^ offset) for i in range(self.dp_n)])


    def shift(self, value):
        own = lax.dynamic_index_in_dim(value, self.top, 0, keepdims=False)
        other = lax.dynamic_index_in_dim(value, 1 - self.top, 0, keepdims=False)
        return jnp.concatenate([own, self.over_seq(other, self.half)], axis=0)

    def unshift(self, value):
        rows = value.shape[0] // 2
        own, other = value[:rows], self.over_seq(value[rows:], self.half)
        return jnp.where(self.top == 0, jnp.stack([own, other]), jnp.stack([other, own]))


    def group_gather(self, value, *behind):
        held = {0: after(value, *behind) if behind else value}
        for bit in reversed(self.group_bits):
            held.update({at ^ bit: self.over_seq(one, bit) for at, one in list(held.items())})
        return held

    def group_scatter(self, held):
        held = dict(held)
        for bit in self.group_bits:
            for at in sorted(held):
                if at & bit:
                    sent = self.over_seq(held.pop(at).astype(BF), bit)
                    held[at ^ bit] = held[at ^ bit].astype(F32) + sent.astype(F32)
        return held[0]


    def gather_columns(self, shard):
        return jnp.stack([shard] + [self.over_seq(shard, 2 * k) for k in range(1, self.columns)])

    def gather_dp(self, sides, orders):
        sides, offsets = list(sides), [[0] for _ in sides]
        for number in range(len(orders[0])):
            received = together(*[self.over_dp(one, order[number]) for one, order in zip(sides, orders)])
            for i, order in enumerate(orders):
                flipped = [at ^ order[number] for at in offsets[i]]
                if number + 1 < len(order):
                    sides[i], offsets[i] = jnp.concatenate([sides[i], received[i]]), offsets[i] + flipped
                else:
                    sides[i], offsets[i] = [sides[i], received[i]], [offsets[i], flipped]
        return sides, offsets

    def gather_core(self, held):
        return [(one, self.over_seq(one, 1)) for one in held]

    def gather_place(self, left, left_offsets, right, right_offsets):
        slots = self.columns
        rows, width = right[0][0].shape[1:]

        def by_offset(held, offsets):
            return {
                at: tuple(one[i * slots : (i + 1) * slots] for one in pair)
                for pair, ats in zip(held, offsets)
                for i, at in enumerate(ats)
            }

        left, right = by_offset(left, left_offsets), by_offset(right, right_offsets)
        if rows % 16 == 0:
            blocks = [(self.dp ^ at) * slots + (self.column ^ slot) for at in left for slot in range(slots)]
            numbers = jnp.stack([self.core] + blocks).astype(jnp.int32)
            return place_rows(
                numbers, list(left.values()), [right[at] for at in left], rows, self.total * rows
            )
        wholes = []
        for held in (left, right):
            pieces = [
                held[number // self.seq_n][number % 2][(number % self.seq_n) // 2]
                for number in range(self.total)
            ]
            stacked = jnp.stack(pieces)

            def place(number, out):
                return lax.dynamic_update_index_in_dim(
                    out, self.pick(stacked, number, 0), number ^ self.me, 0
                )

            ordered = lax.fori_loop(0, self.total, place, jnp.zeros_like(stacked))
            wholes.append(ordered.reshape(self.total * rows, -1))
        left, right = wholes
        return jnp.concatenate([left[:, :width], right], axis=1), left[:, width:]

    def xor_order(self, pieces, number):
        bit = 1
        while bit < len(pieces):
            swapped = (number // bit) % 2 == 1
            pieces = [jnp.where(swapped, pieces[i ^ bit], pieces[i]) for i in range(len(pieces))]
            bit *= 2
        return pieces

    def pick(self, value, number, axis):
        return lax.dynamic_index_in_dim(value, number, axis, keepdims=False)

    def scatter_columns(self, value, axis, wire):
        total = self.pick(value, self.column, axis).astype(F32)
        for k in range(1, self.columns):
            sent = self.over_seq(self.pick(value, self.column ^ k, axis).astype(wire), 2 * k)
            total = total + sent.astype(F32)
        return total


    def scatter_core(self, value):
        bits = len(self.dp_bits)
        value = value.reshape((2,) * bits + (self.columns, 2, value.shape[0] // self.total, value.shape[1]))
        sent = self.over_seq(self.pick(value, 1 - self.core, bits + 1), 1)
        return self.pick(value, self.core, bits + 1), sent

    def scatter_dp(self, halves, done, bit):
        value = (halves[0].astype(F32) + halves[1].astype(F32)).astype(BF)
        axis = [one for one in reversed(self.dp_bits) if one not in done].index(bit)
        mine = (self.dp // bit) % 2
        sent = self.over_dp(self.pick(value, 1 - mine, axis), bit)
        return self.pick(value, mine, axis), sent

    def scatter_dps(self, halves, bits, done=()):
        for bit in bits:
            halves = self.scatter_dp(halves, done, bit)
            done = done + (bit,)
        return halves

    def scatter_last(self, halves):
        return self.scatter_columns(halves[0].astype(F32) + halves[1].astype(F32), 0, BF)


def body(
    plan,
    latents,
    context,
    modulation,
    cotangent,
    modtable,
    selfquery,
    selfkey,
    selfvalue,
    selfout,
    querygain,
    keygain,
    normgain,
    normbias,
    crossquery,
    crosskey,
    crossvalue,
    crossout,
    crossqgain,
    crosskgain,
    upmatrix,
    downmatrix,
):
    plan.start()
    width = latents.shape[2]
    dp_n, seq_n, columns = plan.dp_n, plan.seq_n, plan.columns
    everywhere = ("dp", "seq")
    rows_one = latents.shape[1]
    shard_rows = selfquery.shape[0]
    hidden = upmatrix.shape[1]
    part = hidden // dp_n
    xy, yx = plan.dp_bits, list(reversed(plan.dp_bits))

    small = jnp.concatenate(
        [modtable.T]
        + [gain[:, None] for gain in (querygain, keygain, normgain, normbias, crossqgain, crosskgain)]
        + [jnp.zeros((shard_rows, HEAD_DIM - 12), BF)],
        axis=1,
    )
    middle = 3 * width // 2
    side = jnp.concatenate([selfquery, selfkey, selfvalue], axis=1)
    both = plan.gather_columns(jnp.concatenate([side[:, :middle], small, side[:, middle:]], axis=1))
    token_rows = plan.shift(latents)
    both, token_rows = together(both, token_rows)
    (left_held, right_held), (left_offsets, right_offsets) = plan.gather_dp(
        (both[:, :, : middle + HEAD_DIM], both[:, :, middle + HEAD_DIM :]), (xy, yx)
    )
    left_held, right_held = plan.gather_core(left_held), plan.gather_core(right_held)
    whole_self, small_all = plan.gather_place(left_held, left_offsets, right_held, right_offsets)
    small_all = small_all.T[:12].astype(F32)

    others = jnp.concatenate([selfout, crossquery, crossout, crosskey, crossvalue], axis=1)
    whole_others = lax.all_gather(others, everywhere, axis=0, tiled=True)
    whole_selfout, whole_crossquery, whole_crossout = [
        whole_others[:, i * width : (i + 1) * width] for i in range(3)
    ]
    whole_crosstext = whole_others[:, 3 * width :]

    up_rows = after(upmatrix, both)
    up_parts = [
        lax.dynamic_slice_in_dim(up_rows, (plan.dp ^ j) * part, part, 1) for j in range(dp_n)
    ]
    up_parts = [plan.over_dp(one, j) if j else one for j, one in enumerate(up_parts)]
    up_shard = jnp.concatenate(plan.xor_order(up_parts, plan.dp), axis=0)
    shifted = plan.shift(after(jnp.concatenate([cotangent, context], axis=1), both))
    down_shard, whole_self, shifted, _ = together(downmatrix, whole_self, shifted, whole_others)
    whole_down = lax.all_gather(down_shard, "seq", axis=0, tiled=True)
    text_one = context.shape[1]
    step = rows_one + text_one
    grad_rows = jnp.concatenate([shifted[:rows_one], shifted[step : step + rows_one]])
    text_rows = jnp.concatenate([shifted[rows_one:step], shifted[step + rows_one :]])

    mod_rows = lax.dynamic_index_in_dim(modulation, plan.top, 0, keepdims=False) + small_all[:6]
    shift_a, scale_a, gate_a, shift_m, scale_m, gate_m = [mod_rows[i : i + 1] for i in range(6)]
    gain_query, gain_key, gain_norm, bias_norm, gain_crossq, gain_crossk = [
        small_all[i : i + 1] for i in range(6, 12)
    ]
    span = jnp.arange(rows_one, dtype=jnp.int32)
    positions = jnp.concatenate(
        [plan.seq * rows_one + span, (plan.seq ^ plan.half) * rows_one + span]
    )
    tables = rotary_tables(positions)

    latent_rows = token_rows.astype(F32)
    normed_a = layer_norm(latent_rows)
    attn_in = (normed_a * (1.0 + scale_a) + shift_a).astype(BF)
    self_raw = dot_nn(attn_in, whole_self)
    queries, *keyvalues = self_post(self_raw, gain_query, gain_key, tables, plan.groups)
    per_group = HEADS // plan.groups
    gathered = []
    for one in keyvalues:
        behind = [gathered[-1][plan.group_bits[-1]]] if gathered else []
        gathered.append(plan.group_gather(one, *behind))
    up_shard = after(up_shard, gathered[0][plan.group_bits[-1]])
    whole_up = lax.all_gather(up_shard, "seq", axis=0, tiled=True)
    whole_up = (
        whole_up.reshape(seq_n, dp_n, shard_rows, part)
        .transpose(1, 0, 2, 3)
        .reshape(plan.total * shard_rows, part)
    )
    out_grad = grad_rows.astype(F32)
    down_grad = (out_grad * gate_m).astype(BF)
    down_grads = [down_grad] + [plan.over_dp(down_grad, j) for j in range(1, dp_n)]
    self_outs, self_logs = [], []
    for group in range(plan.groups):
        out, logs = attend(queries, list(gathered[group].values()), group * per_group, per_group)
        self_outs.append(out)
        self_logs.append(logs)
    *self_outs, down_grads = together(*self_outs, down_grads)
    attended = jnp.concatenate(self_outs, axis=1)
    self_branch = dot_nn(attended, whole_selfout)
    hidden_one = latent_rows + self_branch * gate_a

    text_raw = dot_nn(text_rows, whole_crosstext)
    cross_gathered = plan.group_gather(text_post(text_raw, gain_crossk))
    cross_in = (layer_norm(hidden_one) * gain_norm + bias_norm).astype(BF)
    crossq_raw = dot_nn(cross_in, whole_crossquery)
    cross_queries = query_post(crossq_raw, gain_crossq)
    crossed, cross_logs = attend(cross_queries, list(cross_gathered.values()), 0, HEADS)
    hidden_two = hidden_one + dot_nn(crossed, whole_crossout)

    act_grads = [dot_nt(one, whole_down) for one in down_grads]
    normed_m = layer_norm(hidden_two)
    mlp_in = (normed_m * (1.0 + scale_m) + shift_m).astype(BF)
    mlp_ins = [mlp_in] + [plan.over_dp(mlp_in, j) for j in range(1, dp_n)]
    activations, up_grads, mlp_grads = [], [], []
    for j in range(dp_n):
        up_values = dot_nn(mlp_ins[j], whole_up)
        activation, gelu_back = jax.vjp(gelu_tanh, up_values)
        activations.append(activation.astype(BF))
        up_grads.append(gelu_back(act_grads[j])[0].astype(BF))
        mlp_grads.append(dot_nt(up_grads[j], whole_up, BF if j else F32))
    mlp_sent = [plan.over_dp(mlp_grads[j], j) for j in range(1, dp_n)]

    up_in, down_in, _ = together(jnp.concatenate(mlp_ins), jnp.concatenate(activations), mlp_grads[0])
    up_term = dot_tn(up_in, jnp.concatenate(up_grads), BF)
    down_term = dot_tn(down_in, jnp.concatenate(down_grads), BF)
    *mlp_sent, up_term, down_term = together(*mlp_sent, up_term, down_term)
    mlp_grad = mlp_grads[0] + sum(one.astype(F32) for one in mlp_sent)
    downmatrix_gradient = lax.psum_scatter(down_term, "seq", scatter_dimension=0, tiled=True).astype(F32)
    up_term = (
        up_term.reshape(dp_n, seq_n, shard_rows, part)
        .transpose(1, 0, 2, 3)
        .reshape(plan.total * shard_rows, part)
    )
    up_term = lax.psum_scatter(up_term, "seq", scatter_dimension=0, tiled=True)
    up_term = up_term.reshape(dp_n, shard_rows, part)

    shift_m_grad = jnp.sum(mlp_grad, axis=0)
    scale_m_grad = jnp.sum(mlp_grad * normed_m, axis=0)
    two_grad = out_grad + layer_norm_back(hidden_two, mlp_grad * (1.0 + scale_m))
    cross_grad = two_grad.astype(BF)
    crossed_grad = dot_nt(cross_grad, whole_crossout, BF)
    crossout_sum = plan.scatter_core(dot_tn(crossed, cross_grad, BF))
    crossq_grad, *cross_parts = attend_back(
        cross_queries, list(cross_gathered.values()), crossed_grad, cross_logs, 0, HEADS
    )
    crossq_grad, crossout_sum = together(crossq_grad, crossout_sum)
    crossout_sum = plan.scatter_dp(crossout_sum, (), xy[0])
    cross_own = plan.group_scatter(dict(zip(cross_gathered, cross_parts)))
    crossq_low, crossq_gaingrad = query_back(crossq_grad, crossq_raw, gain_crossq)
    crossq_sum = plan.scatter_core(dot_tn(cross_in, crossq_low, BF))
    crossin_grad = dot_nt(crossq_low, whole_crossquery)
    normgain_grad = jnp.sum(crossin_grad * layer_norm(hidden_one), axis=0)
    normbias_grad = jnp.sum(crossin_grad, axis=0)
    one_grad = two_grad + layer_norm_back(hidden_one, crossin_grad * gain_norm)
    gate_a_grad = jnp.sum(one_grad * self_branch, axis=0)
    branch_grad = (one_grad * gate_a).astype(BF)
    branch_grad, crossq_sum, crossout_sum, cross_own = together(branch_grad, crossq_sum, crossout_sum, cross_own)
    crossq_sum = plan.scatter_dp(crossq_sum, (), yx[0])
    crossout_sum = plan.scatter_dps(crossout_sum, xy[1:], (xy[0],))
    text_low, crossk_gaingrad = text_back(cross_own, text_raw, gain_crossk)
    text_gradients = lax.psum_scatter(
        dot_tn(text_rows, text_low, BF), everywhere, scatter_dimension=0, tiled=True
    ).astype(F32)
    context_gradient = plan.unshift(dot_nt(text_low, whole_crosstext, BF))

    attended_grad = dot_nt(branch_grad, whole_selfout, BF)
    selfout_sum = plan.scatter_core(dot_tn(attended, branch_grad, BF))
    query_grads, keyvalue_grads = [], []
    for group in range(plan.groups):
        query_grad, *parts = attend_back(
            queries,
            list(gathered[group].values()),
            attended_grad,
            self_logs[group],
            group * per_group,
            per_group,
        )
        if group == 0:
            query_grad, crossout_sum, crossq_sum, context_gradient, selfout_sum = together(
                query_grad, crossout_sum, crossq_sum, context_gradient, selfout_sum
            )
            crossout_gradient = plan.scatter_last(crossout_sum)
            crossq_sum = plan.scatter_dps(crossq_sum, yx[1:], (yx[0],))
            selfout_sum = plan.scatter_dp(selfout_sum, (), xy[0])
        query_grads.append(query_grad)
        keyvalue_grads.append(plan.group_scatter(dict(zip(gathered[group], parts))))
    query_low, query_gaingrad = self_query_back(query_grads, self_raw, gain_query, tables)
    query_low, crossout_gradient, crossq_sum, selfout_sum = together(
        query_low, crossout_gradient, crossq_sum, selfout_sum
    )
    crossquery_gradient = plan.scatter_last(crossq_sum)
    selfout_sum = plan.scatter_dps(selfout_sum, xy[1:], (xy[0],))
    query_sum = plan.scatter_core(dot_tn(attn_in, query_low, BF))
    attn_grad = dot_nt(query_low, whole_self[:, :width])

    *activations, query_sum = together(*activations, query_sum)
    query_sum = plan.scatter_dp(query_sum, (), yx[0])
    down_all = [dot_nn(activations[j], whole_down, BF if j else F32) for j in range(dp_n)]
    down_sent = [plan.over_dp(down_all[j], j) for j in range(1, dp_n)]

    keyvalue_low, key_gaingrad = self_keyvalue_back(keyvalue_grads, self_raw, gain_key, tables)
    key_sum = plan.scatter_core(dot_tn(attn_in, keyvalue_low[:, :width], BF))
    value_sum = plan.scatter_core(dot_tn(attn_in, keyvalue_low[:, width:], BF))
    kept_low, _, _ = together(keyvalue_low, key_sum[0], value_sum[0])
    attn_grad = attn_grad + dot_nt(kept_low, whole_self[:, width:])
    key_sum, value_sum, selfout_sum, query_sum = together(key_sum, value_sum, selfout_sum, query_sum)
    key_sum = plan.scatter_dp(key_sum, (), xy[0])
    value_sum = plan.scatter_dp(value_sum, (), yx[0])
    down_values = down_all[0] + sum(one.astype(F32) for one in down_sent)
    layer_low = (hidden_two + down_values * gate_m).astype(BF)
    gate_m_grad = jnp.sum(out_grad * down_values, axis=0)
    selfout_gradient = plan.scatter_last(selfout_sum)
    query_sum = plan.scatter_dps(query_sum, yx[1:], (yx[0],))
    shift_a_grad = jnp.sum(attn_grad, axis=0)
    scale_a_grad = jnp.sum(attn_grad * normed_a, axis=0)
    latents_low = (one_grad + layer_norm_back(latent_rows, attn_grad * (1.0 + scale_a))).astype(BF)

    local_mod = jnp.stack(
        [shift_a_grad, scale_a_grad, gate_a_grad, shift_m_grad, scale_m_grad, gate_m_grad]
    )
    sums = jnp.concatenate(
        [
            local_mod,
            query_gaingrad,
            key_gaingrad,
            normgain_grad[None],
            normbias_grad[None],
            crossq_gaingrad,
            crossk_gaingrad,
        ]
    )
    for bit in plan.group_bits:
        sums = sums + plan.over_seq(sums, bit)
    other_sums = plan.over_seq(sums, plan.half)
    both_low = jnp.stack([layer_low, latents_low])
    both_low, key_sum, value_sum, query_sum = together(both_low, key_sum, value_sum, query_sum)
    half_rows = both_low.shape[1] // 2
    both_sent = plan.over_seq(both_low[:, half_rows:], plan.half)
    layer_output, latents_gradient = [
        jnp.where(plan.top == 0, jnp.stack([own, other]), jnp.stack([other, own]))
        for own, other in zip(both_low[:, :half_rows], both_sent)
    ]
    latents_gradient = latents_gradient.astype(F32)
    key_sum = plan.scatter_dps(key_sum, xy[1:], (xy[0],))
    value_sum = plan.scatter_dps(value_sum, yx[1:], (yx[0],))
    selfquery_gradient = plan.scatter_last(query_sum)
    up_pieces = [plan.pick(up_term, plan.dp ^ j, 0) for j in range(dp_n)]
    up_pieces = [plan.over_dp(one, j) if j else one for j, one in enumerate(up_pieces)]
    upmatrix_gradient = jnp.concatenate(plan.xor_order(up_pieces, plan.dp), axis=1).astype(F32)
    key_sum, value_sum = together(key_sum, value_sum)
    selfkey_gradient, selfvalue_gradient = plan.scatter_last(key_sum), plan.scatter_last(value_sum)
    modulation_gradient = jnp.where(
        plan.top == 0, jnp.stack([sums[:6], other_sums[:6]]), jnp.stack([other_sums[:6], sums[:6]])
    )
    sums = sums + other_sums
    for bit in plan.dp_bits:
        sums = sums + plan.over_dp(sums, bit)
    small_grads = lax.dynamic_index_in_dim(
        sums.reshape(12, plan.total, shard_rows), plan.me, 1, keepdims=False
    )
    return (
        layer_output,
        latents_gradient,
        context_gradient.astype(F32),
        modulation_gradient,
        small_grads[:6],
        selfquery_gradient,
        selfkey_gradient,
        selfvalue_gradient,
        selfout_gradient,
        small_grads[6],
        small_grads[7],
        small_grads[8],
        small_grads[9],
        crossquery_gradient,
        text_gradients[:, :width],
        text_gradients[:, width:],
        crossout_gradient,
        small_grads[10],
        small_grads[11],
        upmatrix_gradient,
        downmatrix_gradient,
    )


def solution(mesh):
    tokens = P("dp", "seq", None)
    clip = P("dp", None, None)
    table = P(None, ("dp", "seq"))
    matrix = P(("dp", "seq"), None)
    gain = P(("dp", "seq"))
    weights = (matrix,) * 4 + (gain,) * 4 + (matrix,) * 4 + (gain,) * 2 + (matrix,) * 2
    return jax.shard_map(
        functools.partial(body, Plan(mesh)),
        mesh=mesh,
        in_specs=(tokens, tokens, clip, tokens, table) + weights,
        out_specs=(tokens, tokens, tokens, clip, table) + weights,
        check_vma=False,
    )
```

time: 4530 us -> 1470 us (0.32)
  waiting for transfers between devices: 3070 us -> 725 us
  matrix products: 901 us -> 253 us
  blocking collectives: 148 us -> 0 us
  starting transfers between devices: 2.24 us -> 136 us
  Pallas kernels: 0 us -> 132 us
  local copies, waits for them, and re-layouts: 221 us -> 113 us
  other arithmetic: 141 us -> 85.1 us
    reduce_scatter x15 -> x3, waiting for transfers between devices: 1470 us -> 0.01 us  [the longest x1 0.01 us: body(): up_term = lax.psum_scatter(up_term, 'seq', scatter_dimension=0, tiled=True)]
    all_gather x18 -> x3, waiting for transfers between devices: 846 us -> 0.01 us  [the longest x1 0.01 us: body(): whole_others = lax.all_gather(others, everywhere, axis=0, tiled=True)]
    unnamed x41 -> x6, waiting for transfers between devices: 762 us -> 0.1 us
    ppermute x0 -> x98, waiting for transfers between devices: none -> 725 us  [the longest x62 482 us: over_seq(): lax.ppermute(value, 'seq', [(i, i ^ offset) for i in range(self.seq_n)])]
    dot_general x386 -> x36, matrix products: 901 us -> 253 us  [the longest x14 96.1 us: dot_nt(): lax.dot_general(left, right, (((1,), (1,)), ((), ())), preferred_element_...]
    ppermute x0 -> x98, starting transfers between devices: none -> 135 us  [the longest x62 88.9 us: over_seq(): lax.ppermute(value, 'seq', [(i, i ^ offset) for i in range(self.seq_n)])]
    pallas_call x0 -> x16, Pallas kernels: none -> 132 us  [the longest x4 67.4 us: attend_back(): pl.pallas_call(kernel, grid=(heads,), in_specs=[pl.BlockSpec((rows, HEAD_...]
    unnamed x2 -> x0, blocking collectives: 77.4 us -> none
  transfers between devices with their start and end apart: 37 -> 104, of which waited for: 32 -> 37; matrix products, arithmetic and copies ran while one was open for 13% -> 24% of each run, Pallas kernels for 0% -> 9%
where the time goes in v1:
time: 1470 us; the launch traced here: 1460 us
  waiting for transfers between devices  725 us (49%)
  matrix products  253 us (17%)
  starting transfers between devices  136 us (9%)
  Pallas kernels  132 us (9%)
  local copies, waits for them, and re-layouts  113 us (8%)
  other arithmetic  85.1 us (6%)
  between operations  17.2 us (1%)
    ppermute x62, waiting for transfers between devices, over_seq(): lax.ppermute(value, 'seq', [(i, i ^ offset) for i in range(self.seq_n)])  482 us
    ppermute x36, waiting for transfers between devices, over_dp(): lax.ppermute(value, 'dp', [(i, i ^ offset) for i in range(self.dp_n)])  243 us
    dot_general x14, matrix products, dot_nt(): lax.dot_general(left, right, (((1,), (1,)), ((), ())), preferred_element_...  96.1 us
    dot_general x13, matrix products, dot_nn(): lax.dot_general(left, right, (((1,), (0,)), ((), ())), preferred_element_...  94 us
    ppermute x62, starting transfers between devices, over_seq(): lax.ppermute(value, 'seq', [(i, i ^ offset) for i in range(self.seq_n)])  88.9 us
    pallas_call x4, Pallas kernels, attend_back(): pl.pallas_call(kernel, grid=(heads,), in_specs=[pl.BlockSpec((rows, HEAD_...  67.4 us
    dot_general x9, matrix products, dot_tn(): lax.dot_general(left, right, (((0,), (0,)), ((), ())), preferred_element_...  63.1 us
    ppermute x36, starting transfers between devices, over_dp(): lax.ppermute(value, 'dp', [(i, i ^ offset) for i in range(self.dp_n)])  46.4 us
  transfers between devices with their start and end apart: 104, of which 37 were waited for; matrix products, arithmetic and copies ran while one was open for 24% of the time, Pallas kernels for 9%

profile of v1, /device:TPU:0, one launch (start us, length us, event | category | flops | bytes accessed | tf_op | source)
XLA Modules:
  0.0 1462.5 jit_solution(10299097366294461683)
XLA Ops:
  27.7 14.8 %collective-permute-done.2 = bf16[48,4736]{1,0:T(8,128)(2,1)S(1)} collective-permute-done((bf16[48,4736]{1,0:T(8,128)(2,1)S(1)}, bf16[48,4736]{1,0:T(8,128)(2,1)S(1)}, u32[]{:S(2)}, u32[]{:S(2)}) %collective-permute-start.2) | collective-permute-done | bytes 454688 | tf_op jit(solution)/shard_map/ppermute | solution.py:515
  42.5 76.3 %collective-permute-done.1 = bf16[48,4736]{1,0:T(8,128)(2,1)S(1)} collective-permute-done((bf16[48,4736]{1,0:T(8,128)(2,1)S(1)}, bf16[48,4736]{1,0:T(8,128)(2,1)S(1)}, u32[]{:S(2)}, u32[]{:S(2)}) %collective-permute-start.1) | collective-permute-done | bytes 454688 | tf_op jit(solution)/shard_map/ppermute | solution.py:515
  119.1 25.7 %collective-permute-done.3 = bf16[256,1536]{1,0:T(8,128)(2,1)S(1)} collective-permute-done((bf16[256,1536]{1,0:T(8,128)(2,1)S(1)}, bf16[256,1536]{1,0:T(8,128)(2,1)S(1)}, u32[]{:S(2)}, u32[]{:S(2)}) %collective-permute-start.3) | collective-permute-done | bytes 786464 | tf_op jit(solution)/shard_map/ppermute | solution.py:515
  149.5 39.1 %collective-permute-done.5.refs_10_ = bf16[4,48,2304]{2,1,0:T(8,128)(2,1)S(1)} collective-permute-done((bf16[4,48,2304]{2,1,0:T(8,128)(2,1)S(1)}, bf16[4,48,2304]{2,1,0:T(8,128)(2,1)S(1)}, u32[]{:S(2)}, u32[]{:S(2)}) %collective-permute-start.5) | collective-permute-done | bytes 884768 | tf_op jit(solution)/shard_map/ppermute | solution.py:518
  196.5 68.1 %collective-permute-done.12 = bf16[320,1536]{1,0:T(8,128)(2,1)} collective-permute-done((bf16[320,1536]{1,0:T(8,128)(2,1)}, bf16[320,1536]{1,0:T(8,128)(2,1)}, u32[]{:S(2)}, u32[]{:S(2)}) %collective-permute-start.12) | collective-permute-done | bytes 983072 | tf_op jit(solution)/shard_map/ppermute | solution.py:515
  294.5 10.4 fusion.154.query_ref.key_ref.value_ref.refs_3_
  321.7 51.2 %collective-permute-done.13.refs_1_ = bf16[512,1024]{1,0:T(8,128)(2,1)} collective-permute-done((bf16[512,1024]{1,0:T(8,128)(2,1)}, bf16[512,1024]{1,0:T(8,128)(2,1)}, u32[]{:S(2)}, u32[]{:S(2)}) %collective-permute-start.13) | collective-permute-done | bytes 1048608 | tf_op jit(solution)/shard_map/ppermute | solution.py:515
  376.1 36.1 %collective-permute-done.16.refs_1_ = bf16[512,1024]{1,0:T(8,128)(2,1)} collective-permute-done((bf16[512,1024]{1,0:T(8,128)(2,1)}, bf16[512,1024]{1,0:T(8,128)(2,1)}, u32[]{:S(2)}, u32[]{:S(2)}) %collective-permute-start.16) | collective-permute-done | bytes 1048608 | tf_op jit(solution)/shard_map/ppermute | solution.py:515
  420.9 48.3 %collective-permute-done.19.refs_1_ = bf16[512,1024]{1,0:T(8,128)(2,1)} collective-permute-done((bf16[512,1024]{1,0:T(8,128)(2,1)S(1)}, bf16[512,1024]{1,0:T(8,128)(2,1)}, u32[]{:S(2)}, u32[]{:S(2)}) %collective-permute-start.19) | collective-permute-done | bytes 1048608 | tf_op jit(solution)/shard_map/ppermute | solution.py:515
  515.1 11.6 attend.7
  537.3 33.7 %collective-permute-done.31 = bf16[512,1536]{1,0:T(8,128)(2,1)S(1)} collective-permute-done((bf16[512,1536]{1,0:T(8,128)(2,1)S(1)}, bf16[512,1536]{1,0:T(8,128)(2,1)S(1)}, u32[]{:S(2)}, u32[]{:S(2)}) %collective-permute-start.31) | collective-permute-done | bytes 1572896 | tf_op jit(solution)/shard_map/ppermute | solution.py:518
  571.0 34.2 %collective-permute-done.32 = bf16[512,1536]{1,0:T(8,128)(2,1)S(1)} collective-permute-done((bf16[512,1536]{1,0:T(8,128)(2,1)S(1)}, bf16[512,1536]{1,0:T(8,128)(2,1)S(1)}, u32[]{:S(2)}, u32[]{:S(2)}) %collective-permute-start.32) | collective-permute-done | bytes 1572896 | tf_op jit(solution)/shard_map/ppermute | solution.py:518
  657.4 10.9 multiply_convert_fusion.2
  676.2 11.3 multiply_convert_fusion.1
  717.3 16.3 %convolution_convert_fusion.2 = bf16[2240,1536]{1,0:T(8,128)(2,1)} fusion(bf16[2048,2240]{0,1:T(8,128)(2,1)S(1)} %pad_maximum_fusion, bf16[512,1536]{1,0:T(8,128)(2,1)S(1)} %copy-done.169, bf16[512,1536]{1,0:T(8,128)(2,1)S(1)} %copy-done.166, bf16[512,1536]{1,0:T(8,128)(2,1)S(1)} %copy-done.163, bf16[512,1536]{1,0:T(8,128)(2,1)S(1)} %copy-done.110), kind=kOutput, calls=%fused_computation.2 | convolution fusion | flops 14121467904 | bytes 22347776 | tf_op jit(solution)/shard_map/dot_general | solution.py:52
  733.6 20.5 %convolution_convert_fusion = bf16[1536,2240]{0,1:T(8,128)(2,1)} fusion(bf16[2048,1536]{1,0:T(8,128)(2,1)} %pad_maximum_fusion.1, bf16[512,2240]{0,1:T(8,128)(2,1)} %get-tuple-element.345, bf16[512,2240]{0,1:T(8,128)(2,1)} %get-tuple-element.343, bf16[512,2240]{0,1:T(8,128)(2,1)} %get-tuple-element.341, bf16[512,2240]{0,1:T(8,128)(2,1)S(1)} %copy-done.172), kind=kOutput, calls=%fused_computation | convolution fusion | flops 14133002240 | bytes 22347776 | tf_op jit(solution)/shard_map/dot_general | solution.py:52
  763.8 10.3 copy.67
  795.3 17.6 %attend_back.4 = (f32[512,1536]{1,0:T(8,128)S(1)}, bf16[128,3072]{1,0:T(8,128)(2,1)S(1)}, bf16[128,3072]{1,0:T(8,128)(2,1)S(1)}, bf16[128,3072]{1,0:T(8,128)(2,1)}, bf16[128,3072]{1,0:T(8,128)(2,1)S(1)}) custom-call(bf16[512,1536]{1,0:T(8,128)(2,1)S(1)} %copy-done.19, bf16[512,1536]{1,0:T(8,128)(2,1)S(1)} %fusion.88.grad_ref, ...), custom_call_target="tpu_custom_call" | custom-call | flops 8053063680 | bytes 14155776 | tf_op jit(solution)/shard_map/attend_back/pallas_call | solution.py:410
  824.9 33.4 %collective-permute-done.42 = bf16[128,3072]{1,0:T(8,128)(2,1)} collective-permute-done((bf16[128,3072]{1,0:T(8,128)(2,1)}, bf16[128,3072]{1,0:T(8,128)(2,1)}, u32[]{:S(2)}, u32[]{:S(2)}) %collective-permute-start.42) | collective-permute-done | bytes 786464 | tf_op jit(solution)/shard_map/ppermute | solution.py:515
  884.7 16.7 %collective-permute-done.39 = bf16[2,4,48,1536]{3,2,1,0:T(8,128)(2,1)S(1)} collective-permute-done((bf16[2,4,48,1536]{3,2,1,0:T(8,128)(2,1)S(1)}, bf16[2,4,48,1536]{3,2,1,0:T(8,128)(2,1)S(1)}, u32[]{:S(2)}, u32[]{:S(2)}) %collective-permute-start.39) | collective-permute-done | bytes 1179680 | tf_op jit(solution)/shard_map/ppermute | solution.py:518
  907.8 16.7 %attend_back.5 = (f32[512,512]{1,0:T(8,128)S(1)}, bf16[512,1024]{1,0:T(8,128)(2,1)S(1)}, bf16[512,1024]{1,0:T(8,128)(2,1)S(1)}, bf16[512,1024]{1,0:T(8,128)(2,1)}, bf16[512,1024]{1,0:T(8,128)(2,1)}) custom-call(bf16[512,1536]{1,0:T(8,128)(2,1)S(1)} %copy-done.42, bf16[512,1536]{1,0:T(8,128)(2,1)S(1)} %fusion.85.grad_ref, ...), custom_call_target="tpu_custom_call" | custom-call | flops 10737418240 | bytes 11010048 | tf_op jit(solution)/shard_map/attend_back/pallas_call | solution.py:410
  926.0 16.7 %attend_back.6 = (f32[512,512]{1,0:T(8,128)S(1)}, bf16[512,1024]{1,0:T(8,128)(2,1)S(1)}, bf16[512,1024]{1,0:T(8,128)(2,1)S(1)}, bf16[512,1024]{1,0:T(8,128)(2,1)}, bf16[512,1024]{1,0:T(8,128)(2,1)}) custom-call(bf16[512,1536]{1,0:T(8,128)(2,1)S(1)} %copy-done.42, bf16[512,1536]{1,0:T(8,128)(2,1)S(1)} %fusion.85.grad_ref, ...), custom_call_target="tpu_custom_call" | custom-call | flops 10737418240 | bytes 11010048 | tf_op jit(solution)/shard_map/attend_back/pallas_call | solution.py:410
  945.6 16.3 %attend_back.7 = (f32[512,512]{1,0:T(8,128)S(1)}, bf16[512,1024]{1,0:T(8,128)(2,1)S(1)}, bf16[512,1024]{1,0:T(8,128)(2,1)S(1)}, bf16[512,1024]{1,0:T(8,128)(2,1)}, bf16[512,1024]{1,0:T(8,128)(2,1)}) custom-call(bf16[512,1536]{1,0:T(8,128)(2,1)S(1)} %copy-done.42, bf16[512,1536]{1,0:T(8,128)(2,1)S(1)} %copy-done.56, ...), custom_call_target="tpu_custom_call" | custom-call | flops 10737418240 | bytes 11010048 | tf_op jit(solution)/shard_map/attend_back/pallas_call | solution.py:410
  1006.3 15.8 %collective-permute-done.58 = bf16[512,1024]{1,0:T(8,128)(2,1)} collective-permute-done((bf16[512,1024]{1,0:T(8,128)(2,1)}, bf16[512,1024]{1,0:T(8,128)(2,1)}, u32[]{:S(2)}, u32[]{:S(2)}) %collective-permute-start.58) | collective-permute-done | bytes 1048608 | tf_op jit(solution)/shard_map/ppermute | solution.py:515
  1026.4 18.1 %collective-permute-done.61 = bf16[512,1024]{1,0:T(8,128)(2,1)} collective-permute-done((bf16[512,1024]{1,0:T(8,128)(2,1)}, bf16[512,1024]{1,0:T(8,128)(2,1)}, u32[]{:S(2)}, u32[]{:S(2)}) %collective-permute-start.61) | collective-permute-done | bytes 1048608 | tf_op jit(solution)/shard_map/ppermute | solution.py:515
  1046.7 38.9 %collective-permute-done.64 = bf16[512,1024]{1,0:T(8,128)(2,1)} collective-permute-done((bf16[512,1024]{1,0:T(8,128)(2,1)}, bf16[512,1024]{1,0:T(8,128)(2,1)}, u32[]{:S(2)}, u32[]{:S(2)}) %collective-permute-start.64) | collective-permute-done | bytes 1048608 | tf_op jit(solution)/shard_map/ppermute | solution.py:515
  1139.4 19.8 %collective-permute-done.51 = bf16[2,4,48,1536]{3,2,1,0:T(8,128)(2,1)} collective-permute-done((bf16[2,4,48,1536]{3,2,1,0:T(8,128)(2,1)}, bf16[2,4,48,1536]{3,2,1,0:T(8,128)(2,1)}, u32[]{:S(2)}, u32[]{:S(2)}) %collective-permute-start.51) | collective-permute-done | bytes 1179680 | tf_op jit(solution)/shard_map/ppermute | solution.py:518
  1208.5 29.5 %collective-permute-done.67 = bf16[4,48,1536]{2,1,0:T(8,128)(2,1)S(1)} collective-permute-done((bf16[4,48,1536]{2,1,0:T(8,128)(2,1)S(1)}, bf16[4,48,1536]{2,1,0:T(8,128)(2,1)S(1)}, u32[]{:S(2)}, u32[]{:S(2)}) %collective-permute-start.67) | collective-permute-done | bytes 589856 | tf_op jit(solution)/shard_map/ppermute | solution.py:518
  1240.1 23.2 %collective-permute-done.68 = bf16[2,4,48,1536]{3,2,1,0:T(8,128)(2,1)S(1)} collective-permute-done((bf16[2,4,48,1536]{3,2,1,0:T(8,128)(2,1)S(1)}, bf16[2,4,48,1536]{3,2,1,0:T(8,128)(2,1)S(1)}, u32[]{:S(2)}, u32[]{:S(2)}) %collective-permute-start.68) | collective-permute-done | bytes 1179680 | tf_op jit(solution)/shard_map/ppermute | solution.py:518
  1274.3 22.8 %collective-permute-done.54 = bf16[512,1536]{1,0:T(8,128)(2,1)S(1)} collective-permute-done((bf16[512,1536]{1,0:T(8,128)(2,1)}, bf16[512,1536]{1,0:T(8,128)(2,1)S(1)}, u32[]{:S(2)}, u32[]{:S(2)}) %collective-permute-start.54) | collective-permute-done | bytes 1572896 | tf_op jit(solution)/shard_map/ppermute | solution.py:518
  1360.9 26.3 %collective-permute-done.85 = bf16[48,1536]{1,0:T(8,128)(2,1)S(1)} collective-permute-done((bf16[48,1536]{1,0:T(8,128)(2,1)S(1)}, bf16[48,1536]{1,0:T(8,128)(2,1)S(1)}, u32[]{:S(2)}, u32[]{:S(2)}) %collective-permute-start.85) | collective-permute-done | bytes 147488 | tf_op jit(solution)/shard_map/ppermute | solution.py:515
  1387.2 39.3 %collective-permute-start.87 = (bf16[48,1536]{1,0:T(8,128)(2,1)}, bf16[48,1536]{1,0:T(8,128)(2,1)}, u32[]{:S(2)}, u32[]{:S(2)}) collective-permute-start(bf16[48,1536]{1,0:T(8,128)(2,1)} %get-tuple-element.400), channel_id=1, source_target_pairs={{0,4},{1,5},{2,6},{3,7},{4,0},{5,1},{6,2},{7,3},{8,12},{9,13},{10,... | collective-permute-start | bytes 442376 | tf_op jit(solution)/shard_map/ppermute | solution.py:515
  (772 shorter events, 575.3 us)
Async XLA Ops:
  7.2 278.0 %all-gather.4.cloned.1.call-start = ((), (), s32[]{:S(2)}) async-start(), calls=%async_computation.3 | async-start | bytes 24330240 | tf_op jit(solution)/shard_map/all_gather | solution.py:697
  12.9 597.8 %all-gather.8.cloned.1.call-start = ((), (), s32[]{:S(2)}) async-start(), calls=%async_computation.5 | async-start | bytes 7741440 | tf_op jit(solution)/shard_map/all_gather | solution.py:711
  24.6 94.2 %collective-permute-start.1 = (bf16[48,4736]{1,0:T(8,128)(2,1)S(1)}, bf16[48,4736]{1,0:T(8,128)(2,1)S(1)}, u32[]{:S(2)}, u32[]{:S(2)}) collective-permute-start(bf16[48,4736]{1,0:T(8,128)(2,1)S(1)} %concatenate.95), channel_id=1, source_target_pairs={{0,4},{1,5},{2,6},{3,7},{4,0},{5,1},{6,2},{7,3},{8,12},{9,13},{10,... | collective-permute-start | bytes 1363976 | tf_op jit(solution)/shard_map/ppermute | solution.py:515
  24.6 94.2 %collective-permute-start = (bf16[48,4736]{1,0:T(8,128)(2,1)S(1)}, bf16[48,4736]{1,0:T(8,128)(2,1)S(1)}, u32[]{:S(2)}, u32[]{:S(2)}) collective-permute-start(bf16[48,4736]{1,0:T(8,128)(2,1)S(1)} %concatenate.95), channel_id=1, source_target_pairs={{0,2},{1,3},{2,0},{3,1},{4,6},{5,7},{6,4},{7,5},{8,10},{9,11},{10,... | collective-permute-start | bytes 1363976 | tf_op jit(solution)/shard_map/ppermute | solution.py:515
  25.4 119.4 %collective-permute-start.3 = (bf16[256,1536]{1,0:T(8,128)(2,1)S(1)}, bf16[256,1536]{1,0:T(8,128)(2,1)S(1)}, u32[]{:S(2)}, u32[]{:S(2)}) collective-permute-start(bf16[256,1536]{1,0:T(8,128)(2,1)S(1)} %get-tuple-element.383), channel_id=1, source_target_pairs={{0,4},{1,5},{2,6},{3,7},{4,0},{5,1},{6,2},{7,3},{8,12},{9,13},{10,... | collective-permute-start | bytes 2359304 | tf_op jit(solution)/shard_map/ppermute | solution.py:515
  190.5 77.1 %collective-permute-start.7 = (bf16[8,48,2304]{2,1,0:T(8,128)(2,1)}, bf16[8,48,2304]{2,1,0:T(8,128)(2,1)}, u32[]{:S(2)}, u32[]{:S(2)}) collective-permute-start(bf16[8,48,2304]{2,1,0:T(8,128)(2,1)} %pad_maximum_fusion.7), channel_id=1, source_target_pairs={{0,1},{1,0},{2,3},{3,2},{4,5},{5,4},{6,7},{7,6},{8,9},{9,8},{10,11... | collective-permute-start | bytes 5308424 | tf_op jit(solution)/shard_map/ppermute | solution.py:515
  193.3 75.8 %collective-permute-start.8 = (bf16[8,48,2432]{2,1,0:T(8,128)(2,1)}, bf16[8,48,2432]{2,1,0:T(8,128)(2,1)}, u32[]{:S(2)}, u32[]{:S(2)}) collective-permute-start(bf16[8,48,2432]{2,1,0:T(8,128)(2,1)} %pad_maximum_fusion.5), channel_id=1, source_target_pairs={{0,16},{8,24},{16,0},{24,8},{1,17},{9,25},{17,1},{25,9},{2,18},{10... | collective-permute-start | bytes 5603336 | tf_op jit(solution)/shard_map/ppermute | solution.py:518
  194.8 74.3 %collective-permute-start.9 = (bf16[8,48,2304]{2,1,0:T(8,128)(2,1)}, bf16[8,48,2304]{2,1,0:T(8,128)(2,1)}, u32[]{:S(2)}, u32[]{:S(2)}) collective-permute-start(bf16[8,48,2304]{2,1,0:T(8,128)(2,1)} %pad_maximum_fusion.7), channel_id=1, source_target_pairs={{0,8},{8,0},{16,24},{24,16},{1,9},{9,1},{17,25},{25,17},{2,10},{10... | collective-permute-start | bytes 5308424 | tf_op jit(solution)/shard_map/ppermute | solution.py:518
  196.4 76.5 %collective-permute-start.6 = (bf16[8,48,2432]{2,1,0:T(8,128)(2,1)}, bf16[8,48,2432]{2,1,0:T(8,128)(2,1)S(1)}, u32[]{:S(2)}, u32[]{:S(2)}) collective-permute-start(bf16[8,48,2432]{2,1,0:T(8,128)(2,1)} %pad_maximum_fusion.5), channel_id=1, source_target_pairs={{0,1},{1,0},{2,3},{3,2},{4,5},{5,4},{6,7},{7,6},{8,9},{9,8},{10,11... | collective-permute-start | bytes 5603336 | tf_op jit(solution)/shard_map/ppermute | solution.py:515
  285.2 345.7 %all-gather.6.cloned.1.call-start = ((), (), s32[]{:S(2)}) async-start(), calls=%async_computation.4 | async-start | bytes 7962624 | tf_op jit(solution)/shard_map/all_gather | solution.py:739
  289.6 83.3 %collective-permute-start.28 = (bf16[48,2240]{1,0:T(8,128)(2,1)}, bf16[48,2240]{1,0:T(8,128)(2,1)}, u32[]{:S(2)}, u32[]{:S(2)}) collective-permute-start(bf16[48,2240]{1,0:T(8,128)(2,1)} %get-tuple-element.427), channel_id=1, source_target_pairs={{0,24},{8,16},{16,8},{24,0},{1,25},{9,17},{17,9},{25,1},{2,26},{10... | collective-permute-start | bytes 645128 | tf_op jit(solution)/shard_map/ppermute | solution.py:518
  292.0 80.9 %collective-permute-start.29 = (bf16[48,2240]{1,0:T(8,128)(2,1)}, bf16[48,2240]{1,0:T(8,128)(2,1)}, u32[]{:S(2)}, u32[]{:S(2)}) collective-permute-start(bf16[48,2240]{1,0:T(8,128)(2,1)} %get-tuple-element.426), channel_id=1, source_target_pairs={{0,16},{8,24},{16,0},{24,8},{1,17},{9,25},{17,1},{25,9},{2,18},{10... | collective-permute-start | bytes 645128 | tf_op jit(solution)/shard_map/ppermute | solution.py:518
  292.5 80.4 %collective-permute-start.30 = (bf16[48,2240]{1,0:T(8,128)(2,1)}, bf16[48,2240]{1,0:T(8,128)(2,1)}, u32[]{:S(2)}, u32[]{:S(2)}) collective-permute-start(bf16[48,2240]{1,0:T(8,128)(2,1)} %get-tuple-element.425), channel_id=1, source_target_pairs={{0,8},{8,0},{16,24},{24,16},{1,9},{9,1},{17,25},{25,17},{2,10},{10... | collective-permute-start | bytes 645128 | tf_op jit(solution)/shard_map/ppermute | solution.py:518
  320.2 92.5 %collective-permute-start.25 = (bf16[128,3072]{1,0:T(8,128)(2,1)S(1)}, bf16[128,3072]{1,0:T(8,128)(2,1)}, u32[]{:S(2)}, u32[]{:S(2)}) collective-permute-start(bf16[128,3072]{1,0:T(8,128)(2,1)S(1)} %text_post.1.refs_0_), channel_id=1, source_target_pairs={{0,2},{1,3},{2,0},{3,1},{4,6},{5,7},{6,4},{7,5},{8,10},{9,11},{10,... | collective-permute-start | bytes 2359304 | tf_op jit(solution)/shard_map/ppermute | solution.py:515
  415.4 1014.5 %reduce-scatter.6.cloned.1.call-start = ((), (), s32[]{:S(2)}) async-start(), calls=%async_computation.7 | async-start | bytes 7962624 | tf_op jit(solution)/shard_map/reduce_scatter | solution.py:790
  417.3 79.9 %collective-permute-start.22 = (bf16[512,1536]{1,0:T(8,128)(2,1)S(1)}, bf16[512,1536]{1,0:T(8,128)(2,1)S(1)}, u32[]{:S(2)}, u32[]{:S(2)}) collective-permute-start(bf16[512,1536]{1,0:T(8,128)(2,1)S(1)} %fusion.83), channel_id=1, source_target_pairs={{0,8},{8,0},{16,24},{24,16},{1,9},{9,1},{17,25},{25,17},{2,10},{10... | collective-permute-start | bytes 4718600 | tf_op jit(solution)/shard_map/ppermute | solution.py:518
  419.1 78.1 %collective-permute-start.23 = (bf16[512,1536]{1,0:T(8,128)(2,1)S(1)}, bf16[512,1536]{1,0:T(8,128)(2,1)S(1)}, u32[]{:S(2)}, u32[]{:S(2)}) collective-permute-start(bf16[512,1536]{1,0:T(8,128)(2,1)S(1)} %fusion.83), channel_id=1, source_target_pairs={{0,16},{8,24},{16,0},{24,8},{1,17},{9,25},{17,1},{25,9},{2,18},{10... | collective-permute-start | bytes 4718600 | tf_op jit(solution)/shard_map/ppermute | solution.py:518
  420.5 76.6 %collective-permute-start.24 = (bf16[512,1536]{1,0:T(8,128)(2,1)S(1)}, bf16[512,1536]{1,0:T(8,128)(2,1)S(1)}, u32[]{:S(2)}, u32[]{:S(2)}) collective-permute-start(bf16[512,1536]{1,0:T(8,128)(2,1)S(1)} %fusion.83), channel_id=1, source_target_pairs={{0,24},{8,16},{16,8},{24,0},{1,25},{9,17},{17,9},{25,1},{2,26},{10... | collective-permute-start | bytes 4718600 | tf_op jit(solution)/shard_map/ppermute | solution.py:518
  676.2 78.0 %collective-permute-start.34 = (bf16[512,1536]{1,0:T(8,128)(2,1)}, bf16[512,1536]{1,0:T(8,128)(2,1)}, u32[]{:S(2)}, u32[]{:S(2)}) collective-permute-start(bf16[512,1536]{1,0:T(8,128)(2,1)} %convolution_convert_fusion.14), channel_id=1, source_target_pairs={{0,8},{8,0},{16,24},{24,16},{1,9},{9,1},{17,25},{25,17},{2,10},{10... | collective-permute-start | bytes 4718600 | tf_op jit(solution)/shard_map/ppermute | solution.py:518
  780.6 661.2 %reduce-scatter.8.cloned.1.call-start = ((), (), s32[]{:S(2)}) async-start(), calls=%async_computation.8 | async-start | bytes 7741440 | tf_op jit(solution)/shard_map/reduce_scatter | solution.py:784
  821.3 632.3 %reduce-scatter.4.cloned.1.call-start = ((), (), s32[]{:S(2)}) async-start(), calls=%async_computation.6 | async-start | bytes 9732096 | tf_op jit(solution)/shard_map/reduce_scatter | solution.py:817
  925.5 75.5 %collective-permute-start.56 = (bf16[512,1024]{1,0:T(8,128)(2,1)}, bf16[512,1024]{1,0:T(8,128)(2,1)}, u32[]{:S(2)}, u32[]{:S(2)}) collective-permute-start(bf16[512,1024]{1,0:T(8,128)(2,1)} %get-tuple-element.213), channel_id=1, source_target_pairs={{0,1},{1,0},{2,3},{3,2},{4,5},{5,4},{6,7},{7,6},{8,9},{9,8},{10,11... | collective-permute-start | bytes 3145736 | tf_op jit(solution)/shard_map/ppermute | solution.py:515
  943.7 82.0 %collective-permute-start.59 = (bf16[512,1024]{1,0:T(8,128)(2,1)}, bf16[512,1024]{1,0:T(8,128)(2,1)}, u32[]{:S(2)}, u32[]{:S(2)}) collective-permute-start(bf16[512,1024]{1,0:T(8,128)(2,1)} %get-tuple-element.217), channel_id=1, source_target_pairs={{0,1},{1,0},{2,3},{3,2},{4,5},{5,4},{6,7},{7,6},{8,9},{9,8},{10,11... | collective-permute-start | bytes 3145736 | tf_op jit(solution)/shard_map/ppermute | solution.py:515
  1001.0 84.6 %collective-permute-start.64 = (bf16[512,1024]{1,0:T(8,128)(2,1)}, bf16[512,1024]{1,0:T(8,128)(2,1)}, u32[]{:S(2)}, u32[]{:S(2)}) collective-permute-start(bf16[512,1024]{1,0:T(8,128)(2,1)} %add_convert_fusion.15), channel_id=1, source_target_pairs={{0,2},{1,3},{2,0},{3,1},{4,6},{5,7},{6,4},{7,5},{8,10},{9,11},{10,... | collective-permute-start | bytes 3145736 | tf_op jit(solution)/shard_map/ppermute | solution.py:515
  1022.0 84.9 %collective-permute-start.43 = (bf16[4,48,1536]{2,1,0:T(8,128)(2,1)}, bf16[4,48,1536]{2,1,0:T(8,128)(2,1)S(1)}, u32[]{:S(2)}, u32[]{:S(2)}) collective-permute-start(bf16[4,48,1536]{2,1,0:T(8,128)(2,1)} %get-tuple-element.420), channel_id=1, source_target_pairs={{0,16},{8,24},{16,0},{24,8},{1,17},{9,25},{17,1},{25,9},{2,18},{10... | collective-permute-start | bytes 1769480 | tf_op jit(solution)/shard_map/ppermute | solution.py:518
  1025.7 81.2 %collective-permute-start.44 = (bf16[2,4,48,1536]{3,2,1,0:T(8,128)(2,1)S(1)}, bf16[2,4,48,1536]{3,2,1,0:T(8,128)(2,1)S(1)}, u32[]{:S(2)}, u32[]{:S(2)}) collective-permute-start(bf16[2,4,48,1536]{3,2,1,0:T(8,128)(2,1)S(1)} %copy-done.114), channel_id=1, source_target_pairs={{0,16},{8,24},{16,0},{24,8},{1,17},{9,25},{17,1},{25,9},{2,18},{10... | collective-permute-start | bytes 3538952 | tf_op jit(solution)/shard_map/ppermute | solution.py:518
  1136.4 103.1 %collective-permute-start.65 = (bf16[2,2,4,48,1536]{4,3,2,1,0:T(8,128)(2,1)}, bf16[2,2,4,48,1536]{4,3,2,1,0:T(8,128)(2,1)S(1)}, u32[]{:S(2)}, u32[]{:S(2)}) collective-permute-start(bf16[2,2,4,48,1536]{4,3,2,1,0:T(8,128)(2,1)} %get-tuple-element.328), channel_id=1, source_target_pairs={{0,1},{1,0},{2,3},{3,2},{4,5},{5,4},{6,7},{7,6},{8,9},{9,8},{10,11... | collective-permute-start | bytes 7077896 | tf_op jit(solution)/shard_map/ppermute | solution.py:515
  1195.5 76.4 %collective-permute-start.55 = (bf16[512,1536]{1,0:T(8,128)(2,1)}, bf16[512,1536]{1,0:T(8,128)(2,1)S(1)}, u32[]{:S(2)}, u32[]{:S(2)}) collective-permute-start(bf16[512,1536]{1,0:T(8,128)(2,1)} %convolution_convert_fusion.9), channel_id=1, source_target_pairs={{0,24},{8,16},{16,8},{24,0},{1,25},{9,17},{17,9},{25,1},{2,26},{10... | collective-permute-start | bytes 4718600 | tf_op jit(solution)/shard_map/ppermute | solution.py:518
  1346.2 104.0 %collective-permute-start.72 = (bf16[2,256,1536]{2,1,0:T(8,128)(2,1)}, bf16[2,256,1536]{2,1,0:T(8,128)(2,1)S(1)}, u32[]{:S(2)}, u32[]{:S(2)}) collective-permute-start(bf16[2,256,1536]{2,1,0:T(8,128)(2,1)} %slice.228), channel_id=1, source_target_pairs={{0,4},{1,5},{2,6},{3,7},{4,0},{5,1},{6,2},{7,3},{8,12},{9,13},{10,... | collective-permute-start | bytes 4718600 | tf_op jit(solution)/shard_map/ppermute | solution.py:515
  1355.6 73.5 %collective-permute-start.84 = (bf16[48,1536]{1,0:T(8,128)(2,1)S(1)}, bf16[48,1536]{1,0:T(8,128)(2,1)S(1)}, u32[]{:S(2)}, u32[]{:S(2)}) collective-permute-start(bf16[48,1536]{1,0:T(8,128)(2,1)S(1)} %get-tuple-element.403), channel_id=1, source_target_pairs={{0,4},{1,5},{2,6},{3,7},{4,0},{5,1},{6,2},{7,3},{8,12},{9,13},{10,... | collective-permute-start | bytes 442376 | tf_op jit(solution)/shard_map/ppermute | solution.py:515
  1355.9 73.2 %collective-permute-start.83 = (bf16[48,1536]{1,0:T(8,128)(2,1)S(1)}, bf16[48,1536]{1,0:T(8,128)(2,1)S(1)}, u32[]{:S(2)}, u32[]{:S(2)}) collective-permute-start(bf16[48,1536]{1,0:T(8,128)(2,1)S(1)} %get-tuple-element.401), channel_id=1, source_target_pairs={{0,2},{1,3},{2,0},{3,1},{4,6},{5,7},{6,4},{7,5},{8,10},{9,11},{10,... | collective-permute-start | bytes 442376 | tf_op jit(solution)/shard_map/ppermute | solution.py:515
  1359.5 75.7 %collective-permute-start.88 = (bf16[48,1536]{1,0:T(8,128)(2,1)}, bf16[48,1536]{1,0:T(8,128)(2,1)S(1)}, u32[]{:S(2)}, u32[]{:S(2)}) collective-permute-start(bf16[48,1536]{1,0:T(8,128)(2,1)} %get-tuple-element.399), channel_id=1, source_target_pairs={{0,6},{1,7},{2,4},{3,5},{4,2},{5,3},{6,0},{7,1},{8,14},{9,15},{10,... | collective-permute-start | bytes 442376 | tf_op jit(solution)/shard_map/ppermute | solution.py:515
  (254 other events, 6104.8 us)
Sparse Core Ops, SparseCore 0:
  13.0 249.3 all-gather.3
  285.4 99.2 all-gather.7
  415.5 80.4 all-gather.5
  780.7 96.3 reduce-scatter.5
  879.2 73.7 reduce-scatter.7
  1004.4 155.7 reduce-scatter.3

commit v2 on v1

--- a/solution.py
+++ b/solution.py
@@ -434,9 +434,10 @@
     slots, _, right_width = right[0][0].shape
     left_width = left[0][0].shape[2]
     count = len(left)
+    extra = left_width > right_width
 
     def kernel(numbers_ref, *refs):
-        whole_ref, small_ref = refs[4 * count :]
+        whole_ref = refs[4 * count]
         step = pl.program_id(0)
         for at in range(count):
             for core in range(2):
@@ -448,7 +449,8 @@
                         left_ref, right_ref = refs[4 * at + other], refs[4 * at + 2 + other]
                         whole_ref[place, :right_width] = left_ref[0, :, :right_width]
                         whole_ref[place, right_width:] = right_ref[0]
-                        small_ref[place] = left_ref[0, :, right_width:]
+                        if extra:
+                            refs[4 * count + 1][place] = left_ref[0, :, right_width:]
 
     def source(at, width):
         return pl.BlockSpec(
@@ -472,12 +474,12 @@
             out_specs=[
                 pl.BlockSpec((2 * rows, 2 * right_width), index),
                 pl.BlockSpec((2 * rows, left_width - right_width), index),
-            ],
+            ][: 1 + extra],
         ),
         out_shape=[
             jax.ShapeDtypeStruct((total, 2 * right_width), BF),
             jax.ShapeDtypeStruct((total, left_width - right_width), BF),
-        ],
+        ][: 1 + extra],
         compiler_params=params(32),
         cost_estimate=pl.CostEstimate(flops=0, bytes_accessed=8 * total * right_width, transcendentals=0),
         name="place_rows",
@@ -548,33 +550,16 @@
     def gather_columns(self, shard):
         return jnp.stack([shard] + [self.over_seq(shard, 2 * k) for k in range(1, self.columns)])
 
-    def gather_dp(self, sides, orders):
-        sides, offsets = list(sides), [[0] for _ in sides]
-        for number in range(len(orders[0])):
-            received = together(*[self.over_dp(one, order[number]) for one, order in zip(sides, orders)])
-            for i, order in enumerate(orders):
-                flipped = [at ^ order[number] for at in offsets[i]]
-                if number + 1 < len(order):
-                    sides[i], offsets[i] = jnp.concatenate([sides[i], received[i]]), offsets[i] + flipped
-                else:
-                    sides[i], offsets[i] = [sides[i], received[i]], [offsets[i], flipped]
-        return sides, offsets
-
-    def gather_core(self, held):
-        return [(one, self.over_seq(one, 1)) for one in held]
-
-    def gather_place(self, left, left_offsets, right, right_offsets):
+    def gather_dp(self, sides, orders, number):
+        return [
+            {at ^ order[number]: self.over_dp(one, order[number]) for at, one in side.items()}
+            for side, order in zip(sides, orders)
+        ]
+
+    def gather_place(self, sides):
+        left, right = [{at: (one, self.over_seq(one, 1)) for at, one in side.items()} for side in sides]
         slots = self.columns
         rows, width = right[0][0].shape[1:]
-
-        def by_offset(held, offsets):
-            return {
-                at: tuple(one[i * slots : (i + 1) * slots] for one in pair)
-                for pair, ats in zip(held, offsets)
-                for i, at in enumerate(ats)
-            }
-
-        left, right = by_offset(left, left_offsets), by_offset(right, right_offsets)
         if rows % 16 == 0:
             blocks = [(self.dp ^ at) * slots + (self.column ^ slot) for at in left for slot in range(slots)]
             numbers = jnp.stack([self.core] + blocks).astype(jnp.int32)
@@ -597,7 +582,7 @@
             ordered = lax.fori_loop(0, self.total, place, jnp.zeros_like(stacked))
             wholes.append(ordered.reshape(self.total * rows, -1))
         left, right = wholes
-        return jnp.concatenate([left[:, :width], right], axis=1), left[:, width:]
+        return [jnp.concatenate([left[:, :width], right], axis=1), left[:, width:]]
 
     def xor_order(self, pieces, number):
         bit = 1
@@ -618,11 +603,17 @@
         return total
 
 
-    def scatter_core(self, value):
+    def scatter_core(self, *values):
         bits = len(self.dp_bits)
-        value = value.reshape((2,) * bits + (self.columns, 2, value.shape[0] // self.total, value.shape[1]))
-        sent = self.over_seq(self.pick(value, 1 - self.core, bits + 1), 1)
-        return self.pick(value, self.core, bits + 1), sent
+        values = [
+            one.reshape((2,) * bits + (self.columns, 2, one.shape[0] // self.total, one.shape[1]))
+            for one in values
+        ]
+        kept, sent = [
+            jnp.concatenate([self.pick(one, core, bits + 1) for one in values], axis=-1)
+            for core in (self.core, 1 - self.core)
+        ]
+        return kept, self.over_seq(sent, 1)
 
     def scatter_dp(self, halves, done, bit):
         value = (halves[0].astype(F32) + halves[1].astype(F32)).astype(BF)
@@ -631,14 +622,16 @@
         sent = self.over_dp(self.pick(value, 1 - mine, axis), bit)
         return self.pick(value, mine, axis), sent
 
-    def scatter_dps(self, halves, bits, done=()):
-        for bit in bits:
-            halves = self.scatter_dp(halves, done, bit)
-            done = done + (bit,)
-        return halves
-
-    def scatter_last(self, halves):
-        return self.scatter_columns(halves[0].astype(F32) + halves[1].astype(F32), 0, BF)
+    def scatter_pair(self, pair, orders, number):
+        return [
+            self.scatter_dp(halves, order[:number], order[number]) for halves, order in zip(pair, orders)
+        ]
+
+    def scatter_pair_last(self, pair):
+        value = jnp.concatenate([halves[0].astype(F32) + halves[1].astype(F32) for halves in pair], axis=-1)
+        width = pair[0][0].shape[-1]
+        total = self.scatter_columns(value.astype(BF), 0, BF)
+        return total[:, :width], total[:, width:]
 
 
 def body(
@@ -685,34 +678,29 @@
     side = jnp.concatenate([selfquery, selfkey, selfvalue], axis=1)
     both = plan.gather_columns(jnp.concatenate([side[:, :middle], small, side[:, middle:]], axis=1))
     token_rows = plan.shift(latents)
-    both, token_rows = together(both, token_rows)
-    (left_held, right_held), (left_offsets, right_offsets) = plan.gather_dp(
-        (both[:, :, : middle + HEAD_DIM], both[:, :, middle + HEAD_DIM :]), (xy, yx)
-    )
-    left_held, right_held = plan.gather_core(left_held), plan.gather_core(right_held)
-    whole_self, small_all = plan.gather_place(left_held, left_offsets, right_held, right_offsets)
-    small_all = small_all.T[:12].astype(F32)
-
-    others = jnp.concatenate([selfout, crossquery, crossout, crosskey, crossvalue], axis=1)
-    whole_others = lax.all_gather(others, everywhere, axis=0, tiled=True)
-    whole_selfout, whole_crossquery, whole_crossout = [
-        whole_others[:, i * width : (i + 1) * width] for i in range(3)
-    ]
-    whole_crosstext = whole_others[:, 3 * width :]
-
-    up_rows = after(upmatrix, both)
     up_parts = [
-        lax.dynamic_slice_in_dim(up_rows, (plan.dp ^ j) * part, part, 1) for j in range(dp_n)
+        lax.dynamic_slice_in_dim(upmatrix, (plan.dp ^ j) * part, part, 1) for j in range(dp_n)
     ]
     up_parts = [plan.over_dp(one, j) if j else one for j, one in enumerate(up_parts)]
+    both, token_rows, up_parts = together(both, token_rows, up_parts)
     up_shard = jnp.concatenate(plan.xor_order(up_parts, plan.dp), axis=0)
-    shifted = plan.shift(after(jnp.concatenate([cotangent, context], axis=1), both))
-    down_shard, whole_self, shifted, _ = together(downmatrix, whole_self, shifted, whole_others)
-    whole_down = lax.all_gather(down_shard, "seq", axis=0, tiled=True)
-    text_one = context.shape[1]
-    step = rows_one + text_one
-    grad_rows = jnp.concatenate([shifted[:rows_one], shifted[step : step + rows_one]])
-    text_rows = jnp.concatenate([shifted[rows_one:step], shifted[step + rows_one :]])
+    edge = middle + HEAD_DIM
+    first = [{0: both[:, :, :edge]}, {0: both[:, :, edge:]}]
+
+    others = after(jnp.concatenate([selfout, crossquery, crossout, crosskey, crossvalue], axis=1), both)
+    others = plan.gather_columns(others)
+    for number in range(len(xy)):
+        arrived = plan.gather_dp(first, (xy, yx), number)
+        if number + 1 < len(xy):
+            arrived = together(*arrived)
+        else:
+            *arrived, others = together(*arrived, others)
+        first = [{**side, **more} for side, more in zip(first, arrived)]
+    whole_self, small_all = plan.gather_place(first)
+    small_placed = small_all
+    small_all = small_all.T[:12].astype(F32)
+    edge = 5 * width // 2
+    second = [{0: others[:, :, :edge]}, {0: others[:, :, edge:]}]
 
     mod_rows = lax.dynamic_index_in_dim(modulation, plan.top, 0, keepdims=False) + small_all[:6]
     shift_a, scale_a, gate_a, shift_m, scale_m, gate_m = [mod_rows[i : i + 1] for i in range(6)]
@@ -729,98 +717,132 @@
     normed_a = layer_norm(latent_rows)
     attn_in = (normed_a * (1.0 + scale_a) + shift_a).astype(BF)
     self_raw = dot_nn(attn_in, whole_self)
+    shifted = plan.shift(after(jnp.concatenate([cotangent, context], axis=1), small_placed))
+    *arrived, self_raw = together(*plan.gather_dp(second, (xy, yx), 0), self_raw)
+    second = [{**side, **more} for side, more in zip(second, arrived)]
     queries, *keyvalues = self_post(self_raw, gain_query, gain_key, tables, plan.groups)
+    keyvalues, shifted = together(keyvalues, shifted)
+    text_one = context.shape[1]
+    step = rows_one + text_one
+    grad_rows = jnp.concatenate([shifted[:rows_one], shifted[step : step + rows_one]])
+    text_rows = jnp.concatenate([shifted[rows_one:step], shifted[step + rows_one :]])
     per_group = HEADS // plan.groups
     gathered = []
-    for one in keyvalues:
+    for group, one in enumerate(keyvalues):
         behind = [gathered[-1][plan.group_bits[-1]]] if gathered else []
         gathered.append(plan.group_gather(one, *behind))
-    up_shard = after(up_shard, gathered[0][plan.group_bits[-1]])
+        if group < 2:
+            number = len(xy) - 1
+            if group == 0:
+                for early in range(1, number):
+                    arrived = plan.gather_dp(second, (xy, yx), early)
+                    second = [{**side, **more} for side, more in zip(second, arrived)]
+                half = len(second[0]) // 2
+                parts = [dict(list(side.items())[:half]) for side in second]
+                whole_second = [dict(side) for side in second]
+            else:
+                parts = [dict(list(side.items())[half:]) for side in second]
+                parts, arrived = together(parts, arrived)
+            if plan.groups == 1:
+                parts = second
+            bit = plan.group_bits[-1]
+            arrived, gathered[-1][bit] = together(
+                plan.gather_dp(parts, (xy, yx), number), gathered[-1][bit]
+            )
+            whole_second = [{**side, **more} for side, more in zip(whole_second, arrived)]
+    second = whole_second
+    arrived = gathered[-1][plan.group_bits[-1]]
+    (whole_others,) = plan.gather_place(second)[:1]
+    whole_selfout, whole_crossquery, whole_crossout = [
+        whole_others[:, i * width : (i + 1) * width] for i in range(3)
+    ]
+    whole_crosstext = whole_others[:, 3 * width :]
+    text_raw = dot_nn(text_rows, whole_crosstext)
+    text_keyvalues = text_post(text_raw, gain_crossk)
+    gathered[-1], text_keyvalues = together(gathered[-1], text_keyvalues)
+    cross_gathered = plan.group_gather(text_keyvalues)
+    up_shard = after(up_shard, arrived)
     whole_up = lax.all_gather(up_shard, "seq", axis=0, tiled=True)
     whole_up = (
         whole_up.reshape(seq_n, dp_n, shard_rows, part)
         .transpose(1, 0, 2, 3)
         .reshape(plan.total * shard_rows, part)
     )
-    out_grad = grad_rows.astype(F32)
-    down_grad = (out_grad * gate_m).astype(BF)
-    down_grads = [down_grad] + [plan.over_dp(down_grad, j) for j in range(1, dp_n)]
     self_outs, self_logs = [], []
     for group in range(plan.groups):
         out, logs = attend(queries, list(gathered[group].values()), group * per_group, per_group)
         self_outs.append(out)
         self_logs.append(logs)
-    *self_outs, down_grads = together(*self_outs, down_grads)
+    down_shard = after(downmatrix, cross_gathered[plan.group_bits[-1]])
+    whole_down = lax.all_gather(down_shard, "seq", axis=0, tiled=True)
+    out_grad = grad_rows.astype(F32)
+    down_grad = (out_grad * gate_m).astype(BF)
+    down_grads = [down_grad] + [plan.over_dp(down_grad, j) for j in range(1, dp_n)]
     attended = jnp.concatenate(self_outs, axis=1)
     self_branch = dot_nn(attended, whole_selfout)
     hidden_one = latent_rows + self_branch * gate_a
 
-    text_raw = dot_nn(text_rows, whole_crosstext)
-    cross_gathered = plan.group_gather(text_post(text_raw, gain_crossk))
     cross_in = (layer_norm(hidden_one) * gain_norm + bias_norm).astype(BF)
     crossq_raw = dot_nn(cross_in, whole_crossquery)
     cross_queries = query_post(crossq_raw, gain_crossq)
     crossed, cross_logs = attend(cross_queries, list(cross_gathered.values()), 0, HEADS)
+    crossed, down_grads = together(crossed, down_grads)
     hidden_two = hidden_one + dot_nn(crossed, whole_crossout)
 
-    act_grads = [dot_nt(one, whole_down) for one in down_grads]
     normed_m = layer_norm(hidden_two)
     mlp_in = (normed_m * (1.0 + scale_m) + shift_m).astype(BF)
-    mlp_ins = [mlp_in] + [plan.over_dp(mlp_in, j) for j in range(1, dp_n)]
-    activations, up_grads, mlp_grads = [], [], []
+    received = [plan.over_dp(mlp_in, j) for j in range(1, dp_n)]
+    mlp_ins, activations, up_grads, mlp_grads = [mlp_in], [], [], []
     for j in range(dp_n):
         up_values = dot_nn(mlp_ins[j], whole_up)
         activation, gelu_back = jax.vjp(gelu_tanh, up_values)
         activations.append(activation.astype(BF))
-        up_grads.append(gelu_back(act_grads[j])[0].astype(BF))
+        up_grads.append(gelu_back(dot_nt(down_grads[j], whole_down))[0].astype(BF))
         mlp_grads.append(dot_nt(up_grads[j], whole_up, BF if j else F32))
+        if j + 1 < dp_n:
+            one, activations[j] = together(received[j], activations[j])
+            mlp_ins.append(one)
     mlp_sent = [plan.over_dp(mlp_grads[j], j) for j in range(1, dp_n)]
 
     up_in, down_in, _ = together(jnp.concatenate(mlp_ins), jnp.concatenate(activations), mlp_grads[0])
+    down_term = dot_tn(down_in, jnp.concatenate(down_grads), BF)
     up_term = dot_tn(up_in, jnp.concatenate(up_grads), BF)
-    down_term = dot_tn(down_in, jnp.concatenate(down_grads), BF)
-    *mlp_sent, up_term, down_term = together(*mlp_sent, up_term, down_term)
-    mlp_grad = mlp_grads[0] + sum(one.astype(F32) for one in mlp_sent)
-    downmatrix_gradient = lax.psum_scatter(down_term, "seq", scatter_dimension=0, tiled=True).astype(F32)
     up_term = (
         up_term.reshape(dp_n, seq_n, shard_rows, part)
         .transpose(1, 0, 2, 3)
         .reshape(plan.total * shard_rows, part)
     )
+    mlp_sent, up_term = together(mlp_sent, up_term)
+    downmatrix_gradient = lax.psum_scatter(down_term, "seq", scatter_dimension=0, tiled=True).astype(F32)
     up_term = lax.psum_scatter(up_term, "seq", scatter_dimension=0, tiled=True)
     up_term = up_term.reshape(dp_n, shard_rows, part)
+    mlp_grad = mlp_grads[0] + sum(one.astype(F32) for one in mlp_sent)
+    activations, mlp_grad = together(activations, mlp_grad)
+    down_all = [dot_nn(activations[j], whole_down, BF if j else F32) for j in range(dp_n)]
+    down_sent = [plan.over_dp(down_all[j], j) for j in range(1, dp_n)]
+    mlp_grad, down_all = together(mlp_grad, down_all)
 
     shift_m_grad = jnp.sum(mlp_grad, axis=0)
     scale_m_grad = jnp.sum(mlp_grad * normed_m, axis=0)
     two_grad = out_grad + layer_norm_back(hidden_two, mlp_grad * (1.0 + scale_m))
     cross_grad = two_grad.astype(BF)
     crossed_grad = dot_nt(cross_grad, whole_crossout, BF)
-    crossout_sum = plan.scatter_core(dot_tn(crossed, cross_grad, BF))
+    crossout_term = dot_tn(crossed, cross_grad, BF)
     crossq_grad, *cross_parts = attend_back(
         cross_queries, list(cross_gathered.values()), crossed_grad, cross_logs, 0, HEADS
     )
-    crossq_grad, crossout_sum = together(crossq_grad, crossout_sum)
-    crossout_sum = plan.scatter_dp(crossout_sum, (), xy[0])
     cross_own = plan.group_scatter(dict(zip(cross_gathered, cross_parts)))
     crossq_low, crossq_gaingrad = query_back(crossq_grad, crossq_raw, gain_crossq)
-    crossq_sum = plan.scatter_core(dot_tn(cross_in, crossq_low, BF))
+    cross_sums = [plan.scatter_core(crossout_term), plan.scatter_core(dot_tn(cross_in, crossq_low, BF))]
     crossin_grad = dot_nt(crossq_low, whole_crossquery)
     normgain_grad = jnp.sum(crossin_grad * layer_norm(hidden_one), axis=0)
     normbias_grad = jnp.sum(crossin_grad, axis=0)
     one_grad = two_grad + layer_norm_back(hidden_one, crossin_grad * gain_norm)
     gate_a_grad = jnp.sum(one_grad * self_branch, axis=0)
     branch_grad = (one_grad * gate_a).astype(BF)
-    branch_grad, crossq_sum, crossout_sum, cross_own = together(branch_grad, crossq_sum, crossout_sum, cross_own)
-    crossq_sum = plan.scatter_dp(crossq_sum, (), yx[0])
-    crossout_sum = plan.scatter_dps(crossout_sum, xy[1:], (xy[0],))
-    text_low, crossk_gaingrad = text_back(cross_own, text_raw, gain_crossk)
-    text_gradients = lax.psum_scatter(
-        dot_tn(text_rows, text_low, BF), everywhere, scatter_dimension=0, tiled=True
-    ).astype(F32)
-    context_gradient = plan.unshift(dot_nt(text_low, whole_crosstext, BF))
-
+    branch_grad, cross_sums = together(branch_grad, cross_sums)
+    cross_sums = plan.scatter_pair(cross_sums, (xy, yx), 0)
     attended_grad = dot_nt(branch_grad, whole_selfout, BF)
-    selfout_sum = plan.scatter_core(dot_tn(attended, branch_grad, BF))
     query_grads, keyvalue_grads = [], []
     for group in range(plan.groups):
         query_grad, *parts = attend_back(
@@ -832,45 +854,62 @@
             per_group,
         )
         if group == 0:
-            query_grad, crossout_sum, crossq_sum, context_gradient, selfout_sum = together(
-                query_grad, crossout_sum, crossq_sum, context_gradient, selfout_sum
+            query_grad, cross_own = together(query_grad, cross_own)
+            text_low, crossk_gaingrad = text_back(cross_own, text_raw, gain_crossk)
+            text_term = dot_tn(text_rows, text_low, BF)
+            selfout_term = dot_tn(attended, branch_grad, BF)
+            pieces = [
+                (text_term[:, :width], selfout_term[:, : width // 2]),
+                (text_term[:, width:], selfout_term[:, width // 2 :]),
+            ]
+            text_sums = [plan.scatter_core(*pair) for pair in pieces]
+            context_gradient = plan.unshift(dot_nt(text_low, whole_crosstext, BF))
+        if group == min(1, plan.groups - 1):
+            query_grad, cross_sums, text_sums, context_gradient, down_sent = together(
+                query_grad, cross_sums, text_sums, context_gradient, down_sent
             )
-            crossout_gradient = plan.scatter_last(crossout_sum)
-            crossq_sum = plan.scatter_dps(crossq_sum, yx[1:], (yx[0],))
-            selfout_sum = plan.scatter_dp(selfout_sum, (), xy[0])
+            down_values = down_all[0] + sum(one.astype(F32) for one in down_sent)
+            layer_output = plan.unshift((hidden_two + down_values * gate_m).astype(BF))
+            gate_m_grad = jnp.sum(out_grad * down_values, axis=0)
+            for number in range(1, len(xy)):
+                cross_sums = plan.scatter_pair(cross_sums, (xy, yx), number)
+            text_sums = plan.scatter_pair(text_sums, (xy, yx), 0)
+        if group == plan.groups - 1:
+            query_grad, cross_sums, text_sums, layer_output = together(
+                query_grad, cross_sums, text_sums, layer_output
+            )
+            for number in range(1, len(xy)):
+                text_sums = plan.scatter_pair(text_sums, (xy, yx), number)
+            crossout_gradient, crossquery_gradient = plan.scatter_pair_last(cross_sums)
         query_grads.append(query_grad)
         keyvalue_grads.append(plan.group_scatter(dict(zip(gathered[group], parts))))
+
     query_low, query_gaingrad = self_query_back(query_grads, self_raw, gain_query, tables)
-    query_low, crossout_gradient, crossq_sum, selfout_sum = together(
-        query_low, crossout_gradient, crossq_sum, selfout_sum
-    )
-    crossquery_gradient = plan.scatter_last(crossq_sum)
-    selfout_sum = plan.scatter_dps(selfout_sum, xy[1:], (xy[0],))
-    query_sum = plan.scatter_core(dot_tn(attn_in, query_low, BF))
+    query_low, text_sums, crossout_gradient, crossquery_gradient = together(
+        query_low, text_sums, crossout_gradient, crossquery_gradient
+    )
+    left, right = plan.scatter_pair_last(text_sums)
+    query_term = dot_tn(attn_in, query_low, BF)
     attn_grad = dot_nt(query_low, whole_self[:, :width])
-
-    *activations, query_sum = together(*activations, query_sum)
-    query_sum = plan.scatter_dp(query_sum, (), yx[0])
-    down_all = [dot_nn(activations[j], whole_down, BF if j else F32) for j in range(dp_n)]
-    down_sent = [plan.over_dp(down_all[j], j) for j in range(1, dp_n)]
-
+    keyvalue_grads, attn_grad, query_term = together(keyvalue_grads, attn_grad, query_term)
     keyvalue_low, key_gaingrad = self_keyvalue_back(keyvalue_grads, self_raw, gain_key, tables)
-    key_sum = plan.scatter_core(dot_tn(attn_in, keyvalue_low[:, :width], BF))
-    value_sum = plan.scatter_core(dot_tn(attn_in, keyvalue_low[:, width:], BF))
-    kept_low, _, _ = together(keyvalue_low, key_sum[0], value_sum[0])
+    keyvalue_low, left, right = together(keyvalue_low, left, right)
+    key_middle = middle - width
+    left_term = dot_tn(attn_in, keyvalue_low[:, :key_middle], BF)
+    right_term = dot_tn(attn_in, keyvalue_low[:, key_middle:], BF)
+    self_sums = [
+        plan.scatter_core(query_term, left_term),
+        plan.scatter_core(right_term),
+    ]
+    kept_low, _ = together(keyvalue_low, (left_term, right_term))
     attn_grad = attn_grad + dot_nt(kept_low, whole_self[:, width:])
-    key_sum, value_sum, selfout_sum, query_sum = together(key_sum, value_sum, selfout_sum, query_sum)
-    key_sum = plan.scatter_dp(key_sum, (), xy[0])
-    value_sum = plan.scatter_dp(value_sum, (), yx[0])
-    down_values = down_all[0] + sum(one.astype(F32) for one in down_sent)
-    layer_low = (hidden_two + down_values * gate_m).astype(BF)
-    gate_m_grad = jnp.sum(out_grad * down_values, axis=0)
-    selfout_gradient = plan.scatter_last(selfout_sum)
-    query_sum = plan.scatter_dps(query_sum, yx[1:], (yx[0],))
+    attn_grad, self_sums = together(attn_grad, self_sums)
+    crosskey_gradient, crossvalue_gradient = left[:, :width], right[:, :width]
+    selfout_gradient = jnp.concatenate([left[:, width:], right[:, width:]], axis=1)
+    self_sums = plan.scatter_pair(self_sums, (xy, yx), 0)
     shift_a_grad = jnp.sum(attn_grad, axis=0)
     scale_a_grad = jnp.sum(attn_grad * normed_a, axis=0)
     latents_low = (one_grad + layer_norm_back(latent_rows, attn_grad * (1.0 + scale_a))).astype(BF)
-
     local_mod = jnp.stack(
         [shift_a_grad, scale_a_grad, gate_a_grad, shift_m_grad, scale_m_grad, gate_m_grad]
     )
@@ -888,23 +927,16 @@
     for bit in plan.group_bits:
         sums = sums + plan.over_seq(sums, bit)
     other_sums = plan.over_seq(sums, plan.half)
-    both_low = jnp.stack([layer_low, latents_low])
-    both_low, key_sum, value_sum, query_sum = together(both_low, key_sum, value_sum, query_sum)
-    half_rows = both_low.shape[1] // 2
-    both_sent = plan.over_seq(both_low[:, half_rows:], plan.half)
-    layer_output, latents_gradient = [
-        jnp.where(plan.top == 0, jnp.stack([own, other]), jnp.stack([other, own]))
-        for own, other in zip(both_low[:, :half_rows], both_sent)
-    ]
+    latents_low, other_sums = together(latents_low, other_sums)
+    latents_gradient = plan.unshift(latents_low)
+    for number in range(1, len(xy)):
+        self_sums = plan.scatter_pair(self_sums, (xy, yx), number)
+    self_sums, latents_gradient = together(self_sums, latents_gradient)
     latents_gradient = latents_gradient.astype(F32)
-    key_sum = plan.scatter_dps(key_sum, xy[1:], (xy[0],))
-    value_sum = plan.scatter_dps(value_sum, yx[1:], (yx[0],))
-    selfquery_gradient = plan.scatter_last(query_sum)
+    self_gradients = jnp.concatenate(plan.scatter_pair_last(together(*self_sums)), axis=1)
     up_pieces = [plan.pick(up_term, plan.dp ^ j, 0) for j in range(dp_n)]
     up_pieces = [plan.over_dp(one, j) if j else one for j, one in enumerate(up_pieces)]
     upmatrix_gradient = jnp.concatenate(plan.xor_order(up_pieces, plan.dp), axis=1).astype(F32)
-    key_sum, value_sum = together(key_sum, value_sum)
-    selfkey_gradient, selfvalue_gradient = plan.scatter_last(key_sum), plan.scatter_last(value_sum)
     modulation_gradient = jnp.where(
         plan.top == 0, jnp.stack([sums[:6], other_sums[:6]]), jnp.stack([other_sums[:6], sums[:6]])
     )
@@ -920,17 +952,17 @@
         context_gradient.astype(F32),
         modulation_gradient,
         small_grads[:6],
-        selfquery_gradient,
-        selfkey_gradient,
-        selfvalue_gradient,
+        self_gradients[:, :width],
+        self_gradients[:, width : 2 * width],
+        self_gradients[:, 2 * width :],
         selfout_gradient,
         small_grads[6],
         small_grads[7],
         small_grads[8],
         small_grads[9],
         crossquery_gradient,
-        text_gradients[:, :width],
-        text_gradients[:, width:],
+        crosskey_gradient,
+        crossvalue_gradient,
         crossout_gradient,
         small_grads[10],
         small_grads[11],

time: 1470 us -> 1330 us (0.905)
  waiting for transfers between devices: 725 us -> 554 us
  other arithmetic: 85.1 us -> 126 us
  starting transfers between devices: 136 us -> 95.3 us
  Pallas kernels: 132 us -> 152 us
    ppermute x62 -> x69, waiting for transfers between devices: 482 us -> 394 us  [over_seq(): lax.ppermute(value, 'seq', [(i, i ^ offset) for i in range(self.seq_n)])]
    ppermute x36 -> x44, waiting for transfers between devices: 243 us -> 160 us  [over_dp(): lax.ppermute(value, 'dp', [(i, i ^ offset) for i in range(self.dp_n)])]
    ppermute x62 -> x69, starting transfers between devices: 88.9 us -> 46.4 us  [over_seq(): lax.ppermute(value, 'seq', [(i, i ^ offset) for i in range(self.seq_n)])]
    pallas_call x1 -> x2, Pallas kernels: 9.25 us -> 30.2 us  [place_rows(): pl.pallas_call(kernel, grid_spec=pltpu.PrefetchScalarGridSpec(num_scalar_...]
    unnamed x373 -> x391, local copies, waits for them, and re-layouts: 34.9 us -> 28.6 us
    squeeze x19 -> x22, local copies, waits for them, and re-layouts: 26.9 us -> 31.4 us  [pick(): return lax.dynamic_index_in_dim(value, number, axis, keepdims=False)]
    ppermute x36 -> x44, starting transfers between devices: 46.4 us -> 48.6 us  [over_dp(): lax.ppermute(value, 'dp', [(i, i ^ offset) for i in range(self.dp_n)])]
  transfers between devices with their start and end apart: 104 -> 117, of which waited for: 37 -> 47; matrix products, arithmetic and copies ran while one was open for 24% -> 33% of each run, Pallas kernels for 9% -> 11%
where the time goes in v2:
time: 1330 us; the launch traced here: 1320 us
  waiting for transfers between devices  554 us (42%)
  matrix products  257 us (19%)
  Pallas kernels  152 us (11%)
  other arithmetic  126 us (9%)
  local copies, waits for them, and re-layouts  119 us (9%)
  starting transfers between devices  95.3 us (7%)
  between operations  16.9 us (1%)
    ppermute x69, waiting for transfers between devices, over_seq(): lax.ppermute(value, 'seq', [(i, i ^ offset) for i in range(self.seq_n)])  394 us
    ppermute x44, waiting for transfers between devices, over_dp(): lax.ppermute(value, 'dp', [(i, i ^ offset) for i in range(self.dp_n)])  160 us
    dot_general x13, matrix products, dot_nn(): lax.dot_general(left, right, (((1,), (0,)), ((), ())), preferred_element_...  97.1 us
    dot_general x14, matrix products, dot_nt(): lax.dot_general(left, right, (((1,), (1,)), ((), ())), preferred_element_...  97.1 us
    pallas_call x4, Pallas kernels, attend_back(): pl.pallas_call(kernel, grid=(heads,), in_specs=[pl.BlockSpec((rows, HEAD_...  65.3 us
    dot_general x9, matrix products, dot_tn(): lax.dot_general(left, right, (((0,), (0,)), ((), ())), preferred_element_...  63 us
    ppermute x44, starting transfers between devices, over_dp(): lax.ppermute(value, 'dp', [(i, i ^ offset) for i in range(self.dp_n)])  48.6 us
    ppermute x69, starting transfers between devices, over_seq(): lax.ppermute(value, 'seq', [(i, i ^ offset) for i in range(self.seq_n)])  46.4 us
  transfers between devices with their start and end apart: 117, of which 47 were waited for; matrix products, arithmetic and copies ran while one was open for 33% of the time, Pallas kernels for 11%

profile of v2, /device:TPU:0, one launch (start us, length us, event | category | flops | bytes accessed | tf_op | source)
XLA Modules:
  0.0 1320.5 jit_solution(579579355553070864)
XLA Ops:
  33.3 42.5 %collective-permute-done.1 = bf16[48,4736]{1,0:T(8,128)(2,1)} collective-permute-done((bf16[48,4736]{1,0:T(8,128)(2,1)S(1)}, bf16[48,4736]{1,0:T(8,128)(2,1)}, u32[]{:S(2)}, u32[]{:S(2)}) %collective-permute-start.1) | collective-permute-done | bytes 454688 | tf_op jit(solution)/shard_map/ppermute | solution.py:517
  79.6 11.9 collective-permute-done.3
  103.9 13.3 %collective-permute-done.9.refs_10_ = bf16[4,48,2304]{2,1,0:T(8,128)(2,1)S(1)} collective-permute-done((bf16[4,48,2304]{2,1,0:T(8,128)(2,1)S(1)}, bf16[4,48,2304]{2,1,0:T(8,128)(2,1)S(1)}, u32[]{:S(2)}, u32[]{:S(2)}) %collective-permute-start.9) | collective-permute-done | bytes 884768 | tf_op jit(solution)/shard_map/ppermute | solution.py:520
  124.5 40.0 %collective-permute-done.14 = bf16[48,7680]{1,0:T(8,128)(2,1)S(1)} collective-permute-done((bf16[48,7680]{1,0:T(8,128)(2,1)}, bf16[48,7680]{1,0:T(8,128)(2,1)S(1)}, u32[]{:S(2)}, u32[]{:S(2)}) %collective-permute-start.14) | collective-permute-done | bytes 737312 | tf_op jit(solution)/shard_map/ppermute | solution.py:517
  168.1 18.4 %collective-permute-done.12.refs_14_ = bf16[4,48,2304]{2,1,0:T(8,128)(2,1)S(1)} collective-permute-done((bf16[4,48,2304]{2,1,0:T(8,128)(2,1)S(1)}, bf16[4,48,2304]{2,1,0:T(8,128)(2,1)S(1)}, u32[]{:S(2)}, u32[]{:S(2)}) %collective-permute-start.12) | collective-permute-done | bytes 884768 | tf_op jit(solution)/shard_map/ppermute | solution.py:520
  197.8 12.7 place_rows.2
  227.9 30.1 %collective-permute-done.17.refs_10_ = bf16[4,48,3840]{2,1,0:T(8,128)(2,1)} collective-permute-done((bf16[4,48,3840]{2,1,0:T(8,128)(2,1)S(1)}, bf16[4,48,3840]{2,1,0:T(8,128)(2,1)}, u32[]{:S(2)}, u32[]{:S(2)}) %collective-permute-start.17) | collective-permute-done | bytes 1474592 | tf_op jit(solution)/shard_map/ppermute | solution.py:520
  266.0 24.0 %collective-permute-done.29.refs_1_ = bf16[512,1024]{1,0:T(8,128)(2,1)S(1)} collective-permute-done((bf16[512,1024]{1,0:T(8,128)(2,1)S(1)}, bf16[512,1024]{1,0:T(8,128)(2,1)S(1)}, u32[]{:S(2)}, u32[]{:S(2)}) %collective-permute-start.29) | collective-permute-done | bytes 1048608 | tf_op jit(solution)/shard_map/ppermute | solution.py:517
  292.3 22.9 %collective-permute-done.34.refs_1_ = bf16[512,1024]{1,0:T(8,128)(2,1)} collective-permute-done((bf16[512,1024]{1,0:T(8,128)(2,1)}, bf16[512,1024]{1,0:T(8,128)(2,1)}, u32[]{:S(2)}, u32[]{:S(2)}) %collective-permute-start.34) | collective-permute-done | bytes 1048608 | tf_op jit(solution)/shard_map/ppermute | solution.py:517
  326.9 19.9 %collective-permute-done.38.refs_2_ = bf16[512,1024]{1,0:T(8,128)(2,1)} collective-permute-done((bf16[512,1024]{1,0:T(8,128)(2,1)}, bf16[512,1024]{1,0:T(8,128)(2,1)}, u32[]{:S(2)}, u32[]{:S(2)}) %collective-permute-start.38) | collective-permute-done | bytes 1048608 | tf_op jit(solution)/shard_map/ppermute | solution.py:517
  368.2 17.5 %place_rows.3 = bf16[1536,7680]{1,0:T(8,128)(2,1)} custom-call(s32[17]{0:T(128)S(1)} %stack.203.numbers_ref, bf16[4,48,3840]{2,1,0:T(8,128)(2,1)S(1)} %get-tuple-element.452.refs_0_, bf16[4,48,3840]{2,1,0:T(8,128)(2,1)S(1)} %collective-permute-done.40.refs_1_, bf16[4,48,3840]{2,1,0:T(8,128)(2,1)S(1)} %get-tuple-element.451.refs_2_, ...), custom_call_target="tpu_custom_call" | custom-call | bytes 47185920 | tf_op jit(solution)/shard_map/place_rows/pallas_call | solution.py:468
  395.1 33.8 %collective-permute-done.48.refs_1_ = bf16[128,3072]{1,0:T(8,128)(2,1)} collective-permute-done((bf16[128,3072]{1,0:T(8,128)(2,1)S(1)}, bf16[128,3072]{1,0:T(8,128)(2,1)}, u32[]{:S(2)}, u32[]{:S(2)}) %collective-permute-start.48) | collective-permute-done | bytes 786464 | tf_op jit(solution)/shard_map/ppermute | solution.py:517
  481.6 11.6 attend.7
  528.5 11.0 fusion.28
  554.0 10.6 fusion.35
  564.6 16.3 %collective-permute-done.55 = bf16[512,1536]{1,0:T(8,128)(2,1)} collective-permute-done((bf16[512,1536]{1,0:T(8,128)(2,1)S(1)}, bf16[512,1536]{1,0:T(8,128)(2,1)}, u32[]{:S(2)}, u32[]{:S(2)}) %collective-permute-start.55) | collective-permute-done | bytes 1572896 | tf_op jit(solution)/shard_map/ppermute | solution.py:520
  614.5 10.6 fusion.49
  643.3 18.7 %convolution_convert_fusion.1 = bf16[2240,1536]{1,0:T(8,128)(2,1)} fusion(bf16[2048,2240]{0,1:T(8,128)(2,1)S(1)} %pad_maximum_fusion, bf16[512,1536]{1,0:T(8,128)(2,1)} %copy-done.177, bf16[512,1536]{1,0:T(8,128)(2,1)} %copy-done.175, bf16[512,1536]{1,0:T(8,128)(2,1)S(1)} %copy-done.174, bf16[512,1536]{1,0:T(8,128)(2,1)S(1)} %copy-done.110), kind=kOutput, calls=%fused_computation.1 | convolution fusion | flops 14121467904 | bytes 22347776 | tf_op jit(solution)/shard_map/dot_general | solution.py:52
  673.9 19.8 %convolution_convert_fusion = bf16[1536,2240]{0,1:T(8,128)(2,1)} fusion(bf16[2048,1536]{1,0:T(8,128)(2,1)} %pad_maximum_fusion.1, bf16[512,2240]{0,1:T(8,128)(2,1)} %get-tuple-element.439, bf16[512,2240]{0,1:T(8,128)(2,1)} %get-tuple-element.441, bf16[512,2240]{0,1:T(8,128)(2,1)S(1)} %copy-done.182, bf16[512,2240]{0,1:T(8,128)(2,1)S(1)} %copy-done.180), kind=kOutput, calls=%fused_computation | convolution fusion | flops 14133002240 | bytes 22347776 | tf_op jit(solution)/shard_map/dot_general | solution.py:52
  753.3 17.7 %attend_back.4 = (f32[512,1536]{1,0:T(8,128)S(1)}, bf16[128,3072]{1,0:T(8,128)(2,1)S(1)}, bf16[128,3072]{1,0:T(8,128)(2,1)S(1)}, bf16[128,3072]{1,0:T(8,128)(2,1)S(1)}, bf16[128,3072]{1,0:T(8,128)(2,1)}) custom-call(bf16[512,1536]{1,0:T(8,128)(2,1)S(1)} %copy-done.18, bf16[512,1536]{1,0:T(8,128)(2,1)S(1)} %fusion.87.grad_ref, ...), custom_call_target="tpu_custom_call" | custom-call | flops 8053063680 | bytes 14155776 | tf_op jit(solution)/shard_map/attend_back/pallas_call | solution.py:410
  797.7 22.8 %collective-permute-done.66 = bf16[128,3072]{1,0:T(8,128)(2,1)S(1)} collective-permute-done((bf16[128,3072]{1,0:T(8,128)(2,1)S(1)}, bf16[128,3072]{1,0:T(8,128)(2,1)S(1)}, u32[]{:S(2)}, u32[]{:S(2)}) %collective-permute-start.66) | collective-permute-done | bytes 786464 | tf_op jit(solution)/shard_map/ppermute | solution.py:517
  830.1 15.8 %attend_back.7 = (f32[512,512]{1,0:T(8,128)S(1)}, bf16[512,1024]{1,0:T(8,128)(2,1)S(1)}, bf16[512,1024]{1,0:T(8,128)(2,1)S(1)}, bf16[512,1024]{1,0:T(8,128)(2,1)S(1)}, bf16[512,1024]{1,0:T(8,128)(2,1)S(1)}) custom-call(bf16[512,1536]{1,0:T(8,128)(2,1)S(1)} %copy-done.36, bf16[512,1536]{1,0:T(8,128)(2,1)S(1)} %fusion.84.grad_ref, ...), custom_call_target="tpu_custom_call" | custom-call | flops 10737418240 | bytes 11010048 | tf_op jit(solution)/shard_map/attend_back/pallas_call | solution.py:410
  860.0 15.7 %attend_back.5 = (f32[512,512]{1,0:T(8,128)S(1)}, bf16[512,1024]{1,0:T(8,128)(2,1)S(1)}, bf16[512,1024]{1,0:T(8,128)(2,1)S(1)}, bf16[512,1024]{1,0:T(8,128)(2,1)S(1)}, bf16[512,1024]{1,0:T(8,128)(2,1)S(1)}) custom-call(bf16[512,1536]{1,0:T(8,128)(2,1)S(1)} %copy-done.36, bf16[512,1536]{1,0:T(8,128)(2,1)S(1)} %fusion.84.grad_ref, ...), custom_call_target="tpu_custom_call" | custom-call | flops 10737418240 | bytes 11010048 | tf_op jit(solution)/shard_map/attend_back/pallas_call | solution.py:410
  904.6 16.1 %attend_back.6 = (f32[512,512]{1,0:T(8,128)S(1)}, bf16[512,1024]{1,0:T(8,128)(2,1)S(1)}, bf16[512,1024]{1,0:T(8,128)(2,1)S(1)}, bf16[512,1024]{1,0:T(8,128)(2,1)S(1)}, bf16[512,1024]{1,0:T(8,128)(2,1)S(1)}) custom-call(bf16[512,1536]{1,0:T(8,128)(2,1)S(1)} %copy-done.36, bf16[512,1536]{1,0:T(8,128)(2,1)S(1)} %copy-done.65, ...), custom_call_target="tpu_custom_call" | custom-call | flops 10737418240 | bytes 11010048 | tf_op jit(solution)/shard_map/attend_back/pallas_call | solution.py:410
  943.9 20.1 %collective-permute-done.80 = bf16[512,1024]{1,0:T(8,128)(2,1)S(1)} collective-permute-done((bf16[512,1024]{1,0:T(8,128)(2,1)}, bf16[512,1024]{1,0:T(8,128)(2,1)S(1)}, u32[]{:S(2)}, u32[]{:S(2)}) %collective-permute-start.80) | collective-permute-done | bytes 1048608 | tf_op jit(solution)/shard_map/ppermute | solution.py:517
  965.0 21.2 %collective-permute-done.83 = bf16[512,1024]{1,0:T(8,128)(2,1)} collective-permute-done((bf16[512,1024]{1,0:T(8,128)(2,1)}, bf16[512,1024]{1,0:T(8,128)(2,1)}, u32[]{:S(2)}, u32[]{:S(2)}) %collective-permute-start.83) | collective-permute-done | bytes 1048608 | tf_op jit(solution)/shard_map/ppermute | solution.py:517
  991.0 11.0 collective-permute-done.62
  1037.4 28.8 %collective-permute-done.77 = bf16[256,1536]{1,0:T(8,128)(2,1)S(1)} collective-permute-done((bf16[256,1536]{1,0:T(8,128)(2,1)S(1)}, bf16[256,1536]{1,0:T(8,128)(2,1)S(1)}, u32[]{:S(2)}, u32[]{:S(2)}) %collective-permute-start.77) | collective-permute-done | bytes 786464 | tf_op jit(solution)/shard_map/ppermute | solution.py:517
  1092.1 14.3 %collective-permute-done.90 = bf16[48,3072]{1,0:T(8,128)(2,1)S(1)} collective-permute-done((bf16[48,3072]{1,0:T(8,128)(2,1)S(1)}, bf16[48,3072]{1,0:T(8,128)(2,1)S(1)}, u32[]{:S(2)}, u32[]{:S(2)}) %collective-permute-start.90) | collective-permute-done | bytes 294944 | tf_op jit(solution)/shard_map/ppermute | solution.py:517
  1130.9 23.2 %collective-permute-done.93 = bf16[48,4608]{1,0:T(8,128)(2,1)S(1)} collective-permute-done((bf16[48,4608]{1,0:T(8,128)(2,1)}, bf16[48,4608]{1,0:T(8,128)(2,1)S(1)}, u32[]{:S(2)}, u32[]{:S(2)}) %collective-permute-start.93) | collective-permute-done | bytes 442400 | tf_op jit(solution)/shard_map/ppermute | solution.py:517
  1226.0 16.1 %collective-permute-done.105 = f32[12,1536]{1,0:T(8,128)S(1)} collective-permute-done((f32[12,1536]{1,0:T(8,128)S(1)}, f32[12,1536]{1,0:T(8,128)S(1)}, u32[]{:S(2)}, u32[]{:S(2)}) %collective-permute-start.105) | collective-permute-done | bytes 73760 | tf_op jit(solution)/shard_map/ppermute | solution.py:520
  1290.9 20.3 %collective-permute-done.108 = bf16[48,4608]{1,0:T(8,128)(2,1)} collective-permute-done((bf16[48,4608]{1,0:T(8,128)(2,1)}, bf16[48,4608]{1,0:T(8,128)(2,1)}, u32[]{:S(2)}, u32[]{:S(2)}) %collective-permute-start.108) | collective-permute-done | bytes 442400 | tf_op jit(solution)/shard_map/ppermute | solution.py:517
  (823 shorter events, 674.7 us)
Async XLA Ops:
  7.2 507.4 %all-gather.3.cloned.1.call-start = ((), (), s32[]{:S(2)}) async-start(), calls=%async_computation.2 | async-start | bytes 7962624 | tf_op jit(solution)/shard_map/all_gather | solution.py:765
  19.0 56.7 %collective-permute-start.1 = (bf16[48,4736]{1,0:T(8,128)(2,1)S(1)}, bf16[48,4736]{1,0:T(8,128)(2,1)}, u32[]{:S(2)}, u32[]{:S(2)}) collective-permute-start(bf16[48,4736]{1,0:T(8,128)(2,1)S(1)} %concatenate.123), channel_id=1, source_target_pairs={{0,4},{1,5},{2,6},{3,7},{4,0},{5,1},{6,2},{7,3},{8,12},{9,13},{10,... | collective-permute-start | bytes 1363976 | tf_op jit(solution)/shard_map/ppermute | solution.py:517
  19.0 59.2 %collective-permute-start = (bf16[48,4736]{1,0:T(8,128)(2,1)S(1)}, bf16[48,4736]{1,0:T(8,128)(2,1)}, u32[]{:S(2)}, u32[]{:S(2)}) collective-permute-start(bf16[48,4736]{1,0:T(8,128)(2,1)S(1)} %concatenate.123), channel_id=1, source_target_pairs={{0,2},{1,3},{2,0},{3,1},{4,6},{5,7},{6,4},{7,5},{8,10},{9,11},{10,... | collective-permute-start | bytes 1363976 | tf_op jit(solution)/shard_map/ppermute | solution.py:517
  22.0 69.5 %collective-permute-start.3 = (bf16[256,1536]{1,0:T(8,128)(2,1)}, bf16[256,1536]{1,0:T(8,128)(2,1)S(1)}, u32[]{:S(2)}, u32[]{:S(2)}) collective-permute-start(bf16[256,1536]{1,0:T(8,128)(2,1)} %get-tuple-element.488), channel_id=1, source_target_pairs={{0,4},{1,5},{2,6},{3,7},{4,0},{5,1},{6,2},{7,3},{8,12},{9,13},{10,... | collective-permute-start | bytes 2359304 | tf_op jit(solution)/shard_map/ppermute | solution.py:517
  25.5 67.3 %collective-permute-start.4 = (bf16[48,2240]{1,0:T(8,128)(2,1)}, bf16[48,2240]{1,0:T(8,128)(2,1)}, u32[]{:S(2)}, u32[]{:S(2)}) collective-permute-start(bf16[48,2240]{1,0:T(8,128)(2,1)} %get-tuple-element.513), channel_id=1, source_target_pairs={{0,8},{8,0},{16,24},{24,16},{1,9},{9,1},{17,25},{25,17},{2,10},{10... | collective-permute-start | bytes 645128 | tf_op jit(solution)/shard_map/ppermute | solution.py:520
  31.7 61.1 %collective-permute-start.5 = (bf16[48,2240]{1,0:T(8,128)(2,1)}, bf16[48,2240]{1,0:T(8,128)(2,1)S(1)}, u32[]{:S(2)}, u32[]{:S(2)}) collective-permute-start(bf16[48,2240]{1,0:T(8,128)(2,1)} %get-tuple-element.515), channel_id=1, source_target_pairs={{0,16},{8,24},{16,0},{24,8},{1,17},{9,25},{17,1},{25,9},{2,18},{10... | collective-permute-start | bytes 645128 | tf_op jit(solution)/shard_map/ppermute | solution.py:520
  99.5 66.6 %collective-permute-start.7 = (bf16[4,48,2432]{2,1,0:T(8,128)(2,1)S(1)}, bf16[4,48,2432]{2,1,0:T(8,128)(2,1)}, u32[]{:S(2)}, u32[]{:S(2)}) collective-permute-start(bf16[4,48,2432]{2,1,0:T(8,128)(2,1)S(1)} %slice.207.refs_0_), channel_id=1, source_target_pairs={{0,16},{8,24},{16,0},{24,8},{1,17},{9,25},{17,1},{25,9},{2,18},{10... | collective-permute-start | bytes 2801672 | tf_op jit(solution)/shard_map/ppermute | solution.py:520
  100.0 66.0 %collective-permute-start.11 = (bf16[4,48,2304]{2,1,0:T(8,128)(2,1)S(1)}, bf16[4,48,2304]{2,1,0:T(8,128)(2,1)}, u32[]{:S(2)}, u32[]{:S(2)}) collective-permute-start(bf16[4,48,2304]{2,1,0:T(8,128)(2,1)S(1)} %slice.208.refs_2_), channel_id=1, source_target_pairs={{0,8},{8,0},{16,24},{24,16},{1,9},{9,1},{17,25},{25,17},{2,10},{10... | collective-permute-start | bytes 2654216 | tf_op jit(solution)/shard_map/ppermute | solution.py:520
  117.2 47.3 %collective-permute-start.14 = (bf16[48,7680]{1,0:T(8,128)(2,1)}, bf16[48,7680]{1,0:T(8,128)(2,1)S(1)}, u32[]{:S(2)}, u32[]{:S(2)}) collective-permute-start(bf16[48,7680]{1,0:T(8,128)(2,1)} %copy-done.118), channel_id=1, source_target_pairs={{0,4},{1,5},{2,6},{3,7},{4,0},{5,1},{6,2},{7,3},{8,12},{9,13},{10,... | collective-permute-start | bytes 2211848 | tf_op jit(solution)/shard_map/ppermute | solution.py:517
  124.5 65.4 %collective-permute-start.18 = (bf16[4,48,2432]{2,1,0:T(8,128)(2,1)S(1)}, bf16[4,48,2432]{2,1,0:T(8,128)(2,1)S(1)}, u32[]{:S(2)}, u32[]{:S(2)}) collective-permute-start(bf16[4,48,2432]{2,1,0:T(8,128)(2,1)S(1)} %slice.207.refs_0_), channel_id=1, source_target_pairs={{0,1},{1,0},{2,3},{3,2},{4,5},{5,4},{6,7},{7,6},{8,9},{9,8},{10,11... | collective-permute-start | bytes 2801672 | tf_op jit(solution)/shard_map/ppermute | solution.py:517
  192.0 73.7 %collective-permute-start.27 = (bf16[4,48,3840]{2,1,0:T(8,128)(2,1)S(1)}, bf16[4,48,3840]{2,1,0:T(8,128)(2,1)}, u32[]{:S(2)}, u32[]{:S(2)}) collective-permute-start(bf16[4,48,3840]{2,1,0:T(8,128)(2,1)S(1)} %get-tuple-element.452.refs_0_), channel_id=1, source_target_pairs={{0,16},{8,24},{16,0},{24,8},{1,17},{9,25},{17,1},{25,9},{2,18},{10... | collective-permute-start | bytes 4423688 | tf_op jit(solution)/shard_map/ppermute | solution.py:520
  195.7 62.3 %collective-permute-start.17 = (bf16[4,48,3840]{2,1,0:T(8,128)(2,1)S(1)}, bf16[4,48,3840]{2,1,0:T(8,128)(2,1)}, u32[]{:S(2)}, u32[]{:S(2)}) collective-permute-start(bf16[4,48,3840]{2,1,0:T(8,128)(2,1)S(1)} %get-tuple-element.451.refs_2_), channel_id=1, source_target_pairs={{0,16},{8,24},{16,0},{24,8},{1,17},{9,25},{17,1},{25,9},{2,18},{10... | collective-permute-start | bytes 4423688 | tf_op jit(solution)/shard_map/ppermute | solution.py:520
  197.2 68.5 %collective-permute-start.28 = (bf16[4,48,3840]{2,1,0:T(8,128)(2,1)S(1)}, bf16[4,48,3840]{2,1,0:T(8,128)(2,1)}, u32[]{:S(2)}, u32[]{:S(2)}) collective-permute-start(bf16[4,48,3840]{2,1,0:T(8,128)(2,1)S(1)} %get-tuple-element.451.refs_2_), channel_id=1, source_target_pairs={{0,8},{8,0},{16,24},{24,16},{1,9},{9,1},{17,25},{25,17},{2,10},{10... | collective-permute-start | bytes 4423688 | tf_op jit(solution)/shard_map/ppermute | solution.py:520
  346.8 181.7 %all-gather.5.cloned.1.call-start = ((), (), s32[]{:S(2)}) async-start(), calls=%async_computation.3 | async-start | bytes 7741440 | tf_op jit(solution)/shard_map/all_gather | solution.py:777
  429.0 761.2 %reduce-scatter.5.cloned.1.call-start = ((), (), s32[]{:S(2)}) async-start(), calls=%async_computation.5 | async-start | bytes 7741440 | tf_op jit(solution)/shard_map/reduce_scatter | solution.py:816
  431.9 61.3 %collective-permute-start.51 = (bf16[512,1536]{1,0:T(8,128)(2,1)S(1)}, bf16[512,1536]{1,0:T(8,128)(2,1)S(1)}, u32[]{:S(2)}, u32[]{:S(2)}) collective-permute-start(bf16[512,1536]{1,0:T(8,128)(2,1)S(1)} %fusion.82), channel_id=1, source_target_pairs={{0,8},{8,0},{16,24},{24,16},{1,9},{9,1},{17,25},{25,17},{2,10},{10... | collective-permute-start | bytes 4718600 | tf_op jit(solution)/shard_map/ppermute | solution.py:520
  433.4 69.8 %collective-permute-start.52 = (bf16[512,1536]{1,0:T(8,128)(2,1)S(1)}, bf16[512,1536]{1,0:T(8,128)(2,1)S(1)}, u32[]{:S(2)}, u32[]{:S(2)}) collective-permute-start(bf16[512,1536]{1,0:T(8,128)(2,1)S(1)} %fusion.82), channel_id=1, source_target_pairs={{0,16},{8,24},{16,0},{24,8},{1,17},{9,25},{17,1},{25,9},{2,18},{10... | collective-permute-start | bytes 4718600 | tf_op jit(solution)/shard_map/ppermute | solution.py:520
  434.9 68.3 %collective-permute-start.53 = (bf16[512,1536]{1,0:T(8,128)(2,1)S(1)}, bf16[512,1536]{1,0:T(8,128)(2,1)S(1)}, u32[]{:S(2)}, u32[]{:S(2)}) collective-permute-start(bf16[512,1536]{1,0:T(8,128)(2,1)S(1)} %fusion.82), channel_id=1, source_target_pairs={{0,24},{8,16},{16,8},{24,0},{1,25},{9,17},{17,9},{25,1},{2,26},{10... | collective-permute-start | bytes 4718600 | tf_op jit(solution)/shard_map/ppermute | solution.py:520
  511.7 69.2 %collective-permute-start.55 = (bf16[512,1536]{1,0:T(8,128)(2,1)S(1)}, bf16[512,1536]{1,0:T(8,128)(2,1)}, u32[]{:S(2)}, u32[]{:S(2)}) collective-permute-start(bf16[512,1536]{1,0:T(8,128)(2,1)S(1)} %add_convert_fusion.9), channel_id=1, source_target_pairs={{0,16},{8,24},{16,0},{24,8},{1,17},{9,25},{17,1},{25,9},{2,18},{10... | collective-permute-start | bytes 4718600 | tf_op jit(solution)/shard_map/ppermute | solution.py:520
  513.1 86.5 %collective-permute-start.56 = (bf16[512,1536]{1,0:T(8,128)(2,1)S(1)}, bf16[512,1536]{1,0:T(8,128)(2,1)}, u32[]{:S(2)}, u32[]{:S(2)}) collective-permute-start(bf16[512,1536]{1,0:T(8,128)(2,1)S(1)} %add_convert_fusion.9), channel_id=1, source_target_pairs={{0,24},{8,16},{16,8},{24,0},{1,25},{9,17},{17,9},{25,1},{2,26},{10... | collective-permute-start | bytes 4718600 | tf_op jit(solution)/shard_map/ppermute | solution.py:520
  635.7 74.2 %collective-permute-start.57 = (bf16[512,1536]{1,0:T(8,128)(2,1)}, bf16[512,1536]{1,0:T(8,128)(2,1)}, u32[]{:S(2)}, u32[]{:S(2)}) collective-permute-start(bf16[512,1536]{1,0:T(8,128)(2,1)} %convolution_convert_fusion.14), channel_id=1, source_target_pairs={{0,8},{8,0},{16,24},{24,16},{1,9},{9,1},{17,25},{25,17},{2,10},{10... | collective-permute-start | bytes 4718600 | tf_op jit(solution)/shard_map/ppermute | solution.py:520
  641.4 68.4 %collective-permute-start.58 = (bf16[512,1536]{1,0:T(8,128)(2,1)}, bf16[512,1536]{1,0:T(8,128)(2,1)}, u32[]{:S(2)}, u32[]{:S(2)}) collective-permute-start(bf16[512,1536]{1,0:T(8,128)(2,1)} %convolution_convert_fusion.13), channel_id=1, source_target_pairs={{0,16},{8,24},{16,0},{24,8},{1,17},{9,25},{17,1},{25,9},{2,18},{10... | collective-permute-start | bytes 4718600 | tf_op jit(solution)/shard_map/ppermute | solution.py:520
  662.1 601.5 %reduce-scatter.3.cloned.1.call-start = ((), (), s32[]{:S(2)}) async-start(), calls=%async_computation.4 | async-start | bytes 7962624 | tf_op jit(solution)/shard_map/reduce_scatter | solution.py:817
  722.4 198.3 %collective-permute-start.70 = (bf16[512,1536]{1,0:T(8,128)(2,1)}, bf16[512,1536]{1,0:T(8,128)(2,1)}, u32[]{:S(2)}, u32[]{:S(2)}) collective-permute-start(bf16[512,1536]{1,0:T(8,128)(2,1)} %convolution_convert_fusion.11), channel_id=1, source_target_pairs={{0,8},{8,0},{16,24},{24,16},{1,9},{9,1},{17,25},{25,17},{2,10},{10... | collective-permute-start | bytes 4718600 | tf_op jit(solution)/shard_map/ppermute | solution.py:520
  748.1 73.8 %collective-permute-start.60 = (bf16[2,2,4,48,1536]{4,3,2,1,0:T(8,128)(2,1)}, bf16[2,2,4,48,1536]{4,3,2,1,0:T(8,128)(2,1)}, u32[]{:S(2)}, u32[]{:S(2)}) collective-permute-start(bf16[2,2,4,48,1536]{4,3,2,1,0:T(8,128)(2,1)} %get-tuple-element.437), channel_id=1, source_target_pairs={{0,1},{1,0},{2,3},{3,2},{4,5},{5,4},{6,7},{7,6},{8,9},{9,8},{10,11... | collective-permute-start | bytes 7077896 | tf_op jit(solution)/shard_map/ppermute | solution.py:517
  796.0 128.2 %collective-permute-start.71 = (bf16[512,1536]{1,0:T(8,128)(2,1)}, bf16[512,1536]{1,0:T(8,128)(2,1)}, u32[]{:S(2)}, u32[]{:S(2)}) collective-permute-start(bf16[512,1536]{1,0:T(8,128)(2,1)} %convolution_convert_fusion.10), channel_id=1, source_target_pairs={{0,16},{8,24},{16,0},{24,8},{1,17},{9,25},{17,1},{25,9},{2,18},{10... | collective-permute-start | bytes 4718600 | tf_op jit(solution)/shard_map/ppermute | solution.py:520
  893.4 120.5 %collective-permute-start.67 = (bf16[2,2,4,48,2304]{4,3,2,1,0:T(8,128)(2,1)}, bf16[2,2,4,48,2304]{4,3,2,1,0:T(8,128)(2,1)}, u32[]{:S(2)}, u32[]{:S(2)}) collective-permute-start(bf16[2,2,4,48,2304]{4,3,2,1,0:T(8,128)(2,1)} %pad_maximum_fusion.3), channel_id=1, source_target_pairs={{0,1},{1,0},{2,3},{3,2},{4,5},{5,4},{6,7},{7,6},{8,9},{9,8},{10,11... | collective-permute-start | bytes 10616840 | tf_op jit(solution)/shard_map/ppermute | solution.py:517
  899.4 114.4 %collective-permute-start.68 = (bf16[2,2,4,48,2304]{4,3,2,1,0:T(8,128)(2,1)}, bf16[2,2,4,48,2304]{4,3,2,1,0:T(8,128)(2,1)}, u32[]{:S(2)}, u32[]{:S(2)}) collective-permute-start(bf16[2,2,4,48,2304]{4,3,2,1,0:T(8,128)(2,1)} %pad_maximum_fusion.5), channel_id=1, source_target_pairs={{0,1},{1,0},{2,3},{3,2},{4,5},{5,4},{6,7},{7,6},{8,9},{9,8},{10,11... | collective-permute-start | bytes 10616840 | tf_op jit(solution)/shard_map/ppermute | solution.py:517
  937.9 48.3 %collective-permute-start.83 = (bf16[512,1024]{1,0:T(8,128)(2,1)}, bf16[512,1024]{1,0:T(8,128)(2,1)}, u32[]{:S(2)}, u32[]{:S(2)}) collective-permute-start(bf16[512,1024]{1,0:T(8,128)(2,1)} %add_convert_fusion.14), channel_id=1, source_target_pairs={{0,2},{1,3},{2,0},{3,1},{4,6},{5,7},{6,4},{7,5},{8,10},{9,11},{10,... | collective-permute-start | bytes 3145736 | tf_op jit(solution)/shard_map/ppermute | solution.py:517
  940.1 50.7 %collective-permute-start.72 = (bf16[512,1536]{1,0:T(8,128)(2,1)}, bf16[512,1536]{1,0:T(8,128)(2,1)S(1)}, u32[]{:S(2)}, u32[]{:S(2)}) collective-permute-start(bf16[512,1536]{1,0:T(8,128)(2,1)} %convolution_convert_fusion.9), channel_id=1, source_target_pairs={{0,24},{8,16},{16,8},{24,0},{1,25},{9,17},{17,9},{25,1},{2,26},{10... | collective-permute-start | bytes 4718600 | tf_op jit(solution)/shard_map/ppermute | solution.py:520
  1019.3 56.8 %collective-permute-start.75 = (bf16[2,4,48,2304]{3,2,1,0:T(8,128)(2,1)}, bf16[2,4,48,2304]{3,2,1,0:T(8,128)(2,1)}, u32[]{:S(2)}, u32[]{:S(2)}) collective-permute-start(bf16[2,4,48,2304]{3,2,1,0:T(8,128)(2,1)} %get-tuple-element.449), channel_id=1, source_target_pairs={{0,8},{8,0},{16,24},{24,16},{1,9},{9,1},{17,25},{25,17},{2,10},{10... | collective-permute-start | bytes 5308424 | tf_op jit(solution)/shard_map/ppermute | solution.py:520
  1023.8 52.3 %collective-permute-start.76 = (bf16[2,4,48,2304]{3,2,1,0:T(8,128)(2,1)}, bf16[2,4,48,2304]{3,2,1,0:T(8,128)(2,1)S(1)}, u32[]{:S(2)}, u32[]{:S(2)}) collective-permute-start(bf16[2,4,48,2304]{3,2,1,0:T(8,128)(2,1)} %get-tuple-element.447), channel_id=1, source_target_pairs={{0,16},{8,24},{16,0},{24,8},{1,17},{9,25},{17,1},{25,9},{2,18},{10... | collective-permute-start | bytes 5308424 | tf_op jit(solution)/shard_map/ppermute | solution.py:520
  (276 other events, 5894.9 us)
Sparse Core Ops, SparseCore 0:
  346.9 77.8 all-gather.2
  429.1 75.8 all-gather.4
  662.2 75.6 reduce-scatter.4
  787.9 89.4 reduce-scatter.2

commit v3 on v2

--- a/solution.py
+++ b/solution.py
@@ -400,10 +400,11 @@
             weights.append(weight)
             value_grads.append(value_grad)
         summed = jnp.zeros((HEAD_DIM, rows), F32)
-        for ref, out, weight, value_grad in zip(refs[:count], refs[count + 1 :], weights, value_grads):
+        out = refs[count + 1]
+        for at, (ref, weight, value_grad) in enumerate(zip(refs[:count], weights, value_grads)):
             score_grad = (weight * (value_grad - delta)).astype(BF)
-            out[:, :HEAD_DIM] = (dot_nn(score_grad, query_head) * SCALE).astype(BF)
-            out[:, HEAD_DIM:] = dot_nn(weight.astype(BF), grad_head).astype(BF)
+            out[at, :, :HEAD_DIM] = (dot_nn(score_grad, query_head) * SCALE).astype(BF)
+            out[at, :, HEAD_DIM:] = dot_nn(weight.astype(BF), grad_head).astype(BF)
             summed += dot_tn(ref[:, :HEAD_DIM], score_grad)
         query_grad[...] = (summed * SCALE).T
 
@@ -416,10 +417,14 @@
             pl.BlockSpec((1, 1, rows), lambda head: (head, 0, 0)),
         ]
         + [pl.BlockSpec((keys, 2 * HEAD_DIM), lambda head: (0, head))] * count,
-        out_specs=[pl.BlockSpec((rows, HEAD_DIM), lambda head: (0, head))]
-        + [pl.BlockSpec((keys, 2 * HEAD_DIM), lambda head: (0, head))] * count,
-        out_shape=[jax.ShapeDtypeStruct((rows, heads * HEAD_DIM), F32)]
-        + [jax.ShapeDtypeStruct((keys, heads * 2 * HEAD_DIM), BF)] * count,
+        out_specs=[
+            pl.BlockSpec((rows, HEAD_DIM), lambda head: (0, head)),
+            pl.BlockSpec((count, keys, 2 * HEAD_DIM), lambda head: (0, 0, head)),
+        ],
+        out_shape=[
+            jax.ShapeDtypeStruct((rows, heads * HEAD_DIM), F32),
+            jax.ShapeDtypeStruct((count, keys, heads * 2 * HEAD_DIM), BF),
+        ],
         compiler_params=params(40),
         cost_estimate=pl.CostEstimate(
             flops=heads * rows * keys * count * HEAD_DIM * 10 * 2,
@@ -537,14 +542,18 @@
             held.update({at ^ bit: self.over_seq(one, bit) for at, one in list(held.items())})
         return held
 
-    def group_scatter(self, held):
-        held = dict(held)
+    def chunks(self, held):
+        order = [0]
+        for bit in reversed(self.group_bits):
+            order = order + [at ^ bit for at in order]
+        return [held[at] for at in order]
+
+    def group_scatter(self, parts):
         for bit in self.group_bits:
-            for at in sorted(held):
-                if at & bit:
-                    sent = self.over_seq(held.pop(at).astype(BF), bit)
-                    held[at ^ bit] = held[at ^ bit].astype(F32) + sent.astype(F32)
-        return held[0]
+            half = parts.shape[0] // 2
+            sent = self.over_seq(parts[half:].astype(BF), bit)
+            parts = parts[:half].astype(F32) + sent.astype(F32)
+        return parts[0]
 
 
     def gather_columns(self, shard):
@@ -770,7 +779,7 @@
     )
     self_outs, self_logs = [], []
     for group in range(plan.groups):
-        out, logs = attend(queries, list(gathered[group].values()), group * per_group, per_group)
+        out, logs = attend(queries, plan.chunks(gathered[group]), group * per_group, per_group)
         self_outs.append(out)
         self_logs.append(logs)
     down_shard = after(downmatrix, cross_gathered[plan.group_bits[-1]])
@@ -785,7 +794,7 @@
     cross_in = (layer_norm(hidden_one) * gain_norm + bias_norm).astype(BF)
     crossq_raw = dot_nn(cross_in, whole_crossquery)
     cross_queries = query_post(crossq_raw, gain_crossq)
-    crossed, cross_logs = attend(cross_queries, list(cross_gathered.values()), 0, HEADS)
+    crossed, cross_logs = attend(cross_queries, plan.chunks(cross_gathered), 0, HEADS)
     crossed, down_grads = together(crossed, down_grads)
     hidden_two = hidden_one + dot_nn(crossed, whole_crossout)
 
@@ -828,10 +837,10 @@
     cross_grad = two_grad.astype(BF)
     crossed_grad = dot_nt(cross_grad, whole_crossout, BF)
     crossout_term = dot_tn(crossed, cross_grad, BF)
-    crossq_grad, *cross_parts = attend_back(
-        cross_queries, list(cross_gathered.values()), crossed_grad, cross_logs, 0, HEADS
-    )
-    cross_own = plan.group_scatter(dict(zip(cross_gathered, cross_parts)))
+    crossq_grad, cross_parts = attend_back(
+        cross_queries, plan.chunks(cross_gathered), crossed_grad, cross_logs, 0, HEADS
+    )
+    cross_own = plan.group_scatter(cross_parts)
     crossq_low, crossq_gaingrad = query_back(crossq_grad, crossq_raw, gain_crossq)
     cross_sums = [plan.scatter_core(crossout_term), plan.scatter_core(dot_tn(cross_in, crossq_low, BF))]
     crossin_grad = dot_nt(crossq_low, whole_crossquery)
@@ -845,9 +854,13 @@
     attended_grad = dot_nt(branch_grad, whole_selfout, BF)
     query_grads, keyvalue_grads = [], []
     for group in range(plan.groups):
-        query_grad, *parts = attend_back(
+        if group:
+            if group < len(xy):
+                cross_sums = plan.scatter_pair(cross_sums, (xy, yx), group)
+            attended_grad, cross_sums = together(attended_grad, cross_sums)
+        query_grad, parts = attend_back(
             queries,
-            list(gathered[group].values()),
+            plan.chunks(gathered[group]),
             attended_grad,
             self_logs[group],
             group * per_group,
@@ -865,35 +878,31 @@
             text_sums = [plan.scatter_core(*pair) for pair in pieces]
             context_gradient = plan.unshift(dot_nt(text_low, whole_crosstext, BF))
         if group == min(1, plan.groups - 1):
-            query_grad, cross_sums, text_sums, context_gradient, down_sent = together(
-                query_grad, cross_sums, text_sums, context_gradient, down_sent
-            )
-            down_values = down_all[0] + sum(one.astype(F32) for one in down_sent)
-            layer_output = plan.unshift((hidden_two + down_values * gate_m).astype(BF))
-            gate_m_grad = jnp.sum(out_grad * down_values, axis=0)
-            for number in range(1, len(xy)):
-                cross_sums = plan.scatter_pair(cross_sums, (xy, yx), number)
+            query_grad, text_sums, context_gradient = together(query_grad, text_sums, context_gradient)
             text_sums = plan.scatter_pair(text_sums, (xy, yx), 0)
         if group == plan.groups - 1:
-            query_grad, cross_sums, text_sums, layer_output = together(
-                query_grad, cross_sums, text_sums, layer_output
-            )
-            for number in range(1, len(xy)):
-                text_sums = plan.scatter_pair(text_sums, (xy, yx), number)
+            for number in range(plan.groups, len(xy)):
+                cross_sums = plan.scatter_pair(cross_sums, (xy, yx), number)
+            query_grad, cross_sums, up_term = together(query_grad, cross_sums, up_term)
             crossout_gradient, crossquery_gradient = plan.scatter_pair_last(cross_sums)
+            up_pieces = [plan.pick(up_term, plan.dp ^ j, 0) for j in range(dp_n)]
+            up_pieces = [plan.over_dp(one, j) if j else one for j, one in enumerate(up_pieces)]
         query_grads.append(query_grad)
-        keyvalue_grads.append(plan.group_scatter(dict(zip(gathered[group], parts))))
+        keyvalue_grads.append(plan.group_scatter(parts))
 
     query_low, query_gaingrad = self_query_back(query_grads, self_raw, gain_query, tables)
-    query_low, text_sums, crossout_gradient, crossquery_gradient = together(
-        query_low, text_sums, crossout_gradient, crossquery_gradient
-    )
-    left, right = plan.scatter_pair_last(text_sums)
     query_term = dot_tn(attn_in, query_low, BF)
     attn_grad = dot_nt(query_low, whole_self[:, :width])
-    keyvalue_grads, attn_grad, query_term = together(keyvalue_grads, attn_grad, query_term)
+    keyvalue_grads, attn_grad, query_term, text_sums, down_sent, up_pieces = together(
+        keyvalue_grads, attn_grad, query_term, text_sums, down_sent, up_pieces
+    )
+    down_values = down_all[0] + sum(one.astype(F32) for one in down_sent)
+    layer_low = (hidden_two + down_values * gate_m).astype(BF)
+    gate_m_grad = jnp.sum(out_grad * down_values, axis=0)
+    for number in range(1, len(xy)):
+        text_sums = plan.scatter_pair(text_sums, (xy, yx), number)
+
     keyvalue_low, key_gaingrad = self_keyvalue_back(keyvalue_grads, self_raw, gain_key, tables)
-    keyvalue_low, left, right = together(keyvalue_low, left, right)
     key_middle = middle - width
     left_term = dot_tn(attn_in, keyvalue_low[:, :key_middle], BF)
     right_term = dot_tn(attn_in, keyvalue_low[:, key_middle:], BF)
@@ -903,9 +912,10 @@
     ]
     kept_low, _ = together(keyvalue_low, (left_term, right_term))
     attn_grad = attn_grad + dot_nt(kept_low, whole_self[:, width:])
-    attn_grad, self_sums = together(attn_grad, self_sums)
-    crosskey_gradient, crossvalue_gradient = left[:, :width], right[:, :width]
-    selfout_gradient = jnp.concatenate([left[:, width:], right[:, width:]], axis=1)
+    attn_grad, self_sums, layer_low, crossout_gradient = together(
+        attn_grad, self_sums, layer_low, crossout_gradient
+    )
+    layer_output = plan.unshift(layer_low)
     self_sums = plan.scatter_pair(self_sums, (xy, yx), 0)
     shift_a_grad = jnp.sum(attn_grad, axis=0)
     scale_a_grad = jnp.sum(attn_grad * normed_a, axis=0)
@@ -927,15 +937,24 @@
     for bit in plan.group_bits:
         sums = sums + plan.over_seq(sums, bit)
     other_sums = plan.over_seq(sums, plan.half)
-    latents_low, other_sums = together(latents_low, other_sums)
+    latents_low, other_sums, layer_output, text_sums = together(
+        latents_low, other_sums, layer_output, text_sums
+    )
     latents_gradient = plan.unshift(latents_low)
     for number in range(1, len(xy)):
         self_sums = plan.scatter_pair(self_sums, (xy, yx), number)
     self_sums, latents_gradient = together(self_sums, latents_gradient)
     latents_gradient = latents_gradient.astype(F32)
-    self_gradients = jnp.concatenate(plan.scatter_pair_last(together(*self_sums)), axis=1)
-    up_pieces = [plan.pick(up_term, plan.dp ^ j, 0) for j in range(dp_n)]
-    up_pieces = [plan.over_dp(one, j) if j else one for j, one in enumerate(up_pieces)]
+    left, right = plan.scatter_pair_last(
+        [
+            tuple(jnp.concatenate(side, axis=-1) for side in zip(*two))
+            for two in zip(self_sums, text_sums)
+        ]
+    )
+    self_gradients = jnp.concatenate([left[:, :middle], right[:, :middle]], axis=1)
+    left, right = left[:, middle:], right[:, middle:]
+    crosskey_gradient, crossvalue_gradient = left[:, :width], right[:, :width]
+    selfout_gradient = jnp.concatenate([left[:, width:], right[:, width:]], axis=1)
     upmatrix_gradient = jnp.concatenate(plan.xor_order(up_pieces, plan.dp), axis=1).astype(F32)
     modulation_gradient = jnp.where(
         plan.top == 0, jnp.stack([sums[:6], other_sums[:6]]), jnp.stack([other_sums[:6], sums[:6]])

time: 1330 us -> 1300 us (0.977)
  waiting for transfers between devices: 554 us -> 519 us
    ppermute x69 -> x62, waiting for transfers between devices: 394 us -> 367 us  [over_seq(): lax.ppermute(value, 'seq', [(i, i ^ offset) for i in range(self.seq_n)])]
    ppermute x69 -> x62, starting transfers between devices: 46.4 us -> 35.7 us  [over_seq(): lax.ppermute(value, 'seq', [(i, i ^ offset) for i in range(self.seq_n)])]
    unnamed x391 -> x385, local copies, waits for them, and re-layouts: 28.6 us -> 35.6 us
  transfers between devices with their start and end apart: 117 -> 110, of which waited for: 47 -> 41; matrix products, arithmetic and copies ran while one was open for 33% -> 34% of each run, Pallas kernels for 11% -> 12%
where the time goes in v3:
time: 1300 us; the launch traced here: 1290 us
  waiting for transfers between devices  519 us (40%)
  matrix products  259 us (20%)
  Pallas kernels  151 us (12%)
  other arithmetic  132 us (10%)
  local copies, waits for them, and re-layouts  127 us (10%)
  starting transfers between devices  88.4 us (7%)
  between operations  16.9 us (1%)
    ppermute x62, waiting for transfers between devices, over_seq(): lax.ppermute(value, 'seq', [(i, i ^ offset) for i in range(self.seq_n)])  367 us
    ppermute x44, waiting for transfers between devices, over_dp(): lax.ppermute(value, 'dp', [(i, i ^ offset) for i in range(self.dp_n)])  152 us
    dot_general x13, matrix products, dot_nn(): lax.dot_general(left, right, (((1,), (0,)), ((), ())), preferred_element_...  97.6 us
    dot_general x14, matrix products, dot_nt(): lax.dot_general(left, right, (((1,), (1,)), ((), ())), preferred_element_...  95.5 us
    dot_general x9, matrix products, dot_tn(): lax.dot_general(left, right, (((0,), (0,)), ((), ())), preferred_element_...  66.3 us
    pallas_call x4, Pallas kernels, attend_back(): pl.pallas_call(kernel, grid=(heads,), in_specs=[pl.BlockSpec((rows, HEAD_...  64.9 us
    ppermute x44, starting transfers between devices, over_dp(): lax.ppermute(value, 'dp', [(i, i ^ offset) for i in range(self.dp_n)])  52.2 us
    pallas_call x4, Pallas kernels, attend(): pl.pallas_call(kernel, grid=(heads,), in_specs=[pl.BlockSpec((rows, HEAD_...  39.5 us
  transfers between devices with their start and end apart: 110, of which 41 were waited for; matrix products, arithmetic and copies ran while one was open for 34% of the time, Pallas kernels for 12%

profile of v3, /device:TPU:0, one launch (start us, length us, event | category | flops | bytes accessed | tf_op | source)
XLA Modules:
  0.0 1292.7 jit_solution(2776956221343557746)
XLA Ops:
  33.3 42.5 %collective-permute-done.1 = bf16[48,4736]{1,0:T(8,128)(2,1)} collective-permute-done((bf16[48,4736]{1,0:T(8,128)(2,1)S(1)}, bf16[48,4736]{1,0:T(8,128)(2,1)}, u32[]{:S(2)}, u32[]{:S(2)}) %collective-permute-start.1) | collective-permute-done | bytes 454688 | tf_op jit(solution)/shard_map/ppermute | solution.py:522
  79.6 11.9 collective-permute-done.3
  103.8 13.3 %collective-permute-done.9.refs_10_ = bf16[4,48,2304]{2,1,0:T(8,128)(2,1)S(1)} collective-permute-done((bf16[4,48,2304]{2,1,0:T(8,128)(2,1)S(1)}, bf16[4,48,2304]{2,1,0:T(8,128)(2,1)S(1)}, u32[]{:S(2)}, u32[]{:S(2)}) %collective-permute-start.9) | collective-permute-done | bytes 884768 | tf_op jit(solution)/shard_map/ppermute | solution.py:525
  124.5 39.9 %collective-permute-done.14 = bf16[48,7680]{1,0:T(8,128)(2,1)S(1)} collective-permute-done((bf16[48,7680]{1,0:T(8,128)(2,1)}, bf16[48,7680]{1,0:T(8,128)(2,1)S(1)}, u32[]{:S(2)}, u32[]{:S(2)}) %collective-permute-start.14) | collective-permute-done | bytes 737312 | tf_op jit(solution)/shard_map/ppermute | solution.py:522
  168.1 18.4 %collective-permute-done.12.refs_14_ = bf16[4,48,2304]{2,1,0:T(8,128)(2,1)S(1)} collective-permute-done((bf16[4,48,2304]{2,1,0:T(8,128)(2,1)S(1)}, bf16[4,48,2304]{2,1,0:T(8,128)(2,1)S(1)}, u32[]{:S(2)}, u32[]{:S(2)}) %collective-permute-start.12) | collective-permute-done | bytes 884768 | tf_op jit(solution)/shard_map/ppermute | solution.py:525
  197.7 12.6 place_rows.2
  217.2 10.5 fusion.146.query_ref.key_ref.value_ref.refs_3_
  227.8 30.2 %collective-permute-done.17.refs_10_ = bf16[4,48,3840]{2,1,0:T(8,128)(2,1)} collective-permute-done((bf16[4,48,3840]{2,1,0:T(8,128)(2,1)S(1)}, bf16[4,48,3840]{2,1,0:T(8,128)(2,1)}, u32[]{:S(2)}, u32[]{:S(2)}) %collective-permute-start.17) | collective-permute-done | bytes 1474592 | tf_op jit(solution)/shard_map/ppermute | solution.py:525
  265.9 24.2 %collective-permute-done.29.refs_1_ = bf16[512,1024]{1,0:T(8,128)(2,1)S(1)} collective-permute-done((bf16[512,1024]{1,0:T(8,128)(2,1)S(1)}, bf16[512,1024]{1,0:T(8,128)(2,1)S(1)}, u32[]{:S(2)}, u32[]{:S(2)}) %collective-permute-start.29) | collective-permute-done | bytes 1048608 | tf_op jit(solution)/shard_map/ppermute | solution.py:522
  292.3 22.9 %collective-permute-done.34.refs_1_ = bf16[512,1024]{1,0:T(8,128)(2,1)} collective-permute-done((bf16[512,1024]{1,0:T(8,128)(2,1)}, bf16[512,1024]{1,0:T(8,128)(2,1)}, u32[]{:S(2)}, u32[]{:S(2)}) %collective-permute-start.34) | collective-permute-done | bytes 1048608 | tf_op jit(solution)/shard_map/ppermute | solution.py:522
  327.2 19.6 %collective-permute-done.38.refs_1_ = bf16[512,1024]{1,0:T(8,128)(2,1)} collective-permute-done((bf16[512,1024]{1,0:T(8,128)(2,1)}, bf16[512,1024]{1,0:T(8,128)(2,1)}, u32[]{:S(2)}, u32[]{:S(2)}) %collective-permute-start.38) | collective-permute-done | bytes 1048608 | tf_op jit(solution)/shard_map/ppermute | solution.py:522
  368.4 17.5 %place_rows.3 = bf16[1536,7680]{1,0:T(8,128)(2,1)} custom-call(s32[17]{0:T(128)S(1)} %stack.203.numbers_ref, bf16[4,48,3840]{2,1,0:T(8,128)(2,1)S(1)} %get-tuple-element.429.refs_0_, bf16[4,48,3840]{2,1,0:T(8,128)(2,1)S(1)} %collective-permute-done.40.refs_1_, bf16[4,48,3840]{2,1,0:T(8,128)(2,1)S(1)} %get-tuple-element.428.refs_2_, ...), custom_call_target="tpu_custom_call" | custom-call | bytes 47185920 | tf_op jit(solution)/shard_map/place_rows/pallas_call | solution.py:473
  395.5 33.5 %collective-permute-done.48.refs_1_ = bf16[128,3072]{1,0:T(8,128)(2,1)} collective-permute-done((bf16[128,3072]{1,0:T(8,128)(2,1)S(1)}, bf16[128,3072]{1,0:T(8,128)(2,1)}, u32[]{:S(2)}, u32[]{:S(2)}) %collective-permute-start.48) | collective-permute-done | bytes 786464 | tf_op jit(solution)/shard_map/ppermute | solution.py:522
  481.4 11.6 attend.7
  529.2 11.0 fusion.28
  554.9 10.6 fusion.35
  565.5 16.2 %collective-permute-done.55 = bf16[512,1536]{1,0:T(8,128)(2,1)} collective-permute-done((bf16[512,1536]{1,0:T(8,128)(2,1)}, bf16[512,1536]{1,0:T(8,128)(2,1)}, u32[]{:S(2)}, u32[]{:S(2)}) %collective-permute-start.55) | collective-permute-done | bytes 1572896 | tf_op jit(solution)/shard_map/ppermute | solution.py:525
  616.1 10.8 fusion.49
  654.9 18.7 %convolution_convert_fusion.1 = bf16[2240,1536]{1,0:T(8,128)(2,1)} fusion(bf16[2048,2240]{0,1:T(8,128)(2,1)S(1)} %pad_maximum_fusion, bf16[512,1536]{1,0:T(8,128)(2,1)} %copy-done.179, bf16[512,1536]{1,0:T(8,128)(2,1)} %copy-done.177, bf16[512,1536]{1,0:T(8,128)(2,1)} %copy-done.175, bf16[512,1536]{1,0:T(8,128)(2,1)} %copy-done.115), kind=kOutput, calls=%fused_computation.1 | convolution fusion | flops 14121467904 | bytes 22347776 | tf_op jit(solution)/shard_map/dot_general | solution.py:52
  673.7 20.6 %convolution_convert_fusion = bf16[1536,2240]{0,1:T(8,128)(2,1)} fusion(bf16[2048,1536]{1,0:T(8,128)(2,1)} %pad_maximum_fusion.1, bf16[512,2240]{0,1:T(8,128)(2,1)} %get-tuple-element.413, bf16[512,2240]{0,1:T(8,128)(2,1)} %get-tuple-element.415, bf16[512,2240]{0,1:T(8,128)(2,1)} %get-tuple-element.417, bf16[512,2240]{0,1:T(8,128)(2,1)} %get-tuple-element.419), kind=kOutput, calls=%fused_computation | convolution fusion | flops 14133002240 | bytes 22347776 | tf_op jit(solution)/shard_map/dot_general | solution.py:52
  753.7 17.0 %attend_back.4 = (f32[512,1536]{1,0:T(8,128)S(1)}, bf16[4,128,3072]{2,1,0:T(8,128)(2,1)S(1)}) custom-call(bf16[512,1536]{1,0:T(8,128)(2,1)S(1)} %copy-done.19, bf16[512,1536]{1,0:T(8,128)(2,1)S(1)} %fusion.87.grad_ref, f32[12,1,512]{2,1,0:T(1,128)S(1)} %get-tuple-element.245.log_ref, bf16[128,3072]{1,0:T(8,128)(2,1)S(1)} %text_post.1.refs_0_, ...), custom_call_target="tpu_custom_call" | custom-call | flops 8053063680 | bytes 14155776 | tf_op jit(solution)/shard_map/attend_back/pallas_call | solution.py:411
  803.3 16.1 %attend_back.5 = (f32[512,512]{1,0:T(8,128)S(1)}, bf16[4,512,1024]{2,1,0:T(8,128)(2,1)S(1)}) custom-call(bf16[512,1536]{1,0:T(8,128)(2,1)S(1)} %copy-done.39, bf16[512,1536]{1,0:T(8,128)(2,1)S(1)} %fusion.84.grad_ref, f32[4,1,512]{2,1,0:T(1,128)S(1)} %get-tuple-element.249.log_ref, bf16[512,1024]{1,0:T(8,128)(2,1)S(1)} %copy-done.50, ...), custom_call_target="tpu_custom_call" | custom-call | flops 10737418240 | bytes 11010048 | tf_op jit(solution)/shard_map/attend_back/pallas_call | solution.py:411
  892.4 12.0 collective-permute-done.67
  909.7 16.1 %attend_back.6 = (f32[512,512]{1,0:T(8,128)S(1)}, bf16[4,512,1024]{2,1,0:T(8,128)(2,1)S(1)}) custom-call(bf16[512,1536]{1,0:T(8,128)(2,1)S(1)} %copy-done.39, bf16[512,1536]{1,0:T(8,128)(2,1)S(1)} %copy-done.64, f32[4,1,512]{2,1,0:T(1,128)S(1)} %get-tuple-element.256.log_ref, bf16[512,1024]{1,0:T(8,128)(2,1)} %get-tuple-element.198.refs_0_, ...), custom_call_target="tpu_custom_call" | custom-call | flops 10737418240 | bytes 11010048 | tf_op jit(solution)/shard_map/attend_back/pallas_call | solution.py:411
  928.8 15.7 %attend_back.7 = (f32[512,512]{1,0:T(8,128)S(1)}, bf16[4,512,1024]{2,1,0:T(8,128)(2,1)S(1)}) custom-call(bf16[512,1536]{1,0:T(8,128)(2,1)S(1)} %copy-done.39, bf16[512,1536]{1,0:T(8,128)(2,1)S(1)} %copy-done.64, f32[4,1,512]{2,1,0:T(1,128)S(1)} %get-tuple-element.259.log_ref, bf16[512,1024]{1,0:T(8,128)(2,1)S(1)} %copy-done.42, ...), custom_call_target="tpu_custom_call" | custom-call | flops 10737418240 | bytes 11010048 | tf_op jit(solution)/shard_map/attend_back/pallas_call | solution.py:411
  972.8 17.2 %collective-permute-done.69 = bf16[1,512,1024]{2,1,0:T(8,128)(2,1)S(1)} collective-permute-done((bf16[1,512,1024]{2,1,0:T(8,128)(2,1)S(1)}, bf16[1,512,1024]{2,1,0:T(8,128)(2,1)S(1)}, u32[]{:S(2)}, u32[]{:S(2)}) %collective-permute-start.69) | collective-permute-done | bytes 1048608 | tf_op jit(solution)/shard_map/ppermute | solution.py:522
  991.8 20.3 %collective-permute-done.71 = bf16[1,512,1024]{2,1,0:T(8,128)(2,1)S(1)} collective-permute-done((bf16[1,512,1024]{2,1,0:T(8,128)(2,1)S(1)}, bf16[1,512,1024]{2,1,0:T(8,128)(2,1)S(1)}, u32[]{:S(2)}, u32[]{:S(2)}) %collective-permute-start.71) | collective-permute-done | bytes 1048608 | tf_op jit(solution)/shard_map/ppermute | solution.py:522
  1046.2 12.5 collective-permute-done.78
  1134.4 15.9 %collective-permute-done.93 = bf16[256,1536]{1,0:T(8,128)(2,1)S(1)} collective-permute-done((bf16[256,1536]{1,0:T(8,128)(2,1)S(1)}, bf16[256,1536]{1,0:T(8,128)(2,1)S(1)}, u32[]{:S(2)}, u32[]{:S(2)}) %collective-permute-start.93) | collective-permute-done | bytes 786464 | tf_op jit(solution)/shard_map/ppermute | solution.py:522
  1182.8 12.3 collective-permute-done.100
  1217.4 10.8 collective-permute-done.105
  1228.2 53.0 %collective-permute-done.104 = bf16[48,9216]{1,0:T(8,128)(2,1)} collective-permute-done((bf16[48,9216]{1,0:T(8,128)(2,1)}, bf16[48,9216]{1,0:T(8,128)(2,1)}, u32[]{:S(2)}, u32[]{:S(2)}) %collective-permute-start.104) | collective-permute-done | bytes 884768 | tf_op jit(solution)/shard_map/ppermute | solution.py:522
  (804 shorter events, 660.5 us)
Async XLA Ops:
  7.2 508.0 %all-gather.3.cloned.1.call-start = ((), (), s32[]{:S(2)}) async-start(), calls=%async_computation.2 | async-start | bytes 7962624 | tf_op jit(solution)/shard_map/all_gather | solution.py:774
  19.0 56.7 %collective-permute-start.1 = (bf16[48,4736]{1,0:T(8,128)(2,1)S(1)}, bf16[48,4736]{1,0:T(8,128)(2,1)}, u32[]{:S(2)}, u32[]{:S(2)}) collective-permute-start(bf16[48,4736]{1,0:T(8,128)(2,1)S(1)} %concatenate.133), channel_id=1, source_target_pairs={{0,4},{1,5},{2,6},{3,7},{4,0},{5,1},{6,2},{7,3},{8,12},{9,13},{10,... | collective-permute-start | bytes 1363976 | tf_op jit(solution)/shard_map/ppermute | solution.py:522
  19.0 59.2 %collective-permute-start = (bf16[48,4736]{1,0:T(8,128)(2,1)S(1)}, bf16[48,4736]{1,0:T(8,128)(2,1)}, u32[]{:S(2)}, u32[]{:S(2)}) collective-permute-start(bf16[48,4736]{1,0:T(8,128)(2,1)S(1)} %concatenate.133), channel_id=1, source_target_pairs={{0,2},{1,3},{2,0},{3,1},{4,6},{5,7},{6,4},{7,5},{8,10},{9,11},{10,... | collective-permute-start | bytes 1363976 | tf_op jit(solution)/shard_map/ppermute | solution.py:522
  22.0 69.5 %collective-permute-start.3 = (bf16[256,1536]{1,0:T(8,128)(2,1)}, bf16[256,1536]{1,0:T(8,128)(2,1)S(1)}, u32[]{:S(2)}, u32[]{:S(2)}) collective-permute-start(bf16[256,1536]{1,0:T(8,128)(2,1)} %get-tuple-element.463), channel_id=1, source_target_pairs={{0,4},{1,5},{2,6},{3,7},{4,0},{5,1},{6,2},{7,3},{8,12},{9,13},{10,... | collective-permute-start | bytes 2359304 | tf_op jit(solution)/shard_map/ppermute | solution.py:522
  25.5 67.3 %collective-permute-start.4 = (bf16[48,2240]{1,0:T(8,128)(2,1)}, bf16[48,2240]{1,0:T(8,128)(2,1)}, u32[]{:S(2)}, u32[]{:S(2)}) collective-permute-start(bf16[48,2240]{1,0:T(8,128)(2,1)} %get-tuple-element.484), channel_id=1, source_target_pairs={{0,8},{8,0},{16,24},{24,16},{1,9},{9,1},{17,25},{25,17},{2,10},{10... | collective-permute-start | bytes 645128 | tf_op jit(solution)/shard_map/ppermute | solution.py:525
  31.7 61.1 %collective-permute-start.5 = (bf16[48,2240]{1,0:T(8,128)(2,1)}, bf16[48,2240]{1,0:T(8,128)(2,1)S(1)}, u32[]{:S(2)}, u32[]{:S(2)}) collective-permute-start(bf16[48,2240]{1,0:T(8,128)(2,1)} %get-tuple-element.486), channel_id=1, source_target_pairs={{0,16},{8,24},{16,0},{24,8},{1,17},{9,25},{17,1},{25,9},{2,18},{10... | collective-permute-start | bytes 645128 | tf_op jit(solution)/shard_map/ppermute | solution.py:525
  99.5 66.6 %collective-permute-start.7 = (bf16[4,48,2432]{2,1,0:T(8,128)(2,1)S(1)}, bf16[4,48,2432]{2,1,0:T(8,128)(2,1)}, u32[]{:S(2)}, u32[]{:S(2)}) collective-permute-start(bf16[4,48,2432]{2,1,0:T(8,128)(2,1)S(1)} %slice.267.refs_0_), channel_id=1, source_target_pairs={{0,16},{8,24},{16,0},{24,8},{1,17},{9,25},{17,1},{25,9},{2,18},{10... | collective-permute-start | bytes 2801672 | tf_op jit(solution)/shard_map/ppermute | solution.py:525
  100.0 66.0 %collective-permute-start.11 = (bf16[4,48,2304]{2,1,0:T(8,128)(2,1)S(1)}, bf16[4,48,2304]{2,1,0:T(8,128)(2,1)}, u32[]{:S(2)}, u32[]{:S(2)}) collective-permute-start(bf16[4,48,2304]{2,1,0:T(8,128)(2,1)S(1)} %slice.268.refs_2_), channel_id=1, source_target_pairs={{0,8},{8,0},{16,24},{24,16},{1,9},{9,1},{17,25},{25,17},{2,10},{10... | collective-permute-start | bytes 2654216 | tf_op jit(solution)/shard_map/ppermute | solution.py:525
  124.5 65.4 %collective-permute-start.18 = (bf16[4,48,2432]{2,1,0:T(8,128)(2,1)S(1)}, bf16[4,48,2432]{2,1,0:T(8,128)(2,1)S(1)}, u32[]{:S(2)}, u32[]{:S(2)}) collective-permute-start(bf16[4,48,2432]{2,1,0:T(8,128)(2,1)S(1)} %slice.267.refs_0_), channel_id=1, source_target_pairs={{0,1},{1,0},{2,3},{3,2},{4,5},{5,4},{6,7},{7,6},{8,9},{9,8},{10,11... | collective-permute-start | bytes 2801672 | tf_op jit(solution)/shard_map/ppermute | solution.py:522
  191.9 73.8 %collective-permute-start.27 = (bf16[4,48,3840]{2,1,0:T(8,128)(2,1)S(1)}, bf16[4,48,3840]{2,1,0:T(8,128)(2,1)}, u32[]{:S(2)}, u32[]{:S(2)}) collective-permute-start(bf16[4,48,3840]{2,1,0:T(8,128)(2,1)S(1)} %get-tuple-element.429.refs_0_), channel_id=1, source_target_pairs={{0,16},{8,24},{16,0},{24,8},{1,17},{9,25},{17,1},{25,9},{2,18},{10... | collective-permute-start | bytes 4423688 | tf_op jit(solution)/shard_map/ppermute | solution.py:525
  195.7 62.3 %collective-permute-start.17 = (bf16[4,48,3840]{2,1,0:T(8,128)(2,1)S(1)}, bf16[4,48,3840]{2,1,0:T(8,128)(2,1)}, u32[]{:S(2)}, u32[]{:S(2)}) collective-permute-start(bf16[4,48,3840]{2,1,0:T(8,128)(2,1)S(1)} %get-tuple-element.428.refs_2_), channel_id=1, source_target_pairs={{0,16},{8,24},{16,0},{24,8},{1,17},{9,25},{17,1},{25,9},{2,18},{10... | collective-permute-start | bytes 4423688 | tf_op jit(solution)/shard_map/ppermute | solution.py:525
  197.2 68.6 %collective-permute-start.28 = (bf16[4,48,3840]{2,1,0:T(8,128)(2,1)S(1)}, bf16[4,48,3840]{2,1,0:T(8,128)(2,1)}, u32[]{:S(2)}, u32[]{:S(2)}) collective-permute-start(bf16[4,48,3840]{2,1,0:T(8,128)(2,1)S(1)} %get-tuple-element.428.refs_2_), channel_id=1, source_target_pairs={{0,8},{8,0},{16,24},{24,16},{1,9},{9,1},{17,25},{25,17},{2,10},{10... | collective-permute-start | bytes 4423688 | tf_op jit(solution)/shard_map/ppermute | solution.py:525
  346.9 182.3 %all-gather.5.cloned.1.call-start = ((), (), s32[]{:S(2)}) async-start(), calls=%async_computation.3 | async-start | bytes 7741440 | tf_op jit(solution)/shard_map/all_gather | solution.py:786
  429.0 585.8 %reduce-scatter.5.cloned.1.call-start = ((), (), s32[]{:S(2)}) async-start(), calls=%async_computation.5 | async-start | bytes 7741440 | tf_op jit(solution)/shard_map/reduce_scatter | solution.py:825
  431.9 61.1 %collective-permute-start.51 = (bf16[512,1536]{1,0:T(8,128)(2,1)S(1)}, bf16[512,1536]{1,0:T(8,128)(2,1)S(1)}, u32[]{:S(2)}, u32[]{:S(2)}) collective-permute-start(bf16[512,1536]{1,0:T(8,128)(2,1)S(1)} %fusion.82), channel_id=1, source_target_pairs={{0,8},{8,0},{16,24},{24,16},{1,9},{9,1},{17,25},{25,17},{2,10},{10... | collective-permute-start | bytes 4718600 | tf_op jit(solution)/shard_map/ppermute | solution.py:525
  433.5 69.8 %collective-permute-start.52 = (bf16[512,1536]{1,0:T(8,128)(2,1)S(1)}, bf16[512,1536]{1,0:T(8,128)(2,1)S(1)}, u32[]{:S(2)}, u32[]{:S(2)}) collective-permute-start(bf16[512,1536]{1,0:T(8,128)(2,1)S(1)} %fusion.82), channel_id=1, source_target_pairs={{0,16},{8,24},{16,0},{24,8},{1,17},{9,25},{17,1},{25,9},{2,18},{10... | collective-permute-start | bytes 4718600 | tf_op jit(solution)/shard_map/ppermute | solution.py:525
  434.9 68.3 %collective-permute-start.53 = (bf16[512,1536]{1,0:T(8,128)(2,1)S(1)}, bf16[512,1536]{1,0:T(8,128)(2,1)S(1)}, u32[]{:S(2)}, u32[]{:S(2)}) collective-permute-start(bf16[512,1536]{1,0:T(8,128)(2,1)S(1)} %fusion.82), channel_id=1, source_target_pairs={{0,24},{8,16},{16,8},{24,0},{1,25},{9,17},{17,9},{25,1},{2,26},{10... | collective-permute-start | bytes 4718600 | tf_op jit(solution)/shard_map/ppermute | solution.py:525
  512.4 69.4 %collective-permute-start.55 = (bf16[512,1536]{1,0:T(8,128)(2,1)}, bf16[512,1536]{1,0:T(8,128)(2,1)}, u32[]{:S(2)}, u32[]{:S(2)}) collective-permute-start(bf16[512,1536]{1,0:T(8,128)(2,1)} %add_convert_fusion.11), channel_id=1, source_target_pairs={{0,16},{8,24},{16,0},{24,8},{1,17},{9,25},{17,1},{25,9},{2,18},{10... | collective-permute-start | bytes 4718600 | tf_op jit(solution)/shard_map/ppermute | solution.py:525
  513.8 86.7 %collective-permute-start.56 = (bf16[512,1536]{1,0:T(8,128)(2,1)}, bf16[512,1536]{1,0:T(8,128)(2,1)}, u32[]{:S(2)}, u32[]{:S(2)}) collective-permute-start(bf16[512,1536]{1,0:T(8,128)(2,1)} %add_convert_fusion.11), channel_id=1, source_target_pairs={{0,24},{8,16},{16,8},{24,0},{1,25},{9,17},{17,9},{25,1},{2,26},{10... | collective-permute-start | bytes 4718600 | tf_op jit(solution)/shard_map/ppermute | solution.py:525
  640.1 70.7 %collective-permute-start.57 = (bf16[512,1536]{1,0:T(8,128)(2,1)}, bf16[512,1536]{1,0:T(8,128)(2,1)}, u32[]{:S(2)}, u32[]{:S(2)}) collective-permute-start(bf16[512,1536]{1,0:T(8,128)(2,1)} %convolution_convert_fusion.14), channel_id=1, source_target_pairs={{0,8},{8,0},{16,24},{24,16},{1,9},{9,1},{17,25},{25,17},{2,10},{10... | collective-permute-start | bytes 4718600 | tf_op jit(solution)/shard_map/ppermute | solution.py:525
  645.7 65.0 %collective-permute-start.58 = (bf16[512,1536]{1,0:T(8,128)(2,1)}, bf16[512,1536]{1,0:T(8,128)(2,1)}, u32[]{:S(2)}, u32[]{:S(2)}) collective-permute-start(bf16[512,1536]{1,0:T(8,128)(2,1)} %convolution_convert_fusion.13), channel_id=1, source_target_pairs={{0,16},{8,24},{16,0},{24,8},{1,17},{9,25},{17,1},{25,9},{2,18},{10... | collective-permute-start | bytes 4718600 | tf_op jit(solution)/shard_map/ppermute | solution.py:525
  650.9 59.9 %collective-permute-start.59 = (bf16[512,1536]{1,0:T(8,128)(2,1)}, bf16[512,1536]{1,0:T(8,128)(2,1)}, u32[]{:S(2)}, u32[]{:S(2)}) collective-permute-start(bf16[512,1536]{1,0:T(8,128)(2,1)} %convolution_convert_fusion.12), channel_id=1, source_target_pairs={{0,24},{8,16},{16,8},{24,0},{1,25},{9,17},{17,9},{25,1},{2,26},{10... | collective-permute-start | bytes 4718600 | tf_op jit(solution)/shard_map/ppermute | solution.py:525
  673.7 343.7 %reduce-scatter.3.cloned.1.call-start = ((), (), s32[]{:S(2)}) async-start(), calls=%async_computation.4 | async-start | bytes 7962624 | tf_op jit(solution)/shard_map/reduce_scatter | solution.py:826
  820.9 84.3 %collective-permute-start.62 = (bf16[2,512,1024]{2,1,0:T(8,128)(2,1)}, bf16[2,512,1024]{2,1,0:T(8,128)(2,1)}, u32[]{:S(2)}, u32[]{:S(2)}) collective-permute-start(bf16[2,512,1024]{2,1,0:T(8,128)(2,1)} %slice.294), channel_id=1, source_target_pairs={{0,1},{1,0},{2,3},{3,2},{4,5},{5,4},{6,7},{7,6},{8,9},{9,8},{10,11... | collective-permute-start | bytes 6291464 | tf_op jit(solution)/shard_map/ppermute | solution.py:522
  859.9 89.9 %collective-permute-start.74 = (bf16[2,2,4,48,2304]{4,3,2,1,0:T(8,128)(2,1)}, bf16[2,2,4,48,2304]{4,3,2,1,0:T(8,128)(2,1)}, u32[]{:S(2)}, u32[]{:S(2)}) collective-permute-start(bf16[2,2,4,48,2304]{4,3,2,1,0:T(8,128)(2,1)} %pad_maximum_fusion.3), channel_id=1, source_target_pairs={{0,1},{1,0},{2,3},{3,2},{4,5},{5,4},{6,7},{7,6},{8,9},{9,8},{10,11... | collective-permute-start | bytes 10616840 | tf_op jit(solution)/shard_map/ppermute | solution.py:522
  870.9 81.6 %collective-permute-start.75 = (bf16[2,2,4,48,2304]{4,3,2,1,0:T(8,128)(2,1)}, bf16[2,2,4,48,2304]{4,3,2,1,0:T(8,128)(2,1)}, u32[]{:S(2)}, u32[]{:S(2)}) collective-permute-start(bf16[2,2,4,48,2304]{4,3,2,1,0:T(8,128)(2,1)} %pad_maximum_fusion.5), channel_id=1, source_target_pairs={{0,1},{1,0},{2,3},{3,2},{4,5},{5,4},{6,7},{7,6},{8,9},{9,8},{10,11... | collective-permute-start | bytes 10616840 | tf_op jit(solution)/shard_map/ppermute | solution.py:522
  892.4 148.0 %collective-permute-start.79 = (bf16[512,1536]{1,0:T(8,128)(2,1)}, bf16[512,1536]{1,0:T(8,128)(2,1)}, u32[]{:S(2)}, u32[]{:S(2)}) collective-permute-start(bf16[512,1536]{1,0:T(8,128)(2,1)} %convolution_convert_fusion.11), channel_id=1, source_target_pairs={{0,8},{8,0},{16,24},{24,16},{1,9},{9,1},{17,25},{25,17},{2,10},{10... | collective-permute-start | bytes 4718600 | tf_op jit(solution)/shard_map/ppermute | solution.py:525
  904.4 136.0 %collective-permute-start.80 = (bf16[512,1536]{1,0:T(8,128)(2,1)}, bf16[512,1536]{1,0:T(8,128)(2,1)}, u32[]{:S(2)}, u32[]{:S(2)}) collective-permute-start(bf16[512,1536]{1,0:T(8,128)(2,1)} %convolution_convert_fusion.10), channel_id=1, source_target_pairs={{0,16},{8,24},{16,0},{24,8},{1,17},{9,25},{17,1},{25,9},{2,18},{10... | collective-permute-start | bytes 4718600 | tf_op jit(solution)/shard_map/ppermute | solution.py:525
  949.8 91.9 %collective-permute-start.81 = (bf16[512,1536]{1,0:T(8,128)(2,1)}, bf16[512,1536]{1,0:T(8,128)(2,1)}, u32[]{:S(2)}, u32[]{:S(2)}) collective-permute-start(bf16[512,1536]{1,0:T(8,128)(2,1)} %convolution_convert_fusion.9), channel_id=1, source_target_pairs={{0,24},{8,16},{16,8},{24,0},{1,25},{9,17},{17,9},{25,1},{2,26},{10... | collective-permute-start | bytes 4718600 | tf_op jit(solution)/shard_map/ppermute | solution.py:525
  1044.8 62.7 %collective-permute-start.89 = (bf16[48,3072]{1,0:T(8,128)(2,1)}, bf16[48,3072]{1,0:T(8,128)(2,1)}, u32[]{:S(2)}, u32[]{:S(2)}) collective-permute-start(bf16[48,3072]{1,0:T(8,128)(2,1)} %get-tuple-element.466), channel_id=1, source_target_pairs={{0,6},{1,7},{2,4},{3,5},{4,2},{5,3},{6,0},{7,1},{8,14},{9,15},{10,... | collective-permute-start | bytes 884744 | tf_op jit(solution)/shard_map/ppermute | solution.py:522
  1205.8 75.4 %collective-permute-start.104 = (bf16[48,9216]{1,0:T(8,128)(2,1)}, bf16[48,9216]{1,0:T(8,128)(2,1)}, u32[]{:S(2)}, u32[]{:S(2)}) collective-permute-start(bf16[48,9216]{1,0:T(8,128)(2,1)} %get-tuple-element.422), channel_id=1, source_target_pairs={{0,4},{1,5},{2,6},{3,7},{4,0},{5,1},{6,2},{7,3},{8,12},{9,13},{10,... | collective-permute-start | bytes 2654216 | tf_op jit(solution)/shard_map/ppermute | solution.py:522
  1207.1 74.0 %collective-permute-start.103 = (bf16[48,9216]{1,0:T(8,128)(2,1)}, bf16[48,9216]{1,0:T(8,128)(2,1)}, u32[]{:S(2)}, u32[]{:S(2)}) collective-permute-start(bf16[48,9216]{1,0:T(8,128)(2,1)} %get-tuple-element.421), channel_id=1, source_target_pairs={{0,2},{1,3},{2,0},{3,1},{4,6},{5,7},{6,4},{7,5},{8,10},{9,11},{10,... | collective-permute-start | bytes 2654216 | tf_op jit(solution)/shard_map/ppermute | solution.py:522
  (266 other events, 5538.9 us)
Sparse Core Ops, SparseCore 0:
  347.0 77.5 all-gather.2
  429.1 75.8 all-gather.4
  673.8 73.8 reduce-scatter.4
  792.8 97.0 reduce-scatter.2
